TPU v7x, 512 devices: a whole 4x8x8 slice. The times are simulated.
512 devices in a mesh: ctx: 32 (over z, y_lo, core), dp: 16 (over y_hi, x).
Axes of the slice: x: 4, y: 8 (y_hi: 4, y_lo: 2; y = y_hi * 2 + y_lo), z: 8, core: 2. Of those that a mesh axis runs over, the one named last changes fastest.
Arguments:
- hidden: bfloat16 [16, 4096, 2048], P('dp', 'ctx')
- key_weight: bfloat16 [2048, 1024], P('ctx'), may hold values from -0.125 to 0.125
- cluster_ids: int32 [16, 8, 4096], P('dp', None, 'ctx'), may hold values from 0 to 511, as said below
- old_centroids: float32 [4096, 128], P(('ctx', 'dp')), may hold values from -6 to 6
Outputs:
- centroids: float32 [4096, 128], replicated
Inputs may be any that keep to these rules, and one draw needn't show every extreme that they name: `cluster_ids`: in every head some of the 512 clusters receive no position.
All inputs are finite; a program needn't handle non-finite values.
Results may differ from a plain program's by a relative error of at most 0.0055.
Values may be sent and summed in bfloat16 or wider, within the bound.
No kernel may reach another device: no remote copies, remote signals or barrier semaphores. Data moves between devices by JAX's collectives and lax.ppermute only.
A program may use at most 64 MiB of HBM per device.

v0:
```python
import jax
import jax.numpy as jnp
from jax import lax
from jax.sharding import PartitionSpec as P

EPSILON = 1e-06
DECAY_RATE = 0.5


def normalize_rows(values):
    return values * lax.rsqrt(jnp.mean(values * values, axis=-1, keepdims=True) + EPSILON)


def update_rows(share_sums, share_counts, old_rows):
    scaled = share_sums / jnp.sqrt(jnp.maximum(share_counts.reshape(-1, 1), 1.0))
    mixed = DECAY_RATE * old_rows + (1.0 - DECAY_RATE) * scaled
    return normalize_rows(mixed)


def per_device(hidden, key_weight, cluster_ids, old_centroids):
    model_width = hidden.shape[2]
    heads = cluster_ids.shape[1]
    head_size = key_weight.shape[1] // heads
    clusters = old_centroids.shape[0] * lax.axis_size(("ctx", "dp")) // heads
    flat_rows = hidden.reshape(-1, model_width)
    positions = flat_rows.shape[0]
    projected = jnp.dot(
        flat_rows,
        lax.all_gather(key_weight, "ctx", axis=0, tiled=True),
        preferred_element_type=jnp.float32,
    )
    unit_keys = normalize_rows(projected.reshape(positions, heads, head_size)).astype(jnp.bfloat16)
    head_ids = jnp.moveaxis(cluster_ids, 1, 0).reshape(heads, positions)
    cluster_iota = lax.broadcasted_iota(jnp.int32, (1, clusters, 1), 1)
    one_hot = (head_ids[:, None, :] == cluster_iota).astype(jnp.bfloat16)
    cluster_sums = jnp.einsum(
        "hcn,nhd->hcd", one_hot, unit_keys, preferred_element_type=jnp.float32
    )
    cluster_sums = cluster_sums.reshape(heads * clusters, head_size)
    cluster_counts = jnp.sum(one_hot, axis=2, dtype=jnp.float32).reshape(heads * clusters)
    share_sums, share_counts = (
        lax.psum_scatter(cluster_sums, ("ctx", "dp"), scatter_dimension=0, tiled=True),
        lax.psum_scatter(cluster_counts, ("ctx", "dp"), scatter_dimension=0, tiled=True),
    )
    owned = update_rows(share_sums, share_counts, old_centroids)
    return lax.all_gather(owned, ("ctx", "dp"), axis=0, tiled=True)


def solution(mesh):
    in_specs = (P("dp", "ctx", None), P("ctx", None), P("dp", None, "ctx"), P(("ctx", "dp"), None))
    out_specs = P()
    return jax.shard_map(
        per_device, mesh=mesh, in_specs=in_specs, out_specs=out_specs, check_vma=False
    )
```

profile of v0, /device:TPU:1, one launch (start us, length us, event | category | flops | bytes accessed | tf_op | source)
XLA Modules:
  0.0 1437.3 jit_solution(1724843079825667235)
XLA Ops:
  6.5 0.0 copy-start
  6.5 0.0 all-gather.3.cloned.1.call-start
  6.5 0.7 all-gather.3.cloned.1.call-update
  7.3 0.0 all-reduce.4.cloned.1.call-start
  7.3 78.4 %all-gather.3.cloned.1.call-done = bf16[2048,1024]{1,0:T(8,128)(2,1)} async-done(((bf16[64,1024]{1,0:T(8,128)(2,1)}), bf16[2048,1024]{1,0:T(8,128)(2,1)}) %all-gather.3.cloned.1.call-update) | async-done | bytes 4194320 | tf_op jit(solution)/shard_map/all_gather | solution.py:29
  85.7 6.5 copy.7
  92.3 0.0 copy-done
  92.3 0.0 copy-start.1
  92.3 3.5 multiply_reduce_fusion
  95.7 0.0 copy-done.1
  95.7 0.0 copy-start.2
  95.8 1.8 fusion.1
  97.6 0.0 all-reduce.4.cloned.1.call-update
  97.6 0.0 all-gather.5.cloned.1.call-start
  97.7 0.4 convert_reduce_fusion
  98.1 98.6 %all-reduce.1 = f32[4096]{0:T(1024)S(1)} all-reduce(f32[4096]{0:T(1024)S(1)} %bitcast.17), channel_id=3, replica_groups=mesh['ctx'=32,'dp'=16] {'ctx','dp'}, use_global_device_ids=true, to_apply=%region_3.0.clone | all-reduce | flops 4096 | bytes 32768
  196.6 0.1 fusion.7
  196.7 179.8 %all-reduce.4.cloned.1.call-done = f32[4096,128]{1,0:T(8,128)} async-done(((f32[4096,128]{1,0:T(8,128)}), f32[4096,128]{1,0:T(8,128)}) %all-reduce.4.cloned.1.call-update) | async-done | bytes 2097168
  376.5 0.0 copy-done.2
  376.5 0.9 multiply_reduce_fusion.1
  377.4 1.4 broadcast_multiply_fusion
  378.7 0.0 all-gather.5.cloned.1.call-update
  378.8 1048.9 %all-gather.5.cloned.1.call-done = f32[4096,128]{1,0:T(8,128)} async-done(((f32[8,128]{1,0:T(8,128)}), f32[4096,128]{1,0:T(8,128)}) %all-gather.5.cloned.1.call-update) | async-done | bytes 2097168 | tf_op jit(solution)/shard_map/all_gather | solution.py:46
  1427.7 3.0 copy.13
  (3 shorter events, 0.0 us)
Async XLA Ops:
  6.5 85.7 %copy-start = (bf16[1,128,2048]{2,1,0:T(8,128)(2,1)S(1)}, bf16[1,128,2048]{2,1,0:T(8,128)(2,1)}, u32[]{:S(2)}) copy-start(bf16[1,128,2048]{2,1,0:T(8,128)(2,1)} %param.4) | copy-start | bytes 1572868
  6.5 79.2 %all-gather.3.cloned.1.call-start = ((), (), s32[]{:S(2)}) async-start(), calls=%async_computation | async-start | bytes 4325376 | tf_op jit(solution)/shard_map/all_gather | solution.py:29
  7.3 369.3 %all-reduce.4.cloned.1.call-start = ((), (), s32[]{:S(2)}) async-start(), calls=%async_computation.2 | async-start | bytes 4194304
  92.3 3.5 copy-start.1
  95.7 280.8 %copy-start.2 = (f32[8,128]{1,0:T(8,128)S(1)}, f32[8,128]{1,0:T(8,128)}, u32[]{:S(2)}) copy-start(f32[8,128]{1,0:T(8,128)} %param.7) | copy-start | bytes 12292
  97.6 1330.1 %all-gather.5.cloned.1.call-start = ((), (), s32[]{:S(2)}) async-start(), calls=%async_computation.1 | async-start | bytes 2101248 | tf_op jit(solution)/shard_map/all_gather | solution.py:46
Sparse Core Ops, SparseCore 0:
  9.5 76.1 all-gather.2
  97.7 278.7 all-reduce.3
  378.9 1048.7 all-gather.4
where the time goes:
time: 1440 us
  waiting for transfers between devices  1310 us (91%)
  blocking collectives  98.6 us (7%)
    all_gather x1, waiting for transfers between devices, per_device(): return lax.all_gather(owned, ('ctx', 'dp'), axis=0, tiled=True)  1050 us
    unnamed x4, waiting for transfers between devices  181 us
    unnamed x1, blocking collectives  98.6 us
    all_gather x1, waiting for transfers between devices, per_device(): lax.all_gather(key_weight, 'ctx', axis=0, tiled=True)  78.4 us
  transfers between devices with their start and end apart: 3, of which 3 were waited for; matrix products, arithmetic and copies ran while one was open for 0% of the time, Pallas kernels for 0%

commit v1 on v0

v1 whole, which is shorter than its diff:
```python
import jax
import jax.numpy as jnp
import numpy as np
from jax import lax
from jax.sharding import Mesh, PartitionSpec as P

EPSILON = 1e-06
DECAY_RATE = 0.5

AXES = ("z", "ylo", "core", "yhi", "x")
QUAD = ("ylo", "core")
REST = ("z", "yhi", "x")


def normalize_rows(values):
    return values * lax.rsqrt(jnp.mean(values * values, axis=-1, keepdims=True) + EPSILON)


def old_rows_permutation(quads, z_size, rows_of_quad_z):
    pairs = []
    for z in range(z_size):
        for quad in range(quads):
            source = quad * z_size + z
            pairs.append((source, z * quads + quad))
    return pairs


def per_device(hidden, key_weight, cluster_ids, old_centroids):
    z_size = lax.axis_size("z")
    quads = lax.axis_size(QUAD)
    rest = lax.axis_size(REST)
    heads = cluster_ids.shape[1]
    head_size = key_weight.shape[1] // heads
    model_width = hidden.shape[2]
    positions = hidden.shape[1]
    clusters = old_centroids.shape[0] * quads * rest // heads
    own_heads = heads // quads
    own_rows = own_heads * clusters
    block = own_rows // rest
    bf16, f32 = jnp.bfloat16, jnp.float32

    here = hidden.reshape(positions, model_width)
    swap = [(0, 1), (1, 0)]
    over_y = lax.ppermute(here, "ylo", swap)
    over_core = lax.ppermute(here, "core", swap)
    over_both = lax.ppermute(over_y, "core", swap)

    old_rows = lax.ppermute(old_centroids, ("z",) + QUAD, old_rows_permutation(quads, z_size, None))

    quad_rows = lax.all_to_all(key_weight, QUAD, split_axis=1, concat_axis=0, tiled=True)
    ids = lax.all_to_all(
        cluster_ids.reshape(quads, own_heads, positions), QUAD, split_axis=0, concat_axis=0, tiled=True
    )
    spread = jnp.broadcast_to(quad_rows[None], (z_size,) + quad_rows.shape)
    weight = lax.all_to_all(spread, "z", split_axis=0, concat_axis=0, tiled=True)
    weight = weight.reshape(model_width, own_heads * head_size)

    me = lax.axis_index(QUAD)
    flat = jnp.concatenate([here, over_core, over_y, over_both], axis=0)
    order = me ^ jnp.arange(4)
    ids = jnp.take(ids.reshape(quads, own_heads, positions), order, axis=0)
    ids = jnp.moveaxis(ids, 1, 0).reshape(own_heads, quads * positions)

    projected = jnp.dot(flat, weight, preferred_element_type=f32)
    unit_keys = normalize_rows(projected.reshape(-1, own_heads, head_size)).astype(bf16)
    cluster_iota = lax.broadcasted_iota(jnp.int32, (1, clusters, 1), 1)
    one_hot = (ids[:, None, :] == cluster_iota).astype(bf16)
    sums = jnp.einsum("hcn,nhd->hcd", one_hot, unit_keys, preferred_element_type=f32)
    counts = jnp.sum(one_hot, axis=2, dtype=f32)

    high = jnp.floor(counts * (1.0 / 32.0))
    low = counts - 32.0 * high
    sums = sums.reshape(rest, block, head_size)
    pad = [(0, 0), (0, 0), (0, head_size - block)]
    high = jnp.pad(high.reshape(rest, 1, block), pad)
    low = jnp.pad(low.reshape(rest, 1, block), pad)
    payload = jnp.concatenate(
        [sums, high, low, jnp.zeros((rest, block - 2, head_size), f32)], axis=1
    ).astype(bf16)
    arrived = lax.all_to_all(payload, REST, split_axis=0, concat_axis=0, tiled=True).astype(f32)
    total = jnp.sum(arrived, axis=0)
    share_sums = total[:block]
    share_counts = 32.0 * total[block, :block] + total[block + 1, :block]

    scaled = share_sums / jnp.sqrt(jnp.maximum(share_counts.reshape(-1, 1), 1.0))
    owned = normalize_rows(DECAY_RATE * old_rows + (1.0 - DECAY_RATE) * scaled).astype(bf16)

    spread = jnp.broadcast_to(owned[None], (rest,) + owned.shape)
    quarter = lax.all_to_all(spread, REST, split_axis=0, concat_axis=0, tiled=True)
    quarter = quarter.reshape(own_rows, head_size)
    half = lax.all_gather(quarter, "ylo", axis=0, tiled=False)
    other = lax.ppermute(half, "core", swap)
    core = lax.axis_index("core")
    first = jnp.where(core == 0, half, other)
    second = jnp.where(core == 0, other, half)
    out = jnp.stack([first, second], axis=1).astype(f32)
    return out.reshape(heads * clusters, head_size)


def solution(mesh):
    sizes = {"z": 8, "ylo": 2, "core": 2, "yhi": 4, "x": 4}
    fine = Mesh(np.asarray(mesh.devices).reshape([sizes[a] for a in AXES]), AXES)
    ctx, dp = ("z", "ylo", "core"), ("yhi", "x")
    in_specs = (P(dp, ctx, None), P(ctx, None), P(dp, None, ctx), P(ctx + dp, None))
    return jax.shard_map(
        per_device, mesh=fine, in_specs=in_specs, out_specs=P(), check_vma=False
    )
```

time: 1440 us -> 132 us (0.09)
  waiting for transfers between devices: 1310 us -> 41.8 us
  blocking collectives: 98.6 us -> 40.7 us
  starting transfers between devices: 0.08 us -> 37.9 us
    all_gather x2 -> x0, waiting for transfers between devices: 1130 us -> none  [the longest x1 1050 us: per_device(): return lax.all_gather(owned, ('ctx', 'dp'), axis=0, tiled=True)]
    unnamed x4 -> x0, waiting for transfers between devices: 181 us -> none
    unnamed x1 -> x0, blocking collectives: 98.6 us -> none
    all_to_all x0 -> x2, blocking collectives: none -> 34.8 us  [the longest x1 21.9 us: per_device(): lax.all_to_all(spread, REST, split_axis=0, concat_axis=0, tiled=True)]
    all_to_all x0 -> x3, waiting for transfers between devices: none -> 31.5 us  [the longest x1 18.3 us: per_device(): lax.all_to_all(payload, REST, split_axis=0, concat_axis=0, tiled=True)]
    all_to_all x0 -> x3, starting transfers between devices: none -> 20.4 us  [the longest x1 11.3 us: per_device(): lax.all_to_all(payload, REST, split_axis=0, concat_axis=0, tiled=True)]
    ppermute x0 -> x5, starting transfers between devices: none -> 17.4 us  [the longest x1 5.4 us: per_device(): other = lax.ppermute(half, 'core', swap)]
  transfers between devices with their start and end apart: 3 -> 8, of which waited for: 3 -> 5; matrix products, arithmetic and copies ran while one was open for 0% -> 2% of each run, Pallas kernels for 0% -> 0%
where the time goes in v1:
time: 132 us; the launch traced here: 131 us
  waiting for transfers between devices  41.8 us (32%)
  blocking collectives  40.7 us (31%)
  starting transfers between devices  37.9 us (29%)
  local copies, waits for them, and re-layouts  4.39 us (3%)
  other arithmetic  3.85 us (3%)
  matrix products  2.45 us (2%)
    all_to_all x1, blocking collectives, per_device(): lax.all_to_all(spread, REST, split_axis=0, concat_axis=0, tiled=True)  21.9 us
    all_to_all x1, waiting for transfers between devices, per_device(): lax.all_to_all(payload, REST, split_axis=0, concat_axis=0, tiled=True)  18.3 us
    all_to_all x1, blocking collectives, per_device(): lax.all_to_all(key_weight, QUAD, split_axis=1, concat_axis=0, tiled=True)  12.9 us
    all_to_all x1, starting transfers between devices, per_device(): lax.all_to_all(payload, REST, split_axis=0, concat_axis=0, tiled=True)  11.3 us
    all_to_all x1, waiting for transfers between devices, per_device(): lax.all_to_all(spread, 'z', split_axis=0, concat_axis=0, tiled=True)  10.2 us
    ppermute x1, waiting for transfers between devices, per_device(): over_y = lax.ppermute(here, 'ylo', swap)  8.8 us
    all_gather x1, blocking collectives, per_device(): half = lax.all_gather(quarter, 'ylo', axis=0, tiled=False)  5.89 us
    ppermute x1, starting transfers between devices, per_device(): other = lax.ppermute(half, 'core', swap)  5.4 us
  transfers between devices with their start and end apart: 8, of which 5 were waited for; matrix products, arithmetic and copies ran while one was open for 2% of the time, Pallas kernels for 0%

profile of v1, /device:TPU:1, one launch (start us, length us, event | category | flops | bytes accessed | tf_op | source)
XLA Modules:
  0.0 131.3 jit_solution(12901205390372302464)
XLA Ops:
  0.0 0.0 copy-start
  0.0 1.0 copy.46
  1.0 12.9 %all_to_all.36 = bf16[64,4,256]{2,0,1:T(8,128)(2,1)S(1)} all-to-all(bf16[64,4,256]{2,0,1:T(8,128)(2,1)S(1)} %bitcast.42), channel_id=1, replica_groups=mesh['z'=8,'ylo'=2,'core'=2,'yhi'=4,'x'=4] {'ylo','core'}, dimensions={1} | all-to-all | bytes 262144 | tf_op jit(solution)/shard_map/all_to_all | solution.py:50
  13.8 4.3 %all-to-all-start = ((s32[4,2,128]{2,1,0:T(2,128)}), s32[4,2,128]{2,1,0:T(2,128)S(1)}, u32[]{:S(2)}, u32[]{:S(2)}) async-start(s32[4,2,128]{2,1,0:T(2,128)} %bitcast.45), calls=%async_computation | async-start | bytes 8192 | tf_op jit(solution)/shard_map/all_to_all | solution.py:51
  18.1 0.1 copy.32
  18.2 3.0 %all-to-all-done = s32[4,2,128]{2,1,0:T(2,128)S(1)} async-done(((s32[4,2,128]{2,1,0:T(2,128)}), s32[4,2,128]{2,1,0:T(2,128)S(1)}, u32[]{:S(2)}, u32[]{:S(2)}) %all-to-all-start) | async-done | bytes 4128 | tf_op jit(solution)/shard_map/all_to_all | solution.py:51
  21.2 1.0 broadcast_in_dim.32
  22.2 4.9 %all-to-all-start.2 = ((bf16[8,256,256]{1,2,0:T(8,128)(2,1)}), bf16[8,256,256]{1,2,0:T(8,128)(2,1)S(1)}, u32[]{:S(2)}, u32[]{:S(2)}) async-start(bf16[8,256,256]{1,2,0:T(8,128)(2,1)} %broadcast_in_dim.32), calls=%async_computation.2 | async-start | bytes 2097152 | tf_op jit(solution)/shard_map/all_to_all | solution.py:55
  27.1 0.0 copy-done
  27.1 1.9 %collective-permute-start.2 = (bf16[128,2048]{1,0:T(8,128)(2,1)S(1)}, bf16[128,2048]{1,0:T(8,128)(2,1)S(1)}, u32[]{:S(2)}, u32[]{:S(2)}) collective-permute-start(bf16[128,2048]{1,0:T(8,128)(2,1)S(1)} %bitcast.46), channel_id=1, source_target_pairs={{0,32},{32,0},{1,33},{33,1},{2,34},{34,2},{3,35},{35,3},{4,36},{36... | collective-permute-start | bytes 1572872 | tf_op jit(solution)/shard_map/ppermute | solution.py:44
  29.1 2.9 %collective-permute-start.1 = (bf16[128,2048]{1,0:T(8,128)(2,1)S(1)}, bf16[128,2048]{1,0:T(8,128)(2,1)}, u32[]{:S(2)}, u32[]{:S(2)}) collective-permute-start(bf16[128,2048]{1,0:T(8,128)(2,1)S(1)} %bitcast.47), channel_id=1, source_target_pairs={{0,16},{16,0},{1,17},{17,1},{2,18},{18,2},{3,19},{19,3},{4,20},{20... | collective-permute-start | bytes 1572872 | tf_op jit(solution)/shard_map/ppermute | solution.py:45
  32.0 0.1 pad.16.clone
  32.1 0.6 gather_fusion
  32.7 8.8 %collective-permute-done.2 = bf16[128,2048]{1,0:T(8,128)(2,1)S(1)} collective-permute-done((bf16[128,2048]{1,0:T(8,128)(2,1)S(1)}, bf16[128,2048]{1,0:T(8,128)(2,1)S(1)}, u32[]{:S(2)}, u32[]{:S(2)}) %collective-permute-start.2) | collective-permute-done | bytes 524320 | tf_op jit(solution)/shard_map/ppermute | solution.py:44
  41.5 3.8 %collective-permute-start.3 = (bf16[128,2048]{1,0:T(8,128)(2,1)S(1)}, bf16[128,2048]{1,0:T(8,128)(2,1)}, u32[]{:S(2)}, u32[]{:S(2)}) collective-permute-start(bf16[128,2048]{1,0:T(8,128)(2,1)S(1)} %collective-permute-done.2), channel_id=1, source_target_pairs={{0,16},{16,0},{1,17},{17,1},{2,18},{18,2},{3,19},{19,3},{4,20},{20... | collective-permute-start | bytes 1572872 | tf_op jit(solution)/shard_map/ppermute | solution.py:46
  45.3 0.1 select_bitcast_fusion.2
  45.4 0.3 convert_reduce_fusion
  45.7 0.1 reduce_sum.40
  45.8 0.1 copy.43
  46.0 0.1 copy.42
  46.1 10.2 %all-to-all-done.2 = bf16[8,256,256]{1,2,0:T(8,128)(2,1)S(1)} async-done(((bf16[8,256,256]{1,2,0:T(8,128)(2,1)}), bf16[8,256,256]{1,2,0:T(8,128)(2,1)S(1)}, u32[]{:S(2)}, u32[]{:S(2)}) %all-to-all-start.2) | async-done | bytes 1048608 | tf_op jit(solution)/shard_map/all_to_all | solution.py:55
  56.3 0.5 copy.33
  56.9 0.6 copy.34
  57.5 0.0 collective-permute-done.1
  57.5 0.0 collective-permute-done.3
  57.5 2.0 %multiply_reduce_fusion = (f32[512,2]{0,1:T(2,128)S(1)}, f32[512,2,128]{0,2,1:T(8,128)S(1)}) fusion(bf16[2,128,2048]{2,1,0:T(8,128)(2,1)S(1)} %bitcast.40, bf16[128,2048]{1,0:T(8,128)(2,1)} %collective-permute-done.3, bf16[128,2048]{1,0:T(8,128)(2,1)S(1)} %collective-permute-done.2, bf16[128,2048]{1,0:T(8,128)(2,1)} %collective-permute-done.1, ...), kind=kOutput, calls=%fused_computation.32 | convolution fusion | flops 545520640 | bytes 3674112 | tf_op jit(solution)/shard_map/dot_general | solution.py:64
  59.5 0.0 copy-start.1
  59.5 0.5 fusion.9
  60.0 1.3 %fusion.16 = bf16[128,16,128]{2,1,0:T(8,128)(2,1)} fusion(bf16[128,1,8]{2,1,0:T(2,128)(2,1)S(1)} %copy.43, bf16[128,1,8]{2,1,0:T(2,128)(2,1)S(1)} %copy.42, bf16[128,8,128]{2,1,0:T(8,128)(2,1)S(1)} %bitcast.43, bf16[16]{0:T(256)(128)(2,1)S(1)} %pad.16.clone), kind=kLoop, calls=%fused_computation.27 | loop fusion | flops 4194304 | bytes 790560 | tf_op jit(solution)/shard_map/concatenate | solution.py:77
  61.3 11.3 %all-to-all-start.3 = ((bf16[128,16,128]{2,1,0:T(8,128)(2,1)}), bf16[128,16,128]{2,1,0:T(8,128)(2,1)S(1)}, u32[]{:S(2)}, u32[]{:S(2)}) async-start(bf16[128,16,128]{2,1,0:T(8,128)(2,1)} %fusion.16), calls=%async_computation.3 | async-start | bytes 1048576 | tf_op jit(solution)/shard_map/all_to_all | solution.py:80
  72.6 0.0 copy-done.1
  72.6 3.4 %collective-permute-start = (f32[8,128]{1,0:T(8,128)S(1)}, f32[8,128]{1,0:T(8,128)S(1)}, u32[]{:S(2)}, u32[]{:S(2)}) collective-permute-start(f32[8,128]{1,0:T(8,128)S(1)} %copy-done.1), channel_id=1, source_target_pairs={{0,0},{128,16},{256,32},{384,48},{16,64},{144,80},{272,96},{400,11... | collective-permute-start | bytes 12296 | tf_op jit(solution)/shard_map/ppermute | solution.py:48
  76.1 18.3 %all-to-all-done.3 = bf16[128,16,128]{2,1,0:T(8,128)(2,1)S(1)} async-done(((bf16[128,16,128]{2,1,0:T(8,128)(2,1)}), bf16[128,16,128]{2,1,0:T(8,128)(2,1)S(1)}, u32[]{:S(2)}, u32[]{:S(2)}) %all-to-all-start.3) | async-done | bytes 524320 | tf_op jit(solution)/shard_map/all_to_all | solution.py:80
  94.4 0.1 convert_reduce_fusion.1
  94.5 0.0 collective-permute-done
  94.5 0.2 multiply_reduce_fusion.1
  94.7 0.1 multiply_convert_fusion.2
  94.9 21.9 %all_to_all.37 = bf16[128,8,128]{2,1,0:T(8,128)(2,1)S(1)} all-to-all(bf16[128,8,128]{2,1,0:T(8,128)(2,1)S(1)} %broadcast_in_dim.34), channel_id=1, replica_groups=mesh['z'=8,'ylo'=2,'core'=2,'yhi'=4,'x'=4] {'z','yhi','x'}, dimensions={0} | all-to-all | bytes 524288 | tf_op jit(solution)/shard_map/all_to_all | solution.py:89
  116.8 5.9 %all_gather.3 = bf16[2,1024,128]{2,1,0:T(8,128)(2,1)S(1)} all-gather(bf16[1,1024,128]{2,1,0:T(8,128)(2,1)S(1)} %bitcast.39), channel_id=1, replica_groups=mesh['z'=8,'ylo'=2,'core'=2,'yhi'=4,'x'=4] {'ylo'}, dimensions={0}, use_global_device_ids=true | all-gather | bytes 786432 | tf_op jit(solution)/shard_map/all_gather | solution.py:91
  122.7 5.4 %collective-permute-start.4 = (bf16[2,1024,128]{2,1,0:T(8,128)(2,1)S(1)}, bf16[2,1024,128]{2,1,0:T(8,128)(2,1)S(1)}, u32[]{:S(2)}, u32[]{:S(2)}) collective-permute-start(bf16[2,1024,128]{2,1,0:T(8,128)(2,1)S(1)} %all_gather.3), channel_id=1, source_target_pairs={{0,16},{16,0},{1,17},{17,1},{2,18},{18,2},{3,19},{19,3},{4,20},{20... | collective-permute-start | bytes 1572872 | tf_op jit(solution)/shard_map/ppermute | solution.py:92
  128.1 1.5 %collective-permute-done.4 = bf16[2,1024,128]{2,1,0:T(8,128)(2,1)S(1)} collective-permute-done((bf16[2,1024,128]{2,1,0:T(8,128)(2,1)S(1)}, bf16[2,1024,128]{2,1,0:T(8,128)(2,1)S(1)}, u32[]{:S(2)}, u32[]{:S(2)}) %collective-permute-start.4) | collective-permute-done | bytes 524320 | tf_op jit(solution)/shard_map/ppermute | solution.py:92
  129.6 0.1 select_bitcast_fusion.1
  129.7 0.1 pad_maximum_fusion
  129.8 1.5 %bitcast_convert_fusion = f32[4096,128]{1,0:T(8,128)} fusion(bf16[2,2,1024,128]{3,2,1,0:T(8,128)(2,1)S(1)} %pad_maximum_fusion), kind=kLoop, calls=%fused_computation.19 | loop fusion | flops 524288 | bytes 3145728 | tf_op jit(solution)/shard_map/convert_element_type | solution.py:96
  (10 shorter events, 0.2 us)
Async XLA Ops:
  0.0 27.1 %copy-start = (bf16[1,128,2048]{2,1,0:T(8,128)(2,1)S(1)}, bf16[1,128,2048]{2,1,0:T(8,128)(2,1)}, u32[]{:S(2)}) copy-start(bf16[1,128,2048]{2,1,0:T(8,128)(2,1)} %param.4) | copy-start | bytes 1572868
  13.8 7.3 %all-to-all-start = ((s32[4,2,128]{2,1,0:T(2,128)}), s32[4,2,128]{2,1,0:T(2,128)S(1)}, u32[]{:S(2)}, u32[]{:S(2)}) async-start(s32[4,2,128]{2,1,0:T(2,128)} %bitcast.45), calls=%async_computation | async-start | bytes 8192 | tf_op jit(solution)/shard_map/all_to_all | solution.py:51
  22.2 34.1 %all-to-all-start.2 = ((bf16[8,256,256]{1,2,0:T(8,128)(2,1)}), bf16[8,256,256]{1,2,0:T(8,128)(2,1)S(1)}, u32[]{:S(2)}, u32[]{:S(2)}) async-start(bf16[8,256,256]{1,2,0:T(8,128)(2,1)} %broadcast_in_dim.32), calls=%async_computation.2 | async-start | bytes 2097152 | tf_op jit(solution)/shard_map/all_to_all | solution.py:55
  27.1 14.3 %collective-permute-start.2 = (bf16[128,2048]{1,0:T(8,128)(2,1)S(1)}, bf16[128,2048]{1,0:T(8,128)(2,1)S(1)}, u32[]{:S(2)}, u32[]{:S(2)}) collective-permute-start(bf16[128,2048]{1,0:T(8,128)(2,1)S(1)} %bitcast.46), channel_id=1, source_target_pairs={{0,32},{32,0},{1,33},{33,1},{2,34},{34,2},{3,35},{35,3},{4,36},{36... | collective-permute-start | bytes 1572872 | tf_op jit(solution)/shard_map/ppermute | solution.py:44
  29.1 28.4 %collective-permute-start.1 = (bf16[128,2048]{1,0:T(8,128)(2,1)S(1)}, bf16[128,2048]{1,0:T(8,128)(2,1)}, u32[]{:S(2)}, u32[]{:S(2)}) collective-permute-start(bf16[128,2048]{1,0:T(8,128)(2,1)S(1)} %bitcast.47), channel_id=1, source_target_pairs={{0,16},{16,0},{1,17},{17,1},{2,18},{18,2},{3,19},{19,3},{4,20},{20... | collective-permute-start | bytes 1572872 | tf_op jit(solution)/shard_map/ppermute | solution.py:45
  41.5 16.0 %collective-permute-start.3 = (bf16[128,2048]{1,0:T(8,128)(2,1)S(1)}, bf16[128,2048]{1,0:T(8,128)(2,1)}, u32[]{:S(2)}, u32[]{:S(2)}) collective-permute-start(bf16[128,2048]{1,0:T(8,128)(2,1)S(1)} %collective-permute-done.2), channel_id=1, source_target_pairs={{0,16},{16,0},{1,17},{17,1},{2,18},{18,2},{3,19},{19,3},{4,20},{20... | collective-permute-start | bytes 1572872 | tf_op jit(solution)/shard_map/ppermute | solution.py:46
  59.5 13.1 %copy-start.1 = (f32[8,128]{1,0:T(8,128)S(1)}, f32[8,128]{1,0:T(8,128)}, u32[]{:S(2)}) copy-start(f32[8,128]{1,0:T(8,128)} %param.7) | copy-start | bytes 12292
  61.3 33.0 %all-to-all-start.3 = ((bf16[128,16,128]{2,1,0:T(8,128)(2,1)}), bf16[128,16,128]{2,1,0:T(8,128)(2,1)S(1)}, u32[]{:S(2)}, u32[]{:S(2)}) async-start(bf16[128,16,128]{2,1,0:T(8,128)(2,1)} %fusion.16), calls=%async_computation.3 | async-start | bytes 1048576 | tf_op jit(solution)/shard_map/all_to_all | solution.py:80
  72.6 21.9 %collective-permute-start = (f32[8,128]{1,0:T(8,128)S(1)}, f32[8,128]{1,0:T(8,128)S(1)}, u32[]{:S(2)}, u32[]{:S(2)}) collective-permute-start(f32[8,128]{1,0:T(8,128)S(1)} %copy-done.1), channel_id=1, source_target_pairs={{0,0},{128,16},{256,32},{384,48},{16,64},{144,80},{272,96},{400,11... | collective-permute-start | bytes 12296 | tf_op jit(solution)/shard_map/ppermute | solution.py:48
  122.7 6.9 %collective-permute-start.4 = (bf16[2,1024,128]{2,1,0:T(8,128)(2,1)S(1)}, bf16[2,1024,128]{2,1,0:T(8,128)(2,1)S(1)}, u32[]{:S(2)}, u32[]{:S(2)}) collective-permute-start(bf16[2,1024,128]{2,1,0:T(8,128)(2,1)S(1)} %all_gather.3), channel_id=1, source_target_pairs={{0,16},{16,0},{1,17},{17,1},{2,18},{18,2},{3,19},{19,3},{4,20},{20... | collective-permute-start | bytes 1572872 | tf_op jit(solution)/shard_map/ppermute | solution.py:92

commit v2 on v0

v2 whole, which is shorter than its diff:
```python
import functools

import jax
import jax.numpy as jnp
import numpy as np
from jax import lax
from jax.experimental import pallas as pl
from jax.experimental.pallas import tpu as pltpu
from jax.sharding import Mesh, PartitionSpec as P

EPSILON = 1e-06
DECAY_RATE = 0.5

SIZES = {"z": 8, "ylo": 2, "core": 2, "yhi": 4, "xhi": 2, "xlo": 2}
AXES = tuple(SIZES)
OWNERS = ("z", "xhi")
Y = ("yhi", "ylo")
TILE = 16
COUNT_BASE = 64.0

VMEM = pl.BlockSpec(memory_space=pltpu.VMEM)
PARAMS = pltpu.CompilerParams(vmem_limit_bytes=24 * 1024 * 1024)


def old_rows_permutation():
    pairs = []
    for target, place in enumerate(np.ndindex(*SIZES.values())):
        at = dict(zip(AXES, place))
        quarter = at["core"] * SIZES["xlo"] + at["xlo"]
        owner = at["z"] * SIZES["xhi"] + at["xhi"]
        y = at["yhi"] * SIZES["ylo"] + at["ylo"]
        owners, ys = SIZES["z"] * SIZES["xhi"], SIZES["yhi"] * SIZES["ylo"]
        pairs.append(((quarter * owners + owner) * ys + y, target))
    return pairs


def split_count(counts):
    high = jnp.floor(counts * (1.0 / COUNT_BASE))
    return high, counts - COUNT_BASE * high


def sums_kernel(positions, own_heads, head_size, quarter_ref, *refs):
    pieces, weight_ref, out_ref = refs[:-2], refs[-2], refs[-1]
    owners, rows, _ = out_ref.shape
    block = rows - TILE
    clusters = owners * block // own_heads
    bf16, f32 = jnp.bfloat16, jnp.float32
    heads = pieces[0].shape[1] // (2 * positions)
    projected = [
        jnp.dot(piece[:positions, :], weight_ref[...], preferred_element_type=f32)
        for piece in pieces
    ]
    cluster = lax.broadcasted_iota(jnp.int32, (clusters, positions), 0).astype(f32)
    for head in range(own_heads):
        first = pl.multiple_of((quarter_ref[0] * own_heads + head) * positions, positions)
        second = pl.multiple_of(first + heads * positions, positions)
        sums = jnp.zeros((clusters, head_size), f32)
        counts = jnp.zeros((8, clusters), f32)
        for piece, keys in zip(pieces, projected):
            keys = keys[:, head * head_size:(head + 1) * head_size]
            mean = jnp.mean(keys * keys, axis=1, keepdims=True)
            unit_keys = (keys * lax.rsqrt(mean + EPSILON)).astype(bf16)
            high = piece[positions:, pl.ds(first, positions)].astype(f32)
            low = piece[positions:, pl.ds(second, positions)].astype(f32)
            ids = high[:1] * 32.0 + low[:1]
            one_hot = jnp.where(cluster == ids, 1.0, 0.0).astype(bf16)
            sums += jnp.dot(one_hot, unit_keys, preferred_element_type=f32)
            counts += lax.dot_general(
                jnp.ones((8, positions), bf16), one_hot, (((1,), (1,)), ((), ())),
                preferred_element_type=f32,
            )
        per_head = clusters // block
        out_ref[head * per_head:(head + 1) * per_head, :block, :] = sums.reshape(
            per_head, block, head_size
        ).astype(bf16)
        row = lax.broadcasted_iota(jnp.int32, (TILE, block), 0)
        for part in range(per_head):
            high, low = split_count(counts[:1, part * block:(part + 1) * block])
            lines = jnp.where(row == 0, high, jnp.where(row == 1, low, 0.0))
            lines = jnp.concatenate([lines, jnp.zeros((TILE, head_size - block), f32)], axis=1)
            out_ref[head * per_head + part, block:, :] = lines.astype(bf16)


def share_kernel(arrived_ref, old_ref, out_ref):
    block = arrived_ref.shape[1] - TILE
    bf16, f32 = jnp.bfloat16, jnp.float32
    total = arrived_ref[0].astype(f32)
    for source in range(1, arrived_ref.shape[0]):
        total += arrived_ref[source].astype(f32)
    counts = total[block:block + 1] * COUNT_BASE + total[block + 1:block + 2]
    high, low = split_count(counts)
    row = lax.broadcasted_iota(jnp.int32, (TILE, total.shape[1]), 0)
    lines = jnp.where(row == 0, high, jnp.where(row == 1, low, 0.0))
    old_high = old_ref[...].astype(bf16).astype(f32)
    old = jnp.concatenate([old_high, old_ref[...] - old_high], axis=0)
    for target in range(out_ref.shape[0]):
        out_ref[target, :block, :] = total[:block].astype(bf16)
        out_ref[target, block:block + TILE, :] = lines.astype(bf16)
        out_ref[target, block + TILE:, :] = old.astype(bf16)


def update_kernel(arrived_ref, out_ref):
    sources = arrived_ref.shape[0]
    block = out_ref.shape[1]
    f32 = jnp.float32
    total = arrived_ref[0, :block + TILE, :].astype(f32)
    for source in range(1, sources):
        total += arrived_ref[source, :block + TILE, :].astype(f32)
    counts = total[block:block + 1, :block] * COUNT_BASE + total[block + 1:block + 2, :block]
    diagonal = lax.broadcasted_iota(jnp.int32, (block, block), 0) == lax.broadcasted_iota(
        jnp.int32, (block, block), 1
    )
    counts = jnp.sum(jnp.where(diagonal, counts, 0.0), axis=1, keepdims=True)
    old = []
    for source in range(sources):
        both = arrived_ref[source, block + TILE:, :].astype(f32)
        old.append(both[:TILE // 2] + both[TILE // 2:])
    old = jnp.concatenate(old, axis=0)
    scaled = total[:block] / jnp.sqrt(jnp.maximum(counts, 1.0))
    mixed = DECAY_RATE * old + (1.0 - DECAY_RATE) * scaled
    mean = jnp.mean(mixed * mixed, axis=1, keepdims=True)
    centroids = (mixed * lax.rsqrt(mean + EPSILON)).astype(jnp.bfloat16)
    for target in range(out_ref.shape[0]):
        out_ref[target] = centroids


def per_device(hidden, key_weight, cluster_ids, old_centroids):
    _, positions, model_width = hidden.shape
    heads = cluster_ids.shape[1]
    head_size = key_weight.shape[1] // heads
    cores, xlos = SIZES["core"], SIZES["xlo"]
    quads, owners, ys = cores * xlos, SIZES["z"] * SIZES["xhi"], SIZES["yhi"] * SIZES["ylo"]
    own_heads = heads // quads
    columns = own_heads * head_size
    block = old_centroids.shape[0] * ys
    clusters = block * owners // own_heads
    bf16, f32 = jnp.bfloat16, jnp.float32
    core, xlo = lax.axis_index("core"), lax.axis_index("xlo")
    quarter = core * xlos + xlo

    mine = key_weight.reshape(-1, cores, xlos, columns)
    mine = lax.dynamic_index_in_dim(mine, xlo, axis=2, keepdims=False)
    mine = lax.all_to_all(jnp.moveaxis(mine, 1, 0), "core", split_axis=0, concat_axis=0, tiled=True)
    mine = mine.reshape(1, -1, columns)
    spread = jnp.broadcast_to(mine, (SIZES["z"] * SIZES["ylo"],) + mine.shape[1:])
    weight = lax.all_to_all(spread, ("z", "ylo"), split_axis=0, concat_axis=0, tiled=True)
    weight = weight.reshape(model_width, columns)

    ids = cluster_ids.reshape(1, heads * positions)
    ids = jnp.concatenate([ids >> 5, ids & 31], axis=1).astype(bf16)
    here = jnp.concatenate(
        [hidden.reshape(positions, model_width), ids, jnp.zeros((TILE - 1, model_width), bf16)], axis=0
    )
    swap = [(0, 1), (1, 0)]
    over_x = lax.ppermute(here, "xlo", swap)
    over_core = lax.ppermute(here, "core", swap)
    over_both = lax.ppermute(over_x, "core", swap)
    old_rows = lax.ppermute(old_centroids, AXES, old_rows_permutation())

    payload = pl.pallas_call(
        functools.partial(sums_kernel, positions, own_heads, head_size),
        out_shape=jax.ShapeDtypeStruct((owners, block + TILE, head_size), bf16),
        in_specs=[pl.BlockSpec(memory_space=pltpu.SMEM)] + [VMEM] * 5,
        out_specs=VMEM,
        compiler_params=PARAMS,
        cost_estimate=pl.CostEstimate(flops=10**9, bytes_accessed=4 * 10**6, transcendentals=0),
    )(quarter.reshape(1), here, over_core, over_x, over_both, weight)
    arrived = lax.all_to_all(payload, OWNERS, split_axis=0, concat_axis=0, tiled=True)

    shares = pl.pallas_call(
        share_kernel,
        out_shape=jax.ShapeDtypeStruct((ys, block + 2 * TILE, head_size), bf16),
        in_specs=[VMEM, VMEM],
        out_specs=VMEM,
        compiler_params=PARAMS,
    )(arrived, old_rows)
    arrived = lax.all_to_all(shares, Y, split_axis=0, concat_axis=0, tiled=True)

    owned = pl.pallas_call(
        update_kernel,
        out_shape=jax.ShapeDtypeStruct((xlos * owners, block, head_size), bf16),
        in_specs=[VMEM],
        out_specs=VMEM,
        compiler_params=PARAMS,
    )(arrived)
    half = lax.all_to_all(owned, ("xlo",) + OWNERS, split_axis=0, concat_axis=0, tiled=True)
    half = half.reshape(-1, head_size)
    other = lax.ppermute(half, "core", swap)
    first = jnp.where(core == 0, half, other)
    second = jnp.where(core == 0, other, half)
    return jnp.concatenate([first, second], axis=0).astype(f32)


def solution(mesh):
    fine = Mesh(np.asarray(mesh.devices).reshape(tuple(SIZES.values())), AXES)
    ctx, dp = ("z", "ylo", "core"), ("yhi", "xhi", "xlo")
    in_specs = (P(dp, ctx, None), P(ctx, None), P(dp, None, ctx), P(ctx + dp, None))
    return jax.shard_map(
        per_device, mesh=fine, in_specs=in_specs, out_specs=P(), check_vma=False
    )
```

time: 1440 us -> 114 us (0.08)
  waiting for transfers between devices: 1310 us -> 27.2 us
  blocking collectives: 98.6 us -> 45.6 us
  starting transfers between devices: 0.08 us -> 34.1 us
    all_gather x2 -> x0, waiting for transfers between devices: 1130 us -> none  [the longest x1 1050 us: per_device(): return lax.all_gather(owned, ('ctx', 'dp'), axis=0, tiled=True)]
    unnamed x4 -> x0, waiting for transfers between devices: 181 us -> none
    unnamed x1 -> x0, blocking collectives: 98.6 us -> none
    all_to_all x0 -> x3, blocking collectives: none -> 45.6 us  [the longest x1 20.5 us: per_device(): lax.all_to_all(owned, ('xlo',) + OWNERS, split_axis=0, concat_axis=0, til...]
    ppermute x0 -> x5, waiting for transfers between devices: none -> 22.8 us  [the longest x1 10.2 us: per_device(): over_x = lax.ppermute(here, 'xlo', swap)]
    ppermute x0 -> x5, starting transfers between devices: none -> 20.9 us  [the longest x1 7.16 us: per_device(): other = lax.ppermute(half, 'core', swap)]
  transfers between devices with their start and end apart: 3 -> 7, of which waited for: 3 -> 5; matrix products, arithmetic and copies ran while one was open for 0% -> 0% of each run, Pallas kernels for 0% -> 0%
where the time goes in v2:
time: 114 us; the launch traced here: 113 us
  blocking collectives  45.6 us (40%)
  starting transfers between devices  34.1 us (30%)
  waiting for transfers between devices  27.2 us (24%)
  Pallas kernels  2.4 us (2%)
  local copies, waits for them, and re-layouts  2.31 us (2%)
  other arithmetic  1.73 us (2%)
    all_to_all x1, blocking collectives, per_device(): lax.all_to_all(owned, ('xlo',) + OWNERS, split_axis=0, concat_axis=0, til...  20.5 us
    all_to_all x1, blocking collectives, per_device(): arrived = lax.all_to_all(shares, Y, split_axis=0, concat_axis=0, tiled=True)  14.8 us
    all_to_all x1, blocking collectives, per_device(): lax.all_to_all(jnp.moveaxis(mine, 1, 0), 'core', split_axis=0, concat_axi...  10.3 us
    ppermute x1, waiting for transfers between devices, per_device(): over_x = lax.ppermute(here, 'xlo', swap)  10.2 us
    ppermute x1, waiting for transfers between devices, per_device(): old_rows = lax.ppermute(old_centroids, AXES, old_rows_permutation())  9.49 us
    all_to_all x1, starting transfers between devices, per_device(): lax.all_to_all(payload, OWNERS, split_axis=0, concat_axis=0, tiled=True)  7.37 us
    ppermute x1, starting transfers between devices, per_device(): other = lax.ppermute(half, 'core', swap)  7.16 us
    all_to_all x1, starting transfers between devices, per_device(): lax.all_to_all(spread, ('z', 'ylo'), split_axis=0, concat_axis=0, tiled=T...  5.91 us
  transfers between devices with their start and end apart: 7, of which 5 were waited for; matrix products, arithmetic and copies ran while one was open for 0% of the time, Pallas kernels for 0%

profile of v2, /device:TPU:1, one launch (start us, length us, event | category | flops | bytes accessed | tf_op | source)
XLA Modules:
  0.0 113.5 jit_solution(7190215523642477614)
XLA Ops:
  0.0 1.0 reshape.68
  1.0 0.1 constant_dynamic-slice_fusion
  1.2 10.3 %all_to_all.25 = bf16[2,64,256]{2,1,0:T(8,128)(2,1)S(1)} all-to-all(bf16[2,64,256]{2,1,0:T(8,128)(2,1)S(1)} %bitcast.23), channel_id=1, replica_groups=mesh['z'=8,'ylo'=2,'core'=2,'yhi'=4,'xhi'=2,'xlo'=2] {'core'}, dimensions={0} | all-to-all | bytes 131072 | tf_op jit(solution)/shard_map/all_to_all | solution.py:143
  11.5 1.1 broadcast_in_dim.12
  12.6 0.0 copy-start.1
  12.6 0.0 copy-start
  12.6 5.9 %all-to-all-start.1 = ((bf16[16,128,256]{2,1,0:T(8,128)(2,1)}), bf16[16,128,256]{2,1,0:T(8,128)(2,1)S(1)}, u32[]{:S(2)}, u32[]{:S(2)}) async-start(bf16[16,128,256]{2,1,0:T(8,128)(2,1)} %broadcast_in_dim.12), calls=%async_computation.1 | async-start | bytes 2097152 | tf_op jit(solution)/shard_map/all_to_all | solution.py:146
  18.5 0.0 copy-done.1
  18.5 0.1 pad.5.clone
  18.6 0.0 copy-done
  18.6 0.2 maximum_maximum_fusion.refs_0_
  18.8 3.1 %collective-permute-start.1 = (bf16[144,2048]{1,0:T(8,128)(2,1)S(1)}, bf16[144,2048]{1,0:T(8,128)(2,1)S(1)}, u32[]{:S(2)}, u32[]{:S(2)}) collective-permute-start(bf16[144,2048]{1,0:T(8,128)(2,1)S(1)} %maximum_maximum_fusion.refs_0_), channel_id=1, source_target_pairs={{0,1},{1,0},{2,3},{3,2},{4,5},{5,4},{6,7},{7,6},{8,9},{9,8},{10,11... | collective-permute-start | bytes 1769480 | tf_op jit(solution)/shard_map/ppermute | solution.py:155
  21.9 2.8 %collective-permute-start = (bf16[144,2048]{1,0:T(8,128)(2,1)S(1)}, bf16[144,2048]{1,0:T(8,128)(2,1)S(1)}, u32[]{:S(2)}, u32[]{:S(2)}) collective-permute-start(bf16[144,2048]{1,0:T(8,128)(2,1)S(1)} %maximum_maximum_fusion.refs_0_), channel_id=1, source_target_pairs={{0,16},{16,0},{1,17},{17,1},{2,18},{18,2},{3,19},{19,3},{4,20},{20... | collective-permute-start | bytes 1769480 | tf_op jit(solution)/shard_map/ppermute | solution.py:156
  24.7 10.2 %collective-permute-done.1.refs_2_ = bf16[144,2048]{1,0:T(8,128)(2,1)S(1)} collective-permute-done((bf16[144,2048]{1,0:T(8,128)(2,1)S(1)}, bf16[144,2048]{1,0:T(8,128)(2,1)S(1)}, u32[]{:S(2)}, u32[]{:S(2)}) %collective-permute-start.1) | collective-permute-done | bytes 589856 | tf_op jit(solution)/shard_map/ppermute | solution.py:155
  34.9 3.4 %collective-permute-start.2 = (bf16[144,2048]{1,0:T(8,128)(2,1)S(1)}, bf16[144,2048]{1,0:T(8,128)(2,1)S(1)}, u32[]{:S(2)}, u32[]{:S(2)}) collective-permute-start(bf16[144,2048]{1,0:T(8,128)(2,1)S(1)} %collective-permute-done.1.refs_2_), channel_id=1, source_target_pairs={{0,16},{16,0},{1,17},{17,1},{2,18},{18,2},{3,19},{19,3},{4,20},{20... | collective-permute-start | bytes 1769480 | tf_op jit(solution)/shard_map/ppermute | solution.py:157
  38.3 0.0 collective-permute-done.refs_1_
  38.3 1.6 %collective-permute-done.2.refs_3_ = bf16[144,2048]{1,0:T(8,128)(2,1)S(1)} collective-permute-done((bf16[144,2048]{1,0:T(8,128)(2,1)S(1)}, bf16[144,2048]{1,0:T(8,128)(2,1)S(1)}, u32[]{:S(2)}, u32[]{:S(2)}) %collective-permute-start.2) | collective-permute-done | bytes 589856 | tf_op jit(solution)/shard_map/ppermute | solution.py:157
  39.9 4.4 %all-to-all-done.1 = bf16[16,128,256]{2,1,0:T(8,128)(2,1)S(1)} async-done(((bf16[16,128,256]{2,1,0:T(8,128)(2,1)}), bf16[16,128,256]{2,1,0:T(8,128)(2,1)S(1)}, u32[]{:S(2)}, u32[]{:S(2)}) %all-to-all-start.1) | async-done | bytes 1048608 | tf_op jit(solution)/shard_map/all_to_all | solution.py:146
  44.3 0.0 copy-start.2
  44.3 2.1 %shard_map.46 = bf16[16,80,128]{2,1,0:T(8,128)(2,1)} custom-call(s32[1]{0:T(128)} %bitcast.quarter_ref, bf16[144,2048]{1,0:T(8,128)(2,1)S(1)} %maximum_maximum_fusion.refs_0_, bf16[144,2048]{1,0:T(8,128)(2,1)S(1)} %collective-permute-done.refs_1_, bf16[144,2048]{1,0:T(8,128)(2,1)S(1)} %collective-permute-done.1.refs_2_, ...), custom_call_target="tpu_custom_call" | custom-call | flops 1000000000 | bytes 4000000 | tf_op jit(solution)/shard_map/pallas_call | solution.py:160
  46.4 7.4 %all-to-all-start.2 = ((bf16[16,80,128]{2,1,0:T(8,128)(2,1)}), bf16[16,80,128]{2,1,0:T(8,128)(2,1)S(1)}, u32[]{:S(2)}, u32[]{:S(2)}) async-start(bf16[16,80,128]{2,1,0:T(8,128)(2,1)} %shard_map.46), calls=%async_computation.2 | async-start | bytes 655360 | tf_op jit(solution)/shard_map/all_to_all | solution.py:168
  53.8 0.0 copy-done.2
  53.8 4.4 %collective-permute-start.3 = (f32[8,128]{1,0:T(8,128)S(1)}, f32[8,128]{1,0:T(8,128)S(1)}, u32[]{:S(2)}, u32[]{:S(2)}) collective-permute-start(f32[8,128]{1,0:T(8,128)S(1)} %copy-done.2), channel_id=1, source_target_pairs={{0,0},{128,1},{8,2},{136,3},{2,4},{130,5},{10,6},{138,7},{4,8},{13... | collective-permute-start | bytes 12296 | tf_op jit(solution)/shard_map/ppermute | solution.py:158
  58.2 9.5 %collective-permute-done.3.old_ref = f32[8,128]{1,0:T(8,128)S(1)} collective-permute-done((f32[8,128]{1,0:T(8,128)S(1)}, f32[8,128]{1,0:T(8,128)S(1)}, u32[]{:S(2)}, u32[]{:S(2)}) %collective-permute-start.3) | collective-permute-done | bytes 4128 | tf_op jit(solution)/shard_map/ppermute | solution.py:158
  67.7 0.0 all-to-all-done.2.arrived_ref
  67.7 0.1 shard_map.47
  67.7 14.8 %all_to_all.26.arrived_ref = bf16[8,96,128]{2,1,0:T(8,128)(2,1)S(1)} all-to-all(bf16[8,96,128]{2,1,0:T(8,128)(2,1)S(1)} %shard_map.47), channel_id=1, replica_groups=mesh['z'=8,'ylo'=2,'core'=2,'yhi'=4,'xhi'=2,'xlo'=2] {'yhi','ylo'}, dimensions={0} | all-to-all | bytes 393216 | tf_op jit(solution)/shard_map/all_to_all | solution.py:177
  82.5 0.2 shard_map.48
  82.7 20.5 %all_to_all.27 = bf16[32,64,128]{2,1,0:T(8,128)(2,1)S(1)} all-to-all(bf16[32,64,128]{2,1,0:T(8,128)(2,1)S(1)} %shard_map.48), channel_id=1, replica_groups=mesh['z'=8,'ylo'=2,'core'=2,'yhi'=4,'xhi'=2,'xlo'=2] {'xlo','z','xhi'}, dimensions={0} | all-to-all | bytes 1048576 | tf_op jit(solution)/shard_map/all_to_all | solution.py:186
  103.2 7.2 %collective-permute-start.4 = (bf16[2048,128]{1,0:T(8,128)(2,1)S(1)}, bf16[2048,128]{1,0:T(8,128)(2,1)S(1)}, u32[]{:S(2)}, u32[]{:S(2)}) collective-permute-start(bf16[2048,128]{1,0:T(8,128)(2,1)S(1)} %bitcast.21), channel_id=1, source_target_pairs={{0,16},{16,0},{1,17},{17,1},{2,18},{18,2},{3,19},{19,3},{4,20},{20... | collective-permute-start | bytes 1572872 | tf_op jit(solution)/shard_map/ppermute | solution.py:188
  110.4 1.5 %collective-permute-done.4 = bf16[2048,128]{1,0:T(8,128)(2,1)S(1)} collective-permute-done((bf16[2048,128]{1,0:T(8,128)(2,1)S(1)}, bf16[2048,128]{1,0:T(8,128)(2,1)S(1)}, u32[]{:S(2)}, u32[]{:S(2)}) %collective-permute-start.4) | collective-permute-done | bytes 524320 | tf_op jit(solution)/shard_map/ppermute | solution.py:188
  111.9 0.1 broadcast_select_fusion.1
  112.0 1.5 %maximum_convert_fusion = f32[4096,128]{1,0:T(8,128)} fusion(bf16[2048,128]{1,0:T(8,128)(2,1)S(1)} %get-tuple-element.6, bf16[2048,128]{1,0:T(8,128)(2,1)S(1)} %get-tuple-element.5), kind=kLoop, calls=%fused_computation | loop fusion | flops 2097152 | bytes 3145728 | tf_op jit(solution)/shard_map/convert_element_type | solution.py:191
  (4 shorter events, 0.0 us)
Async XLA Ops:
  12.6 5.9 %copy-start.1 = (s32[1,8,128]{2,1,0:T(8,128)S(1)}, s32[1,8,128]{2,1,0:T(8,128)}, u32[]{:S(2)}) copy-start(s32[1,8,128]{2,1,0:T(8,128)} %param.6) | copy-start | bytes 12292
  12.6 6.0 %copy-start = (bf16[1,128,2048]{2,1,0:T(8,128)(2,1)S(1)}, bf16[1,128,2048]{2,1,0:T(8,128)(2,1)}, u32[]{:S(2)}) copy-start(bf16[1,128,2048]{2,1,0:T(8,128)(2,1)} %param.4) | copy-start | bytes 1572868
  12.6 31.8 %all-to-all-start.1 = ((bf16[16,128,256]{2,1,0:T(8,128)(2,1)}), bf16[16,128,256]{2,1,0:T(8,128)(2,1)S(1)}, u32[]{:S(2)}, u32[]{:S(2)}) async-start(bf16[16,128,256]{2,1,0:T(8,128)(2,1)} %broadcast_in_dim.12), calls=%async_computation.1 | async-start | bytes 2097152 | tf_op jit(solution)/shard_map/all_to_all | solution.py:146
  18.8 16.1 %collective-permute-start.1 = (bf16[144,2048]{1,0:T(8,128)(2,1)S(1)}, bf16[144,2048]{1,0:T(8,128)(2,1)S(1)}, u32[]{:S(2)}, u32[]{:S(2)}) collective-permute-start(bf16[144,2048]{1,0:T(8,128)(2,1)S(1)} %maximum_maximum_fusion.refs_0_), channel_id=1, source_target_pairs={{0,1},{1,0},{2,3},{3,2},{4,5},{5,4},{6,7},{7,6},{8,9},{9,8},{10,11... | collective-permute-start | bytes 1769480 | tf_op jit(solution)/shard_map/ppermute | solution.py:155
  21.9 16.4 %collective-permute-start = (bf16[144,2048]{1,0:T(8,128)(2,1)S(1)}, bf16[144,2048]{1,0:T(8,128)(2,1)S(1)}, u32[]{:S(2)}, u32[]{:S(2)}) collective-permute-start(bf16[144,2048]{1,0:T(8,128)(2,1)S(1)} %maximum_maximum_fusion.refs_0_), channel_id=1, source_target_pairs={{0,16},{16,0},{1,17},{17,1},{2,18},{18,2},{3,19},{19,3},{4,20},{20... | collective-permute-start | bytes 1769480 | tf_op jit(solution)/shard_map/ppermute | solution.py:156
  34.9 5.0 %collective-permute-start.2 = (bf16[144,2048]{1,0:T(8,128)(2,1)S(1)}, bf16[144,2048]{1,0:T(8,128)(2,1)S(1)}, u32[]{:S(2)}, u32[]{:S(2)}) collective-permute-start(bf16[144,2048]{1,0:T(8,128)(2,1)S(1)} %collective-permute-done.1.refs_2_), channel_id=1, source_target_pairs={{0,16},{16,0},{1,17},{17,1},{2,18},{18,2},{3,19},{19,3},{4,20},{20... | collective-permute-start | bytes 1769480 | tf_op jit(solution)/shard_map/ppermute | solution.py:157
  44.3 9.5 %copy-start.2 = (f32[8,128]{1,0:T(8,128)S(1)}, f32[8,128]{1,0:T(8,128)}, u32[]{:S(2)}) copy-start(f32[8,128]{1,0:T(8,128)} %param.7) | copy-start | bytes 12292
  46.4 21.3 %all-to-all-start.2 = ((bf16[16,80,128]{2,1,0:T(8,128)(2,1)}), bf16[16,80,128]{2,1,0:T(8,128)(2,1)S(1)}, u32[]{:S(2)}, u32[]{:S(2)}) async-start(bf16[16,80,128]{2,1,0:T(8,128)(2,1)} %shard_map.46), calls=%async_computation.2 | async-start | bytes 655360 | tf_op jit(solution)/shard_map/all_to_all | solution.py:168
  53.8 13.9 %collective-permute-start.3 = (f32[8,128]{1,0:T(8,128)S(1)}, f32[8,128]{1,0:T(8,128)S(1)}, u32[]{:S(2)}, u32[]{:S(2)}) collective-permute-start(f32[8,128]{1,0:T(8,128)S(1)} %copy-done.2), channel_id=1, source_target_pairs={{0,0},{128,1},{8,2},{136,3},{2,4},{130,5},{10,6},{138,7},{4,8},{13... | collective-permute-start | bytes 12296 | tf_op jit(solution)/shard_map/ppermute | solution.py:158
  103.2 8.7 %collective-permute-start.4 = (bf16[2048,128]{1,0:T(8,128)(2,1)S(1)}, bf16[2048,128]{1,0:T(8,128)(2,1)S(1)}, u32[]{:S(2)}, u32[]{:S(2)}) collective-permute-start(bf16[2048,128]{1,0:T(8,128)(2,1)S(1)} %bitcast.21), channel_id=1, source_target_pairs={{0,16},{16,0},{1,17},{17,1},{2,18},{18,2},{3,19},{19,3},{4,20},{20... | collective-permute-start | bytes 1572872 | tf_op jit(solution)/shard_map/ppermute | solution.py:188

commit v3 on v0

v3 whole, which is shorter than its diff:
```python
import functools

import jax
import jax.numpy as jnp
import numpy as np
from jax import lax
from jax.experimental import pallas as pl
from jax.experimental.pallas import tpu as pltpu
from jax.sharding import Mesh, PartitionSpec as P

EPSILON = 1e-06
DECAY_RATE = 0.5

SIZES = {"z": 8, "ylo": 2, "core": 2, "yhi": 4, "x": 4}
AXES = tuple(SIZES)
RING = ("core", "x")
Y = ("yhi", "ylo")
TILE = 16
COUNT_BASE = 64.0
OLD_AT = 8

VMEM = pl.BlockSpec(memory_space=pltpu.VMEM)
ANY = pl.BlockSpec(memory_space=pl.ANY)
ALONE = pltpu.CompilerParams(vmem_limit_bytes=56 * 1024 * 1024)
PARAMS = pltpu.CompilerParams(vmem_limit_bytes=24 * 1024 * 1024)


def turn(step):
    xs = SIZES["x"]
    return [
        (core * xs + x, core * xs + (x + (step if core == 0 else -step)) % xs)
        for core in range(SIZES["core"])
        for x in range(xs)
    ]


def place_of(ids):
    ylo, core = ids >> 8, (ids >> 7) & 1
    yhi, x, row = (ids >> 5) & 3, (ids >> 3) & 3, ids & 7
    return (core * 4 + x) * 64 + (yhi * 2 + ylo) * 8 + row


def block_of(z, y):
    core, x, yhi, ylo = z // 4, z % 4, y // 2, y % 2
    return ylo * 32 + core * 16 + yhi * 4 + x


def count_lines(counts, rest):
    high = jnp.floor(counts * (1.0 / COUNT_BASE))
    low = counts - COUNT_BASE * high
    row = lax.broadcasted_iota(jnp.int32, rest.shape, 0)
    return jnp.where(row == 0, high, jnp.where(row == 1, low, jnp.where(row < OLD_AT, 0.0, rest)))


def join_kernel(
    hidden_ref, ids_ref, old_ref, weight_ref, out_ref, spread_ref,
    ids_held, old_held, held, weight_held, spread_held, sems,
):
    positions = hidden_ref.shape[0]
    targets, cores, _, head_size = spread_ref.shape
    bf16, f32 = jnp.bfloat16, jnp.float32
    xs = weight_ref.shape[1] // (cores * head_size)
    x = lax.axis_index("x")
    moves = [
        pltpu.make_async_copy(ids_ref, ids_held, sems.at[0]),
        pltpu.make_async_copy(old_ref, old_held, sems.at[1]),
        pltpu.make_async_copy(weight_ref, weight_held, sems.at[2]),
        pltpu.make_async_copy(hidden_ref, held.at[pl.ds(0, positions)], sems.at[3]),
    ]
    for move in moves:
        move.start()
    moves[0].wait()
    moves[1].wait()
    place = place_of(ids_held[...])
    heads, width = place.shape
    parts = ((place >> 5).astype(f32), (place & 31).astype(f32))
    row = lax.broadcasted_iota(jnp.int32, (OLD_AT, width), 0)
    old = old_held[...]
    for number in range(2 * heads):
        part, head = divmod(number, heads)
        line = jnp.where(row == 0, parts[part][head:head + 1], 0.0)
        rest = old if number == 0 else jnp.zeros_like(old)
        lines = jnp.concatenate([line, rest], axis=0).astype(bf16)
        held[positions:, number * width:(number + 1) * width] = lines
    moves[3].wait()
    out = pltpu.make_async_copy(held, out_ref, sems.at[4])
    out.start()
    moves[2].wait()
    for core in range(cores):
        first = pl.multiple_of((core * xs + x) * head_size, head_size)
        columns = weight_held[:, pl.ds(first, head_size)]
        for target in range(targets):
            spread_held[target, core] = columns
    spread = pltpu.make_async_copy(spread_held, spread_ref, sems.at[5])
    spread.start()
    out.wait()
    spread.wait()


def sums_kernel(positions, *refs):
    pieces = refs[:8]
    mine_ref, others_ref, out_ref, held, mine_held, others_held, weight, old_ref, sems = refs[8:]
    owners, rows, head_size = out_ref.shape
    block = rows - TILE
    clusters = owners * block
    xs = owners // 2
    bf16, f32 = jnp.bfloat16, jnp.float32
    core, x, z = lax.axis_index("core"), lax.axis_index("x"), lax.axis_index("z")
    moves = [
        pltpu.make_async_copy(mine_ref, mine_held, sems.at[0]),
        pltpu.make_async_copy(others_ref, others_held, sems.at[1]),
    ]
    moves += [
        pltpu.make_async_copy(piece, held.at[number], sems.at[2 + number])
        for number, piece in enumerate(pieces)
    ]
    for move in moves:
        move.start()
    head = core * xs + x
    heads = held.shape[2] // (2 * positions)
    first = pl.multiple_of(head * positions, positions)
    second = pl.multiple_of(first + heads * positions, positions)
    cluster = lax.broadcasted_iota(jnp.int32, (clusters, positions), 0).astype(f32)
    mine = (head == z).astype(f32)
    moves[0].wait()
    moves[1].wait()
    for source in range(mine_held.shape[0]):
        weight[source, core] = mine_held[source, core]
        weight[source, 1 - core] = others_held[source, core]
    whole = weight[...].reshape(held.shape[2], head_size)
    keys, hots = [], []
    for number in range(len(pieces)):
        moves[2 + number].wait()
        key = jnp.dot(held[number, :positions, :], whole, preferred_element_type=f32)
        mean = jnp.mean(key * key, axis=1, keepdims=True)
        keys.append((key * lax.rsqrt(mean + EPSILON)).astype(bf16))
        high = held[number, positions:, pl.ds(first, positions)].astype(f32)
        low = held[number, positions:, pl.ds(second, positions)].astype(f32)
        ids = high[:1] * 32.0 + low[:1]
        hots.append(jnp.where(cluster == ids, 1.0, 0.0).astype(bf16))
        other, kind = divmod(number, xs)
        source = 1 - core if other else core
        sign = 2 * source - 1
        moved = (x + (0, sign, -sign, 2)[kind] + xs) % xs
        old_ref[source * xs + moved] = held[number, positions:, :head_size].astype(f32) * mine
    one_hot, unit_keys = jnp.concatenate(hots, axis=1), jnp.concatenate(keys, axis=0)
    sums = jnp.dot(one_hot, unit_keys, preferred_element_type=f32)
    counts = lax.dot_general(
        jnp.ones((8, one_hot.shape[1]), bf16), one_hot, (((1,), (1,)), ((), ())),
        preferred_element_type=f32,
    )[:1]
    empty = jnp.zeros((1, head_size - block), f32)
    for owner in range(owners):
        own = slice(owner * block, (owner + 1) * block)
        out_ref[owner, :block, :] = sums[own].astype(bf16)
        padded = jnp.concatenate([counts[:, own], empty], axis=1)
        out_ref[owner, block:, :] = count_lines(padded, old_ref[owner]).astype(bf16)


def share_kernel(arrived_ref, out_ref):
    block = arrived_ref.shape[1] - TILE
    bf16, f32 = jnp.bfloat16, jnp.float32
    total = arrived_ref[0].astype(f32)
    for source in range(1, arrived_ref.shape[0]):
        total += arrived_ref[source].astype(f32)
    counts = total[block:block + 1] * COUNT_BASE + total[block + 1:block + 2]
    sums = total[:block].astype(bf16)
    lines = count_lines(counts, total[block:]).astype(bf16)
    for target in range(out_ref.shape[0]):
        out_ref[target, :block, :] = sums
        out_ref[target, block:, :] = lines


def update_kernel(arrived_ref, out_ref):
    sources = arrived_ref.shape[0]
    block = out_ref.shape[1]
    f32 = jnp.float32
    total = arrived_ref[0].astype(f32)
    old = [total[block + OLD_AT:]]
    for source in range(1, sources):
        arrived = arrived_ref[source].astype(f32)
        old.append(arrived[block + OLD_AT:])
        total += arrived
    old = jnp.concatenate(old, axis=0)
    counts = total[block:block + 1, :block] * COUNT_BASE + total[block + 1:block + 2, :block]
    diagonal = lax.broadcasted_iota(jnp.int32, (block, block), 0) == lax.broadcasted_iota(
        jnp.int32, (block, block), 1
    )
    counts = jnp.sum(jnp.where(diagonal, counts, 0.0), axis=1, keepdims=True)
    scaled = total[:block] / jnp.sqrt(jnp.maximum(counts, 1.0))
    mixed = DECAY_RATE * old + (1.0 - DECAY_RATE) * scaled
    mean = jnp.mean(mixed * mixed, axis=1, keepdims=True)
    centroids = (mixed * lax.rsqrt(mean + EPSILON)).astype(jnp.bfloat16)
    for target in range(out_ref.shape[0]):
        out_ref[target] = centroids


def rows_kernel(mine_ref, other_ref, out_ref, held, rows_held, in_sems, out_sems):
    core = lax.axis_index("core")
    cores, xs, owners, block, _ = held.shape
    moves = []
    for number, ref in enumerate((mine_ref, other_ref)):
        for x in range(xs):
            moves.append(pltpu.make_async_copy(
                ref.at[x], held.at[number, x], in_sems.at[number * xs + x]
            ))
    for move in moves:
        move.start()
    lasts = []
    for number, place in enumerate((core, 1 - core)):
        for x in range(xs):
            moves[number * xs + x].wait()
            for z in range(owners):
                rows = held[number, x, z].astype(jnp.float32)
                for y in range(block // 8):
                    at = block_of(z, y) * 8
                    rows_held[number, x, at:at + 8, :] = rows[y * 8:(y + 1) * 8]
            last = pltpu.make_async_copy(
                rows_held.at[number, x], out_ref.at[place, x], out_sems.at[number * xs + x]
            )
            last.start()
            lasts.append(last)
    for last in lasts:
        last.wait()


def per_device(hidden, key_weight, cluster_ids, old_centroids):
    _, positions, model_width = hidden.shape
    heads = cluster_ids.shape[1]
    head_size = key_weight.shape[1] // heads
    cores, xs, zs = SIZES["core"], SIZES["x"], SIZES["z"]
    ylos = SIZES["ylo"]
    ys = SIZES["yhi"] * ylos
    block = old_centroids.shape[0] * ys
    clusters = block * zs
    bf16, f32 = jnp.bfloat16, jnp.float32

    here, spread = pl.pallas_call(
        join_kernel,
        out_shape=(
            jax.ShapeDtypeStruct((positions + TILE, model_width), bf16),
            jax.ShapeDtypeStruct((zs * ylos, cores, key_weight.shape[0], head_size), bf16),
        ),
        in_specs=[ANY] * 4,
        out_specs=(ANY, ANY),
        scratch_shapes=[
            pltpu.VMEM((heads, positions), jnp.int32),
            pltpu.VMEM(old_centroids.shape, f32),
            pltpu.VMEM((positions + TILE, model_width), bf16),
            pltpu.VMEM(key_weight.shape, bf16),
            pltpu.VMEM((zs * ylos, cores, key_weight.shape[0], head_size), bf16),
            pltpu.SemaphoreType.DMA((6,)),
        ],
        compiler_params=ALONE,
    )(
        hidden.reshape(positions, model_width), cluster_ids.reshape(heads, positions),
        old_centroids, key_weight,
    )
    swap = [(0, 1), (1, 0)]
    up = lax.ppermute(here, RING, turn(1))
    down = lax.ppermute(here, RING, turn(-1))
    weight = lax.all_to_all(spread, ("z", "ylo"), split_axis=0, concat_axis=0, tiled=True)
    others = lax.ppermute(weight, "core", swap)
    far = lax.ppermute(up, RING, turn(1))
    pieces = [here, up, down, far]
    pieces += [lax.ppermute(piece, "core", swap) for piece in pieces]

    payload = pl.pallas_call(
        functools.partial(sums_kernel, positions),
        out_shape=jax.ShapeDtypeStruct((zs, block + TILE, head_size), bf16),
        in_specs=[ANY] * (len(pieces) + 2),
        out_specs=VMEM,
        scratch_shapes=[
            pltpu.VMEM((len(pieces),) + here.shape, bf16),
            pltpu.VMEM(weight.shape, bf16),
            pltpu.VMEM(weight.shape, bf16),
            pltpu.VMEM(weight.shape, bf16),
            pltpu.VMEM((zs, TILE, head_size), f32),
            pltpu.SemaphoreType.DMA((len(pieces) + 2,)),
        ],
        compiler_params=ALONE,
        cost_estimate=pl.CostEstimate(flops=10**9, bytes_accessed=6 * 10**6, transcendentals=0),
    )(*pieces, weight, others)
    arrived = lax.all_to_all(payload, "z", split_axis=0, concat_axis=0, tiled=True)

    shares = pl.pallas_call(
        share_kernel,
        out_shape=jax.ShapeDtypeStruct((ys, block + TILE, head_size), bf16),
        in_specs=[VMEM],
        out_specs=VMEM,
        compiler_params=PARAMS,
    )(arrived)
    arrived = lax.all_to_all(shares, Y, split_axis=0, concat_axis=0, tiled=True)

    owned = pl.pallas_call(
        update_kernel,
        out_shape=jax.ShapeDtypeStruct((xs * zs, block, head_size), bf16),
        in_specs=[VMEM],
        out_specs=VMEM,
        compiler_params=PARAMS,
    )(arrived)
    half = lax.all_to_all(owned, ("x", "z"), split_axis=0, concat_axis=0, tiled=True)
    half = half.reshape(xs, zs, block, head_size)
    other = lax.ppermute(half, "core", swap)
    out = pl.pallas_call(
        rows_kernel,
        out_shape=jax.ShapeDtypeStruct((cores, xs, clusters, head_size), f32),
        in_specs=[ANY, ANY],
        out_specs=ANY,
        scratch_shapes=[
            pltpu.VMEM((cores,) + half.shape, bf16),
            pltpu.VMEM((cores, xs, clusters, head_size), f32),
            pltpu.SemaphoreType.DMA((cores * xs,)),
            pltpu.SemaphoreType.DMA((cores * xs,)),
        ],
        compiler_params=ALONE,
    )(half, other)
    return out.reshape(heads * clusters, head_size)


def solution(mesh):
    fine = Mesh(np.asarray(mesh.devices).reshape(tuple(SIZES.values())), AXES)
    ctx, dp = ("z", "ylo", "core"), ("yhi", "x")
    in_specs = (P(dp, ctx, None), P(ctx, None), P(dp, None, ctx), P(ctx + dp, None))
    return jax.shard_map(
        per_device, mesh=fine, in_specs=in_specs, out_specs=P(), check_vma=False
    )
```

time: 1440 us -> 112 us (0.08)
  waiting for transfers between devices: 1310 us -> 9.57 us
  blocking collectives: 98.6 us -> 47.1 us
  starting transfers between devices: 0.08 us -> 42.5 us
    all_gather x2 -> x0, waiting for transfers between devices: 1130 us -> none  [the longest x1 1050 us: per_device(): return lax.all_gather(owned, ('ctx', 'dp'), axis=0, tiled=True)]
    unnamed x4 -> x0, waiting for transfers between devices: 181 us -> none
    unnamed x1 -> x0, blocking collectives: 98.6 us -> none
    all_to_all x0 -> x3, blocking collectives: none -> 47.1 us  [the longest x1 16.9 us: per_device(): lax.all_to_all(owned, ('x', 'z'), split_axis=0, concat_axis=0, tiled=True)]
    ppermute x0 -> x9, starting transfers between devices: none -> 31.3 us  [the longest x4 10.4 us: per_device(): pieces += [lax.ppermute(piece, 'core', swap) for piece in pieces]]
  transfers between devices with their start and end apart: 3 -> 10, of which waited for: 3 -> 3; matrix products, arithmetic and copies ran while one was open for 0% -> 0% of each run, Pallas kernels for 0% -> 0%
where the time goes in v3:
time: 112 us; the launch traced here: 111 us
  blocking collectives  47.1 us (42%)
  starting transfers between devices  42.5 us (38%)
  Pallas kernels  10.5 us (9%)
  waiting for transfers between devices  9.57 us (9%)
  local copies, waits for them, and re-layouts  1.57 us (1%)
    all_to_all x1, blocking collectives, per_device(): lax.all_to_all(owned, ('x', 'z'), split_axis=0, concat_axis=0, tiled=True)  16.9 us
    all_to_all x1, blocking collectives, per_device(): lax.all_to_all(payload, 'z', split_axis=0, concat_axis=0, tiled=True)  16.2 us
    all_to_all x1, blocking collectives, per_device(): arrived = lax.all_to_all(shares, Y, split_axis=0, concat_axis=0, tiled=True)  14 us
    all_to_all x1, starting transfers between devices, per_device(): lax.all_to_all(spread, ('z', 'ylo'), split_axis=0, concat_axis=0, tiled=T...  11.2 us
    ppermute x4, starting transfers between devices, per_device(): pieces += [lax.ppermute(piece, 'core', swap) for piece in pieces]  10.4 us
    ppermute x1, starting transfers between devices, per_device(): other = lax.ppermute(half, 'core', swap)  7.29 us
    ppermute x1, waiting for transfers between devices, per_device(): down = lax.ppermute(here, RING, turn(-1))  6.22 us
    pallas_call x1, Pallas kernels, per_device(): pl.pallas_call(functools.partial(sums_kernel, positions), out_shape=jax.S...  5.64 us
  transfers between devices with their start and end apart: 10, of which 3 were waited for; matrix products, arithmetic and copies ran while one was open for 0% of the time, Pallas kernels for 0%

profile of v3, /device:TPU:1, one launch (start us, length us, event | category | flops | bytes accessed | tf_op | source)
XLA Modules:
  0.0 111.4 jit_solution(17359859390687918835)
XLA Ops:
  0.0 2.2 %shard_map.46 = (bf16[144,2048]{1,0:T(8,128)(2,1)}, bf16[16,2,64,128]{3,2,1,0:T(8,128)(2,1)}) custom-call(bf16[128,2048]{1,0:T(8,128)(2,1)} %bitcast.6, s32[8,128]{1,0:T(8,128)} %bitcast.7, f32[8,128]{1,0:T(8,128)} %old_ref.1, bf16[64,1024]{1,0:T(8,128)(2,1)} %weight_ref.1), custom_call_target="tpu_custom_call" | custom-call | tf_op jit(solution)/shard_map/pallas_call | solution.py:238
  2.2 5.2 %collective-permute-start = (bf16[144,2048]{1,0:T(8,128)(2,1)}, bf16[144,2048]{1,0:T(8,128)(2,1)S(1)}, u32[]{:S(2)}, u32[]{:S(2)}) collective-permute-start(bf16[144,2048]{1,0:T(8,128)(2,1)} %get-tuple-element.7.refs_0_), channel_id=1, source_target_pairs={{0,1},{1,2},{2,3},{3,0},{16,19},{17,16},{18,17},{19,18},{4,5},{5,6... | collective-permute-start | bytes 1769480 | tf_op jit(solution)/shard_map/ppermute | solution.py:260
  7.4 11.2 %all-to-all-start = ((bf16[16,2,64,128]{3,2,1,0:T(8,128)(2,1)}), bf16[16,2,64,128]{3,2,1,0:T(8,128)(2,1)S(1)}, u32[]{:S(2)}, u32[]{:S(2)}) async-start(bf16[16,2,64,128]{3,2,1,0:T(8,128)(2,1)} %get-tuple-element.8), calls=%async_computation | async-start | bytes 1048576 | tf_op jit(solution)/shard_map/all_to_all | solution.py:262
  18.6 1.9 %collective-permute-start.1 = (bf16[144,2048]{1,0:T(8,128)(2,1)}, bf16[144,2048]{1,0:T(8,128)(2,1)S(1)}, u32[]{:S(2)}, u32[]{:S(2)}) collective-permute-start(bf16[144,2048]{1,0:T(8,128)(2,1)} %get-tuple-element.7.refs_0_), channel_id=1, source_target_pairs={{0,3},{1,0},{2,1},{3,2},{16,17},{17,18},{18,19},{19,16},{4,7},{5,4... | collective-permute-start | bytes 1769480 | tf_op jit(solution)/shard_map/ppermute | solution.py:261
  20.5 0.0 collective-permute-done.refs_1_
  20.5 0.0 copy-start.2
  20.5 4.6 %collective-permute-start.2 = (bf16[144,2048]{1,0:T(8,128)(2,1)S(1)}, bf16[144,2048]{1,0:T(8,128)(2,1)S(1)}, u32[]{:S(2)}, u32[]{:S(2)}) collective-permute-start(bf16[144,2048]{1,0:T(8,128)(2,1)S(1)} %collective-permute-done.refs_1_), channel_id=1, source_target_pairs={{0,1},{1,2},{2,3},{3,0},{16,19},{17,16},{18,17},{19,18},{4,5},{5,6... | collective-permute-start | bytes 1769480 | tf_op jit(solution)/shard_map/ppermute | solution.py:264
  25.1 1.9 %collective-permute-start.3 = (bf16[144,2048]{1,0:T(8,128)(2,1)}, bf16[144,2048]{1,0:T(8,128)(2,1)S(1)}, u32[]{:S(2)}, u32[]{:S(2)}) collective-permute-start(bf16[144,2048]{1,0:T(8,128)(2,1)} %get-tuple-element.7.refs_0_), channel_id=1, source_target_pairs={{0,16},{16,0},{1,17},{17,1},{2,18},{18,2},{3,19},{19,3},{4,20},{20... | collective-permute-start | bytes 1769480 | tf_op jit(solution)/shard_map/ppermute | solution.py:266
  27.0 6.2 %collective-permute-done.1.refs_2_ = bf16[144,2048]{1,0:T(8,128)(2,1)S(1)} collective-permute-done((bf16[144,2048]{1,0:T(8,128)(2,1)}, bf16[144,2048]{1,0:T(8,128)(2,1)S(1)}, u32[]{:S(2)}, u32[]{:S(2)}) %collective-permute-start.1) | collective-permute-done | bytes 589856 | tf_op jit(solution)/shard_map/ppermute | solution.py:261
  33.3 0.0 copy-start.3
  33.3 4.1 %collective-permute-start.5 = (bf16[144,2048]{1,0:T(8,128)(2,1)S(1)}, bf16[144,2048]{1,0:T(8,128)(2,1)S(1)}, u32[]{:S(2)}, u32[]{:S(2)}) collective-permute-start(bf16[144,2048]{1,0:T(8,128)(2,1)S(1)} %collective-permute-done.1.refs_2_), channel_id=1, source_target_pairs={{0,16},{16,0},{1,17},{17,1},{2,18},{18,2},{3,19},{19,3},{4,20},{20... | collective-permute-start | bytes 1769480 | tf_op jit(solution)/shard_map/ppermute | solution.py:266
  37.4 1.9 %collective-permute-start.4 = (bf16[144,2048]{1,0:T(8,128)(2,1)S(1)}, bf16[144,2048]{1,0:T(8,128)(2,1)}, u32[]{:S(2)}, u32[]{:S(2)}) collective-permute-start(bf16[144,2048]{1,0:T(8,128)(2,1)S(1)} %collective-permute-done.refs_1_), channel_id=1, source_target_pairs={{0,16},{16,0},{1,17},{17,1},{2,18},{18,2},{3,19},{19,3},{4,20},{20... | collective-permute-start | bytes 1769480 | tf_op jit(solution)/shard_map/ppermute | solution.py:266
  39.3 0.0 collective-permute-done.2.refs_3_
  39.4 0.0 copy-start.4
  39.4 2.4 %collective-permute-start.6 = (bf16[144,2048]{1,0:T(8,128)(2,1)S(1)}, bf16[144,2048]{1,0:T(8,128)(2,1)}, u32[]{:S(2)}, u32[]{:S(2)}) collective-permute-start(bf16[144,2048]{1,0:T(8,128)(2,1)S(1)} %collective-permute-done.2.refs_3_), channel_id=1, source_target_pairs={{0,16},{16,0},{1,17},{17,1},{2,18},{18,2},{3,19},{19,3},{4,20},{20... | collective-permute-start | bytes 1769480 | tf_op jit(solution)/shard_map/ppermute | solution.py:266
  41.8 0.0 all-to-all-done.refs_8_
  41.8 0.0 copy-start
  41.8 1.9 %collective-permute-start.7 = (bf16[16,2,64,128]{3,2,1,0:T(8,128)(2,1)S(1)}, bf16[16,2,64,128]{3,2,1,0:T(8,128)(2,1)S(1)}, u32[]{:S(2)}, u32[]{:S(2)}) collective-permute-start(bf16[16,2,64,128]{3,2,1,0:T(8,128)(2,1)S(1)} %all-to-all-done.refs_8_), channel_id=1, source_target_pairs={{0,16},{16,0},{1,17},{17,1},{2,18},{18,2},{3,19},{19,3},{4,20},{20... | collective-permute-start | bytes 1572872 | tf_op jit(solution)/shard_map/ppermute | solution.py:263
  43.7 0.0 collective-permute-done.3.refs_4_
  43.7 0.0 copy-start.5
  43.7 0.0 collective-permute-done.5.refs_6_
  43.8 0.0 copy-start.6
  43.8 0.0 collective-permute-done.4.refs_5_
  43.8 1.8 %collective-permute-done.7.refs_9_ = bf16[16,2,64,128]{3,2,1,0:T(8,128)(2,1)S(1)} collective-permute-done((bf16[16,2,64,128]{3,2,1,0:T(8,128)(2,1)S(1)}, bf16[16,2,64,128]{3,2,1,0:T(8,128)(2,1)S(1)}, u32[]{:S(2)}, u32[]{:S(2)}) %collective-permute-start.7) | collective-permute-done | bytes 524320 | tf_op jit(solution)/shard_map/ppermute | solution.py:263
  45.6 0.0 copy-start.7
  45.6 0.0 collective-permute-done.6.refs_7_
  45.6 0.0 copy-done.2
  45.6 0.0 copy-done.3
  45.6 0.0 copy-done.4
  45.6 0.0 copy-done
  45.6 0.0 copy-done.5
  45.7 0.0 copy-done.6
  45.7 0.7 copy-done.7
  46.4 5.6 %shard_map.47 = bf16[8,80,128]{2,1,0:T(8,128)(2,1)} custom-call(bf16[144,2048]{1,0:T(8,128)(2,1)} %get-tuple-element.7.refs_0_, bf16[144,2048]{1,0:T(8,128)(2,1)} %copy-done.2, bf16[144,2048]{1,0:T(8,128)(2,1)} %copy-done.3, bf16[144,2048]{1,0:T(8,128)(2,1)} %copy-done.4, bf16[144,2048]{1,0:T(8,128)(2,1)} %copy-done.5, ...), custom_call_target="tpu_custom_call" | custom-call | flops 1000000000 | bytes 6000000 | tf_op jit(solution)/shard_map/pallas_call | solution.py:268
  52.1 16.2 %all_to_all.20.arrived_ref = bf16[8,80,128]{2,1,0:T(8,128)(2,1)S(1)} all-to-all(bf16[8,80,128]{2,1,0:T(8,128)(2,1)} %shard_map.47), channel_id=1, replica_groups=mesh['z'=8,'ylo'=2,'core'=2,'yhi'=4,'x'=4] {'z'}, dimensions={0} | all-to-all | bytes 327680 | tf_op jit(solution)/shard_map/all_to_all | solution.py:284
  68.3 14.0 %all_to_all.21.arrived_ref = bf16[8,80,128]{2,1,0:T(8,128)(2,1)S(1)} all-to-all(bf16[8,80,128]{2,1,0:T(8,128)(2,1)S(1)} %shard_map.48), channel_id=1, replica_groups=mesh['z'=8,'ylo'=2,'core'=2,'yhi'=4,'x'=4] {'yhi','ylo'}, dimensions={0} | all-to-all | bytes 327680 | tf_op jit(solution)/shard_map/all_to_all | solution.py:293
  82.3 0.2 shard_map.49
  82.5 16.9 %all_to_all.22 = bf16[32,64,128]{2,1,0:T(8,128)(2,1)S(1)} all-to-all(bf16[32,64,128]{2,1,0:T(8,128)(2,1)S(1)} %shard_map.49), channel_id=1, replica_groups=mesh['z'=8,'ylo'=2,'core'=2,'yhi'=4,'x'=4] {'x','z'}, dimensions={0} | all-to-all | bytes 1048576 | tf_op jit(solution)/shard_map/all_to_all | solution.py:302
  99.4 0.0 copy-start.1
  99.4 7.3 %collective-permute-start.8 = (bf16[4,8,64,128]{3,2,1,0:T(8,128)(2,1)S(1)}, bf16[4,8,64,128]{3,2,1,0:T(8,128)(2,1)S(1)}, u32[]{:S(2)}, u32[]{:S(2)}) collective-permute-start(bf16[4,8,64,128]{3,2,1,0:T(8,128)(2,1)S(1)} %bitcast.4), channel_id=1, source_target_pairs={{0,16},{16,0},{1,17},{17,1},{2,18},{18,2},{3,19},{19,3},{4,20},{20... | collective-permute-start | bytes 1572872 | tf_op jit(solution)/shard_map/ppermute | solution.py:304
  106.7 1.5 %collective-permute-done.8.other_ref = bf16[4,8,64,128]{3,2,1,0:T(8,128)(2,1)S(1)} collective-permute-done((bf16[4,8,64,128]{3,2,1,0:T(8,128)(2,1)S(1)}, bf16[4,8,64,128]{3,2,1,0:T(8,128)(2,1)S(1)}, u32[]{:S(2)}, u32[]{:S(2)}) %collective-permute-start.8) | collective-permute-done | bytes 524320 | tf_op jit(solution)/shard_map/ppermute | solution.py:304
  108.2 0.0 copy-done.1
  108.2 0.0 copy-start.8
  108.2 0.8 copy-done.8
  109.0 2.4 %shard_map.50 = f32[2,4,512,128]{3,2,1,0:T(8,128)} custom-call(bf16[4,8,64,128]{3,2,1,0:T(8,128)(2,1)} %bitcast.5, bf16[4,8,64,128]{3,2,1,0:T(8,128)(2,1)} %copy-done.8), custom_call_target="tpu_custom_call" | custom-call | tf_op jit(solution)/shard_map/pallas_call | solution.py:305
  (1 shorter events, 0.0 us)
Async XLA Ops:
  2.2 18.3 %collective-permute-start = (bf16[144,2048]{1,0:T(8,128)(2,1)}, bf16[144,2048]{1,0:T(8,128)(2,1)S(1)}, u32[]{:S(2)}, u32[]{:S(2)}) collective-permute-start(bf16[144,2048]{1,0:T(8,128)(2,1)} %get-tuple-element.7.refs_0_), channel_id=1, source_target_pairs={{0,1},{1,2},{2,3},{3,0},{16,19},{17,16},{18,17},{19,18},{4,5},{5,6... | collective-permute-start | bytes 1769480 | tf_op jit(solution)/shard_map/ppermute | solution.py:260
  7.4 34.4 %all-to-all-start = ((bf16[16,2,64,128]{3,2,1,0:T(8,128)(2,1)}), bf16[16,2,64,128]{3,2,1,0:T(8,128)(2,1)S(1)}, u32[]{:S(2)}, u32[]{:S(2)}) async-start(bf16[16,2,64,128]{3,2,1,0:T(8,128)(2,1)} %get-tuple-element.8), calls=%async_computation | async-start | bytes 1048576 | tf_op jit(solution)/shard_map/all_to_all | solution.py:262
  18.6 14.7 %collective-permute-start.1 = (bf16[144,2048]{1,0:T(8,128)(2,1)}, bf16[144,2048]{1,0:T(8,128)(2,1)S(1)}, u32[]{:S(2)}, u32[]{:S(2)}) collective-permute-start(bf16[144,2048]{1,0:T(8,128)(2,1)} %get-tuple-element.7.refs_0_), channel_id=1, source_target_pairs={{0,3},{1,0},{2,1},{3,2},{16,17},{17,18},{18,19},{19,16},{4,7},{5,4... | collective-permute-start | bytes 1769480 | tf_op jit(solution)/shard_map/ppermute | solution.py:261
  20.5 25.1 %copy-start.2 = (bf16[144,2048]{1,0:T(8,128)(2,1)}, bf16[144,2048]{1,0:T(8,128)(2,1)S(1)}, u32[]{:S(2)}) copy-start(bf16[144,2048]{1,0:T(8,128)(2,1)S(1)} %collective-permute-done.refs_1_) | copy-start | bytes 1769476
  20.5 18.8 %collective-permute-start.2 = (bf16[144,2048]{1,0:T(8,128)(2,1)S(1)}, bf16[144,2048]{1,0:T(8,128)(2,1)S(1)}, u32[]{:S(2)}, u32[]{:S(2)}) collective-permute-start(bf16[144,2048]{1,0:T(8,128)(2,1)S(1)} %collective-permute-done.refs_1_), channel_id=1, source_target_pairs={{0,1},{1,2},{2,3},{3,0},{16,19},{17,16},{18,17},{19,18},{4,5},{5,6... | collective-permute-start | bytes 1769480 | tf_op jit(solution)/shard_map/ppermute | solution.py:264
  25.1 18.6 %collective-permute-start.3 = (bf16[144,2048]{1,0:T(8,128)(2,1)}, bf16[144,2048]{1,0:T(8,128)(2,1)S(1)}, u32[]{:S(2)}, u32[]{:S(2)}) collective-permute-start(bf16[144,2048]{1,0:T(8,128)(2,1)} %get-tuple-element.7.refs_0_), channel_id=1, source_target_pairs={{0,16},{16,0},{1,17},{17,1},{2,18},{18,2},{3,19},{19,3},{4,20},{20... | collective-permute-start | bytes 1769480 | tf_op jit(solution)/shard_map/ppermute | solution.py:266
  33.3 12.4 %copy-start.3 = (bf16[144,2048]{1,0:T(8,128)(2,1)}, bf16[144,2048]{1,0:T(8,128)(2,1)S(1)}, u32[]{:S(2)}) copy-start(bf16[144,2048]{1,0:T(8,128)(2,1)S(1)} %collective-permute-done.1.refs_2_) | copy-start | bytes 1769476
  33.3 10.5 %collective-permute-start.5 = (bf16[144,2048]{1,0:T(8,128)(2,1)S(1)}, bf16[144,2048]{1,0:T(8,128)(2,1)S(1)}, u32[]{:S(2)}, u32[]{:S(2)}) collective-permute-start(bf16[144,2048]{1,0:T(8,128)(2,1)S(1)} %collective-permute-done.1.refs_2_), channel_id=1, source_target_pairs={{0,16},{16,0},{1,17},{17,1},{2,18},{18,2},{3,19},{19,3},{4,20},{20... | collective-permute-start | bytes 1769480 | tf_op jit(solution)/shard_map/ppermute | solution.py:266
  37.4 6.4 %collective-permute-start.4 = (bf16[144,2048]{1,0:T(8,128)(2,1)S(1)}, bf16[144,2048]{1,0:T(8,128)(2,1)}, u32[]{:S(2)}, u32[]{:S(2)}) collective-permute-start(bf16[144,2048]{1,0:T(8,128)(2,1)S(1)} %collective-permute-done.refs_1_), channel_id=1, source_target_pairs={{0,16},{16,0},{1,17},{17,1},{2,18},{18,2},{3,19},{19,3},{4,20},{20... | collective-permute-start | bytes 1769480 | tf_op jit(solution)/shard_map/ppermute | solution.py:266
  39.4 6.3 %copy-start.4 = (bf16[144,2048]{1,0:T(8,128)(2,1)}, bf16[144,2048]{1,0:T(8,128)(2,1)S(1)}, u32[]{:S(2)}) copy-start(bf16[144,2048]{1,0:T(8,128)(2,1)S(1)} %collective-permute-done.2.refs_3_) | copy-start | bytes 1769476
  39.4 6.2 %collective-permute-start.6 = (bf16[144,2048]{1,0:T(8,128)(2,1)S(1)}, bf16[144,2048]{1,0:T(8,128)(2,1)}, u32[]{:S(2)}, u32[]{:S(2)}) collective-permute-start(bf16[144,2048]{1,0:T(8,128)(2,1)S(1)} %collective-permute-done.2.refs_3_), channel_id=1, source_target_pairs={{0,16},{16,0},{1,17},{17,1},{2,18},{18,2},{3,19},{19,3},{4,20},{20... | collective-permute-start | bytes 1769480 | tf_op jit(solution)/shard_map/ppermute | solution.py:266
  41.8 3.8 %copy-start = (bf16[16,2,64,128]{3,2,1,0:T(8,128)(2,1)}, bf16[16,2,64,128]{3,2,1,0:T(8,128)(2,1)S(1)}, u32[]{:S(2)}) copy-start(bf16[16,2,64,128]{3,2,1,0:T(8,128)(2,1)S(1)} %all-to-all-done.refs_8_) | copy-start | bytes 1572868
  41.8 3.8 %collective-permute-start.7 = (bf16[16,2,64,128]{3,2,1,0:T(8,128)(2,1)S(1)}, bf16[16,2,64,128]{3,2,1,0:T(8,128)(2,1)S(1)}, u32[]{:S(2)}, u32[]{:S(2)}) collective-permute-start(bf16[16,2,64,128]{3,2,1,0:T(8,128)(2,1)S(1)} %all-to-all-done.refs_8_), channel_id=1, source_target_pairs={{0,16},{16,0},{1,17},{17,1},{2,18},{18,2},{3,19},{19,3},{4,20},{20... | collective-permute-start | bytes 1572872 | tf_op jit(solution)/shard_map/ppermute | solution.py:263
  43.7 1.9 %copy-start.5 = (bf16[144,2048]{1,0:T(8,128)(2,1)}, bf16[144,2048]{1,0:T(8,128)(2,1)S(1)}, u32[]{:S(2)}) copy-start(bf16[144,2048]{1,0:T(8,128)(2,1)S(1)} %collective-permute-done.3.refs_4_) | copy-start | bytes 1769476
  43.8 1.9 %copy-start.6 = (bf16[144,2048]{1,0:T(8,128)(2,1)}, bf16[144,2048]{1,0:T(8,128)(2,1)S(1)}, u32[]{:S(2)}) copy-start(bf16[144,2048]{1,0:T(8,128)(2,1)S(1)} %collective-permute-done.5.refs_6_) | copy-start | bytes 1769476
  45.6 0.8 copy-start.7
  99.4 8.8 %copy-start.1 = (bf16[32,64,128]{2,1,0:T(8,128)(2,1)}, bf16[32,64,128]{2,1,0:T(8,128)(2,1)S(1)}, u32[]{:S(2)}) copy-start(bf16[32,64,128]{2,1,0:T(8,128)(2,1)S(1)} %all_to_all.22) | copy-start | bytes 1572868
  99.4 8.8 %collective-permute-start.8 = (bf16[4,8,64,128]{3,2,1,0:T(8,128)(2,1)S(1)}, bf16[4,8,64,128]{3,2,1,0:T(8,128)(2,1)S(1)}, u32[]{:S(2)}, u32[]{:S(2)}) collective-permute-start(bf16[4,8,64,128]{3,2,1,0:T(8,128)(2,1)S(1)} %bitcast.4), channel_id=1, source_target_pairs={{0,16},{16,0},{1,17},{17,1},{2,18},{18,2},{3,19},{19,3},{4,20},{20... | collective-permute-start | bytes 1572872 | tf_op jit(solution)/shard_map/ppermute | solution.py:304
  108.2 0.8 copy-start.8

commit v4 on v3

--- a/solution.py
+++ b/solution.py
@@ -21,7 +21,7 @@
 
 VMEM = pl.BlockSpec(memory_space=pltpu.VMEM)
 ANY = pl.BlockSpec(memory_space=pl.ANY)
-ALONE = pltpu.CompilerParams(vmem_limit_bytes=56 * 1024 * 1024)
+ALONE = pltpu.CompilerParams(vmem_limit_bytes=63_200_000)
 PARAMS = pltpu.CompilerParams(vmem_limit_bytes=24 * 1024 * 1024)
 
 
@@ -99,50 +99,45 @@
 
 def sums_kernel(positions, *refs):
     pieces = refs[:8]
-    mine_ref, others_ref, out_ref, held, mine_held, others_held, weight, old_ref, sems = refs[8:]
+    mine_ref, others_ref, out_ref, weight, old_ref = refs[8:]
     owners, rows, head_size = out_ref.shape
     block = rows - TILE
     clusters = owners * block
     xs = owners // 2
     bf16, f32 = jnp.bfloat16, jnp.float32
     core, x, z = lax.axis_index("core"), lax.axis_index("x"), lax.axis_index("z")
-    moves = [
-        pltpu.make_async_copy(mine_ref, mine_held, sems.at[0]),
-        pltpu.make_async_copy(others_ref, others_held, sems.at[1]),
-    ]
-    moves += [
-        pltpu.make_async_copy(piece, held.at[number], sems.at[2 + number])
-        for number, piece in enumerate(pieces)
-    ]
-    for move in moves:
-        move.start()
     head = core * xs + x
-    heads = held.shape[2] // (2 * positions)
+    model_width = pieces[0].shape[1]
+    heads = model_width // (2 * positions)
     first = pl.multiple_of(head * positions, positions)
     second = pl.multiple_of(first + heads * positions, positions)
     cluster = lax.broadcasted_iota(jnp.int32, (clusters, positions), 0).astype(f32)
     mine = (head == z).astype(f32)
-    moves[0].wait()
-    moves[1].wait()
-    for source in range(mine_held.shape[0]):
-        weight[source, core] = mine_held[source, core]
-        weight[source, 1 - core] = others_held[source, core]
-    whole = weight[...].reshape(held.shape[2], head_size)
+    @pl.when(core == 0)
+    def _():
+        weight[:, 0] = mine_ref[:, 0]
+        weight[:, 1] = others_ref[:, 0]
+
+    @pl.when(core == 1)
+    def _():
+        weight[:, 1] = mine_ref[:, 1]
+        weight[:, 0] = others_ref[:, 1]
+
+    whole = weight[...].reshape(model_width, head_size)
     keys, hots = [], []
-    for number in range(len(pieces)):
-        moves[2 + number].wait()
-        key = jnp.dot(held[number, :positions, :], whole, preferred_element_type=f32)
+    for number, piece in enumerate(pieces):
+        key = jnp.dot(piece[:positions, :], whole, preferred_element_type=f32)
         mean = jnp.mean(key * key, axis=1, keepdims=True)
         keys.append((key * lax.rsqrt(mean + EPSILON)).astype(bf16))
-        high = held[number, positions:, pl.ds(first, positions)].astype(f32)
-        low = held[number, positions:, pl.ds(second, positions)].astype(f32)
+        high = piece[positions:, pl.ds(first, positions)].astype(f32)
+        low = piece[positions:, pl.ds(second, positions)].astype(f32)
         ids = high[:1] * 32.0 + low[:1]
         hots.append(jnp.where(cluster == ids, 1.0, 0.0).astype(bf16))
         other, kind = divmod(number, xs)
         source = 1 - core if other else core
         sign = 2 * source - 1
         moved = (x + (0, sign, -sign, 2)[kind] + xs) % xs
-        old_ref[source * xs + moved] = held[number, positions:, :head_size].astype(f32) * mine
+        old_ref[source * xs + moved] = piece[positions:, :head_size].astype(f32) * mine
     one_hot, unit_keys = jnp.concatenate(hots, axis=1), jnp.concatenate(keys, axis=0)
     sums = jnp.dot(one_hot, unit_keys, preferred_element_type=f32)
     counts = lax.dot_general(
@@ -195,35 +190,6 @@
         out_ref[target] = centroids
 
 
-def rows_kernel(mine_ref, other_ref, out_ref, held, rows_held, in_sems, out_sems):
-    core = lax.axis_index("core")
-    cores, xs, owners, block, _ = held.shape
-    moves = []
-    for number, ref in enumerate((mine_ref, other_ref)):
-        for x in range(xs):
-            moves.append(pltpu.make_async_copy(
-                ref.at[x], held.at[number, x], in_sems.at[number * xs + x]
-            ))
-    for move in moves:
-        move.start()
-    lasts = []
-    for number, place in enumerate((core, 1 - core)):
-        for x in range(xs):
-            moves[number * xs + x].wait()
-            for z in range(owners):
-                rows = held[number, x, z].astype(jnp.float32)
-                for y in range(block // 8):
-                    at = block_of(z, y) * 8
-                    rows_held[number, x, at:at + 8, :] = rows[y * 8:(y + 1) * 8]
-            last = pltpu.make_async_copy(
-                rows_held.at[number, x], out_ref.at[place, x], out_sems.at[number * xs + x]
-            )
-            last.start()
-            lasts.append(last)
-    for last in lasts:
-        last.wait()
-
-
 def per_device(hidden, key_weight, cluster_ids, old_centroids):
     _, positions, model_width = hidden.shape
     heads = cluster_ids.shape[1]
@@ -235,6 +201,7 @@
     clusters = block * zs
     bf16, f32 = jnp.bfloat16, jnp.float32
 
+    core = lax.axis_index("core")
     here, spread = pl.pallas_call(
         join_kernel,
         out_shape=(
@@ -261,24 +228,21 @@
     down = lax.ppermute(here, RING, turn(-1))
     weight = lax.all_to_all(spread, ("z", "ylo"), split_axis=0, concat_axis=0, tiled=True)
     others = lax.ppermute(weight, "core", swap)
+    up, down, here_too = lax.optimization_barrier((up, down, here))
     far = lax.ppermute(up, RING, turn(1))
     pieces = [here, up, down, far]
-    pieces += [lax.ppermute(piece, "core", swap) for piece in pieces]
+    pieces += [lax.ppermute(piece, "core", swap) for piece in (here_too, up, down, far)]
 
     payload = pl.pallas_call(
         functools.partial(sums_kernel, positions),
         out_shape=jax.ShapeDtypeStruct((zs, block + TILE, head_size), bf16),
-        in_specs=[ANY] * (len(pieces) + 2),
+        in_specs=[VMEM] * (len(pieces) + 2),
         out_specs=VMEM,
         scratch_shapes=[
-            pltpu.VMEM((len(pieces),) + here.shape, bf16),
-            pltpu.VMEM(weight.shape, bf16),
-            pltpu.VMEM(weight.shape, bf16),
             pltpu.VMEM(weight.shape, bf16),
             pltpu.VMEM((zs, TILE, head_size), f32),
-            pltpu.SemaphoreType.DMA((len(pieces) + 2,)),
         ],
-        compiler_params=ALONE,
+        compiler_params=PARAMS,
         cost_estimate=pl.CostEstimate(flops=10**9, bytes_accessed=6 * 10**6, transcendentals=0),
     )(*pieces, weight, others)
     arrived = lax.all_to_all(payload, "z", split_axis=0, concat_axis=0, tiled=True)
@@ -302,19 +266,10 @@
     half = lax.all_to_all(owned, ("x", "z"), split_axis=0, concat_axis=0, tiled=True)
     half = half.reshape(xs, zs, block, head_size)
     other = lax.ppermute(half, "core", swap)
-    out = pl.pallas_call(
-        rows_kernel,
-        out_shape=jax.ShapeDtypeStruct((cores, xs, clusters, head_size), f32),
-        in_specs=[ANY, ANY],
-        out_specs=ANY,
-        scratch_shapes=[
-            pltpu.VMEM((cores,) + half.shape, bf16),
-            pltpu.VMEM((cores, xs, clusters, head_size), f32),
-            pltpu.SemaphoreType.DMA((cores * xs,)),
-            pltpu.SemaphoreType.DMA((cores * xs,)),
-        ],
-        compiler_params=ALONE,
-    )(half, other)
+    first = jnp.where(core == 0, half, other)
+    second = jnp.where(core == 0, other, half)
+    out = jnp.stack([first, second]).reshape(cores, xs, cores, xs, SIZES["yhi"], ylos, 8, head_size)
+    out = jnp.transpose(out, (0, 1, 5, 2, 4, 3, 6, 7)).astype(f32)
     return out.reshape(heads * clusters, head_size)
 
 

time: 112 us -> 106 us (0.946)
  Pallas kernels: 10.5 us -> 5.62 us
  waiting for transfers between devices: 9.57 us -> 6.89 us
  starting transfers between devices: 42.5 us -> 44.8 us
  blocking collectives: 47.1 us -> 45 us
  other arithmetic: 0 us -> 1.67 us
    ppermute x4, starting transfers between devices: 10.4 us -> 15.2 us  [per_device(): lax.ppermute(piece, 'core', swap)]
    ppermute x1, waiting for transfers between devices: 6.22 us -> 3.37 us  [per_device(): down = lax.ppermute(here, RING, turn(-1))]
    pallas_call x1, Pallas kernels: 5.64 us -> 3.16 us  [per_device(): pl.pallas_call(functools.partial(sums_kernel, positions), out_shape=jax.S...]
    ppermute x1, starting transfers between devices: 4.57 us -> 2.09 us  [per_device(): far = lax.ppermute(up, RING, turn(1))]
    pallas_call x1 -> x0, Pallas kernels: 2.36 us -> none  [per_device(): pl.pallas_call(rows_kernel, out_shape=jax.ShapeDtypeStruct((cores, xs, cl...]
    all_to_all x1, blocking collectives: 16.2 us -> 14 us  [per_device(): lax.all_to_all(payload, 'z', split_axis=0, concat_axis=0, tiled=True)]
    reshape x0 -> x1, other arithmetic: none -> 1.6 us  [per_device(): return out.reshape(heads * clusters, head_size)]
  transfers between devices with their start and end apart: 10 -> 10, of which waited for: 3 -> 4; matrix products, arithmetic and copies ran while one was open for 0% -> 0% of each run, Pallas kernels for 0% -> 0%
where the time goes in v4:
time: 106 us; the launch traced here: 105 us
  blocking collectives  45 us (42%)
  starting transfers between devices  44.8 us (42%)
  waiting for transfers between devices  6.89 us (6%)
  Pallas kernels  5.62 us (5%)
  other arithmetic  1.67 us (2%)
  local copies, waits for them, and re-layouts  1.07 us (1%)
    all_to_all x1, blocking collectives, per_device(): lax.all_to_all(owned, ('x', 'z'), split_axis=0, concat_axis=0, tiled=True)  16.1 us
    ppermute x4, starting transfers between devices, per_device(): lax.ppermute(piece, 'core', swap)  15.2 us
    all_to_all x1, blocking collectives, per_device(): arrived = lax.all_to_all(shares, Y, split_axis=0, concat_axis=0, tiled=True)  14.9 us
    all_to_all x1, blocking collectives, per_device(): lax.all_to_all(payload, 'z', split_axis=0, concat_axis=0, tiled=True)  14 us
    all_to_all x1, starting transfers between devices, per_device(): lax.all_to_all(spread, ('z', 'ylo'), split_axis=0, concat_axis=0, tiled=T...  11.2 us
    ppermute x1, starting transfers between devices, per_device(): other = lax.ppermute(half, 'core', swap)  7.29 us
    ppermute x1, starting transfers between devices, per_device(): up = lax.ppermute(here, RING, turn(1))  5.22 us
    ppermute x1, waiting for transfers between devices, per_device(): down = lax.ppermute(here, RING, turn(-1))  3.37 us
  transfers between devices with their start and end apart: 10, of which 4 were waited for; matrix products, arithmetic and copies ran while one was open for 0% of the time, Pallas kernels for 0%

profile of v4, /device:TPU:1, one launch (start us, length us, event | category | flops | bytes accessed | tf_op | source)
XLA Modules:
  0.0 105.2 jit_solution(9768551771013928219)
XLA Ops:
  0.0 2.2 %shard_map.46 = (bf16[144,2048]{1,0:T(8,128)(2,1)}, bf16[16,2,64,128]{3,2,1,0:T(8,128)(2,1)}) custom-call(bf16[128,2048]{1,0:T(8,128)(2,1)} %bitcast.12, s32[8,128]{1,0:T(8,128)} %bitcast.13, f32[8,128]{1,0:T(8,128)} %old_ref.1, bf16[64,1024]{1,0:T(8,128)(2,1)} %weight_ref.1), custom_call_target="tpu_custom_call" | custom-call | tf_op jit(solution)/shard_map/pallas_call | solution.py:205
  2.2 5.2 %collective-permute-start = (bf16[144,2048]{1,0:T(8,128)(2,1)}, bf16[144,2048]{1,0:T(8,128)(2,1)S(1)}, u32[]{:S(2)}, u32[]{:S(2)}) collective-permute-start(bf16[144,2048]{1,0:T(8,128)(2,1)} %get-tuple-element.13.refs_0_), channel_id=1, source_target_pairs={{0,1},{1,2},{2,3},{3,0},{16,19},{17,16},{18,17},{19,18},{4,5},{5,6... | collective-permute-start | bytes 1769480 | tf_op jit(solution)/shard_map/ppermute | solution.py:227
  7.4 1.9 %collective-permute-start.1 = (bf16[144,2048]{1,0:T(8,128)(2,1)}, bf16[144,2048]{1,0:T(8,128)(2,1)S(1)}, u32[]{:S(2)}, u32[]{:S(2)}) collective-permute-start(bf16[144,2048]{1,0:T(8,128)(2,1)} %get-tuple-element.13.refs_0_), channel_id=1, source_target_pairs={{0,3},{1,0},{2,1},{3,2},{16,17},{17,18},{18,19},{19,16},{4,7},{5,4... | collective-permute-start | bytes 1769480 | tf_op jit(solution)/shard_map/ppermute | solution.py:228
  9.3 11.2 %all-to-all-start = ((bf16[16,2,64,128]{3,2,1,0:T(8,128)(2,1)}), bf16[16,2,64,128]{3,2,1,0:T(8,128)(2,1)S(1)}, u32[]{:S(2)}, u32[]{:S(2)}) async-start(bf16[16,2,64,128]{3,2,1,0:T(8,128)(2,1)} %get-tuple-element.14), calls=%async_computation | async-start | bytes 1048576 | tf_op jit(solution)/shard_map/all_to_all | solution.py:229
  20.5 0.0 collective-permute-done.refs_1_
  20.5 3.4 %collective-permute-done.1.refs_2_ = bf16[144,2048]{1,0:T(8,128)(2,1)S(1)} collective-permute-done((bf16[144,2048]{1,0:T(8,128)(2,1)}, bf16[144,2048]{1,0:T(8,128)(2,1)S(1)}, u32[]{:S(2)}, u32[]{:S(2)}) %collective-permute-start.1) | collective-permute-done | bytes 589856 | tf_op jit(solution)/shard_map/ppermute | solution.py:228
  23.9 2.1 %collective-permute-start.2 = (bf16[144,2048]{1,0:T(8,128)(2,1)S(1)}, bf16[144,2048]{1,0:T(8,128)(2,1)S(1)}, u32[]{:S(2)}, u32[]{:S(2)}) collective-permute-start(bf16[144,2048]{1,0:T(8,128)(2,1)S(1)} %collective-permute-done.refs_1_), channel_id=1, source_target_pairs={{0,1},{1,2},{2,3},{3,0},{16,19},{17,16},{18,17},{19,18},{4,5},{5,6... | collective-permute-start | bytes 1769480 | tf_op jit(solution)/shard_map/ppermute | solution.py:232
  26.0 4.3 %collective-permute-start.4 = (bf16[144,2048]{1,0:T(8,128)(2,1)S(1)}, bf16[144,2048]{1,0:T(8,128)(2,1)S(1)}, u32[]{:S(2)}, u32[]{:S(2)}) collective-permute-start(bf16[144,2048]{1,0:T(8,128)(2,1)S(1)} %collective-permute-done.refs_1_), channel_id=1, source_target_pairs={{0,16},{16,0},{1,17},{17,1},{2,18},{18,2},{3,19},{19,3},{4,20},{20... | collective-permute-start | bytes 1769480 | tf_op jit(solution)/shard_map/ppermute | solution.py:234
  30.3 1.9 %collective-permute-start.5 = (bf16[144,2048]{1,0:T(8,128)(2,1)S(1)}, bf16[144,2048]{1,0:T(8,128)(2,1)S(1)}, u32[]{:S(2)}, u32[]{:S(2)}) collective-permute-start(bf16[144,2048]{1,0:T(8,128)(2,1)S(1)} %collective-permute-done.1.refs_2_), channel_id=1, source_target_pairs={{0,16},{16,0},{1,17},{17,1},{2,18},{18,2},{3,19},{19,3},{4,20},{20... | collective-permute-start | bytes 1769480 | tf_op jit(solution)/shard_map/ppermute | solution.py:234
  32.2 2.4 %collective-permute-start.3 = (bf16[144,2048]{1,0:T(8,128)(2,1)}, bf16[144,2048]{1,0:T(8,128)(2,1)}, u32[]{:S(2)}, u32[]{:S(2)}) collective-permute-start(bf16[144,2048]{1,0:T(8,128)(2,1)} %get-tuple-element.13.refs_0_), channel_id=1, source_target_pairs={{0,16},{16,0},{1,17},{17,1},{2,18},{18,2},{3,19},{19,3},{4,20},{20... | collective-permute-start | bytes 1769480 | tf_op jit(solution)/shard_map/ppermute | solution.py:234
  34.7 0.2 collective-permute-done.2.refs_3_
  34.8 6.5 %collective-permute-start.6 = (bf16[144,2048]{1,0:T(8,128)(2,1)S(1)}, bf16[144,2048]{1,0:T(8,128)(2,1)}, u32[]{:S(2)}, u32[]{:S(2)}) collective-permute-start(bf16[144,2048]{1,0:T(8,128)(2,1)S(1)} %collective-permute-done.2.refs_3_), channel_id=1, source_target_pairs={{0,16},{16,0},{1,17},{17,1},{2,18},{18,2},{3,19},{19,3},{4,20},{20... | collective-permute-start | bytes 1769480 | tf_op jit(solution)/shard_map/ppermute | solution.py:234
  41.4 0.0 all-to-all-done.refs_8_
  41.4 1.9 %collective-permute-start.7 = (bf16[16,2,64,128]{3,2,1,0:T(8,128)(2,1)S(1)}, bf16[16,2,64,128]{3,2,1,0:T(8,128)(2,1)S(1)}, u32[]{:S(2)}, u32[]{:S(2)}) collective-permute-start(bf16[16,2,64,128]{3,2,1,0:T(8,128)(2,1)S(1)} %all-to-all-done.refs_8_), channel_id=1, source_target_pairs={{0,16},{16,0},{1,17},{17,1},{2,18},{18,2},{3,19},{19,3},{4,20},{20... | collective-permute-start | bytes 1572872 | tf_op jit(solution)/shard_map/ppermute | solution.py:230
  43.3 0.0 collective-permute-done.4.refs_5_
  43.3 0.0 collective-permute-done.5.refs_6_
  43.3 0.0 collective-permute-done.3.refs_4_
  43.3 1.8 %collective-permute-done.7.refs_9_ = bf16[16,2,64,128]{3,2,1,0:T(8,128)(2,1)S(1)} collective-permute-done((bf16[16,2,64,128]{3,2,1,0:T(8,128)(2,1)S(1)}, bf16[16,2,64,128]{3,2,1,0:T(8,128)(2,1)S(1)}, u32[]{:S(2)}, u32[]{:S(2)}) %collective-permute-start.7) | collective-permute-done | bytes 524320 | tf_op jit(solution)/shard_map/ppermute | solution.py:230
  45.2 0.0 collective-permute-done.6.refs_7_
  45.2 0.0 copy-start
  45.2 1.1 %copy-done = bf16[144,2048]{1,0:T(8,128)(2,1)S(1)} copy-done((bf16[144,2048]{1,0:T(8,128)(2,1)S(1)}, bf16[144,2048]{1,0:T(8,128)(2,1)}, u32[]{:S(2)}) %copy-start) | copy-done | bytes 589848
  46.2 3.2 %shard_map.47 = bf16[8,80,128]{2,1,0:T(8,128)(2,1)S(1)} custom-call(bf16[144,2048]{1,0:T(8,128)(2,1)S(1)} %copy-done, bf16[144,2048]{1,0:T(8,128)(2,1)S(1)} %collective-permute-done.refs_1_, bf16[144,2048]{1,0:T(8,128)(2,1)S(1)} %collective-permute-done.1.refs_2_, bf16[144,2048]{1,0:T(8,128)(2,1)S(1)} %collective-permute-done.2.refs_3_, ...), custom_call_target="tpu_custom_call" | custom-call | flops 1000000000 | bytes 6000000 | tf_op jit(solution)/shard_map/pallas_call | solution.py:236
  49.4 14.0 %all_to_all.20.arrived_ref = bf16[8,80,128]{2,1,0:T(8,128)(2,1)S(1)} all-to-all(bf16[8,80,128]{2,1,0:T(8,128)(2,1)S(1)} %shard_map.47), channel_id=1, replica_groups=mesh['z'=8,'ylo'=2,'core'=2,'yhi'=4,'x'=4] {'z'}, dimensions={0} | all-to-all | bytes 327680 | tf_op jit(solution)/shard_map/all_to_all | solution.py:248
  63.4 14.9 %all_to_all.21.arrived_ref = bf16[8,80,128]{2,1,0:T(8,128)(2,1)S(1)} all-to-all(bf16[8,80,128]{2,1,0:T(8,128)(2,1)S(1)} %shard_map.48), channel_id=1, replica_groups=mesh['z'=8,'ylo'=2,'core'=2,'yhi'=4,'x'=4] {'yhi','ylo'}, dimensions={0} | all-to-all | bytes 327680 | tf_op jit(solution)/shard_map/all_to_all | solution.py:257
  78.3 0.2 shard_map.49
  78.6 16.1 %all_to_all.22 = bf16[32,64,128]{2,1,0:T(8,128)(2,1)S(1)} all-to-all(bf16[32,64,128]{2,1,0:T(8,128)(2,1)S(1)} %shard_map.49), channel_id=1, replica_groups=mesh['z'=8,'ylo'=2,'core'=2,'yhi'=4,'x'=4] {'x','z'}, dimensions={0} | all-to-all | bytes 1048576 | tf_op jit(solution)/shard_map/all_to_all | solution.py:266
  94.7 7.3 %collective-permute-start.8 = (bf16[4,8,64,128]{3,2,1,0:T(8,128)(2,1)S(1)}, bf16[4,8,64,128]{3,2,1,0:T(8,128)(2,1)S(1)}, u32[]{:S(2)}, u32[]{:S(2)}) collective-permute-start(bf16[4,8,64,128]{3,2,1,0:T(8,128)(2,1)S(1)} %bitcast.8), channel_id=1, source_target_pairs={{0,16},{16,0},{1,17},{17,1},{2,18},{18,2},{3,19},{19,3},{4,20},{20... | collective-permute-start | bytes 1572872 | tf_op jit(solution)/shard_map/ppermute | solution.py:268
  102.0 1.5 %collective-permute-done.8 = bf16[4,8,64,128]{3,2,1,0:T(8,128)(2,1)S(1)} collective-permute-done((bf16[4,8,64,128]{3,2,1,0:T(8,128)(2,1)S(1)}, bf16[4,8,64,128]{3,2,1,0:T(8,128)(2,1)S(1)}, u32[]{:S(2)}, u32[]{:S(2)}) %collective-permute-start.8) | collective-permute-done | bytes 524320 | tf_op jit(solution)/shard_map/ppermute | solution.py:268
  103.5 0.1 broadcast_select_fusion.1
  103.6 1.6 %copy_convert_fusion = f32[2,4,2,4,4,2,8,128]{7,6,3,4,2,5,1,0:T(8,128)} fusion(bf16[1,4,2,4,4,2,8,128]{7,6,5,4,3,2,1,0:T(8,128)(2,1)S(1)} %bitcast.11, bf16[1,4,2,4,4,2,8,128]{7,6,5,4,3,2,1,0:T(8,128)(2,1)S(1)} %bitcast.10), kind=kLoop, calls=%fused_computation.1 | loop fusion | flops 1048576 | bytes 3145728 | tf_op jit(solution)/shard_map/reshape | solution.py:273
  (1 shorter events, 0.0 us)
Async XLA Ops:
  2.2 18.3 %collective-permute-start = (bf16[144,2048]{1,0:T(8,128)(2,1)}, bf16[144,2048]{1,0:T(8,128)(2,1)S(1)}, u32[]{:S(2)}, u32[]{:S(2)}) collective-permute-start(bf16[144,2048]{1,0:T(8,128)(2,1)} %get-tuple-element.13.refs_0_), channel_id=1, source_target_pairs={{0,1},{1,2},{2,3},{3,0},{16,19},{17,16},{18,17},{19,18},{4,5},{5,6... | collective-permute-start | bytes 1769480 | tf_op jit(solution)/shard_map/ppermute | solution.py:227
  7.4 16.5 %collective-permute-start.1 = (bf16[144,2048]{1,0:T(8,128)(2,1)}, bf16[144,2048]{1,0:T(8,128)(2,1)S(1)}, u32[]{:S(2)}, u32[]{:S(2)}) collective-permute-start(bf16[144,2048]{1,0:T(8,128)(2,1)} %get-tuple-element.13.refs_0_), channel_id=1, source_target_pairs={{0,3},{1,0},{2,1},{3,2},{16,17},{17,18},{18,19},{19,16},{4,7},{5,4... | collective-permute-start | bytes 1769480 | tf_op jit(solution)/shard_map/ppermute | solution.py:228
  9.3 32.0 %all-to-all-start = ((bf16[16,2,64,128]{3,2,1,0:T(8,128)(2,1)}), bf16[16,2,64,128]{3,2,1,0:T(8,128)(2,1)S(1)}, u32[]{:S(2)}, u32[]{:S(2)}) async-start(bf16[16,2,64,128]{3,2,1,0:T(8,128)(2,1)} %get-tuple-element.14), calls=%async_computation | async-start | bytes 1048576 | tf_op jit(solution)/shard_map/all_to_all | solution.py:229
  23.9 10.9 %collective-permute-start.2 = (bf16[144,2048]{1,0:T(8,128)(2,1)S(1)}, bf16[144,2048]{1,0:T(8,128)(2,1)S(1)}, u32[]{:S(2)}, u32[]{:S(2)}) collective-permute-start(bf16[144,2048]{1,0:T(8,128)(2,1)S(1)} %collective-permute-done.refs_1_), channel_id=1, source_target_pairs={{0,1},{1,2},{2,3},{3,0},{16,19},{17,16},{18,17},{19,18},{4,5},{5,6... | collective-permute-start | bytes 1769480 | tf_op jit(solution)/shard_map/ppermute | solution.py:232
  26.0 17.3 %collective-permute-start.4 = (bf16[144,2048]{1,0:T(8,128)(2,1)S(1)}, bf16[144,2048]{1,0:T(8,128)(2,1)S(1)}, u32[]{:S(2)}, u32[]{:S(2)}) collective-permute-start(bf16[144,2048]{1,0:T(8,128)(2,1)S(1)} %collective-permute-done.refs_1_), channel_id=1, source_target_pairs={{0,16},{16,0},{1,17},{17,1},{2,18},{18,2},{3,19},{19,3},{4,20},{20... | collective-permute-start | bytes 1769480 | tf_op jit(solution)/shard_map/ppermute | solution.py:234
  30.3 13.0 %collective-permute-start.5 = (bf16[144,2048]{1,0:T(8,128)(2,1)S(1)}, bf16[144,2048]{1,0:T(8,128)(2,1)S(1)}, u32[]{:S(2)}, u32[]{:S(2)}) collective-permute-start(bf16[144,2048]{1,0:T(8,128)(2,1)S(1)} %collective-permute-done.1.refs_2_), channel_id=1, source_target_pairs={{0,16},{16,0},{1,17},{17,1},{2,18},{18,2},{3,19},{19,3},{4,20},{20... | collective-permute-start | bytes 1769480 | tf_op jit(solution)/shard_map/ppermute | solution.py:234
  32.2 11.1 %collective-permute-start.3 = (bf16[144,2048]{1,0:T(8,128)(2,1)}, bf16[144,2048]{1,0:T(8,128)(2,1)}, u32[]{:S(2)}, u32[]{:S(2)}) collective-permute-start(bf16[144,2048]{1,0:T(8,128)(2,1)} %get-tuple-element.13.refs_0_), channel_id=1, source_target_pairs={{0,16},{16,0},{1,17},{17,1},{2,18},{18,2},{3,19},{19,3},{4,20},{20... | collective-permute-start | bytes 1769480 | tf_op jit(solution)/shard_map/ppermute | solution.py:234
  34.8 10.4 %collective-permute-start.6 = (bf16[144,2048]{1,0:T(8,128)(2,1)S(1)}, bf16[144,2048]{1,0:T(8,128)(2,1)}, u32[]{:S(2)}, u32[]{:S(2)}) collective-permute-start(bf16[144,2048]{1,0:T(8,128)(2,1)S(1)} %collective-permute-done.2.refs_3_), channel_id=1, source_target_pairs={{0,16},{16,0},{1,17},{17,1},{2,18},{18,2},{3,19},{19,3},{4,20},{20... | collective-permute-start | bytes 1769480 | tf_op jit(solution)/shard_map/ppermute | solution.py:234
  41.4 3.8 %collective-permute-start.7 = (bf16[16,2,64,128]{3,2,1,0:T(8,128)(2,1)S(1)}, bf16[16,2,64,128]{3,2,1,0:T(8,128)(2,1)S(1)}, u32[]{:S(2)}, u32[]{:S(2)}) collective-permute-start(bf16[16,2,64,128]{3,2,1,0:T(8,128)(2,1)S(1)} %all-to-all-done.refs_8_), channel_id=1, source_target_pairs={{0,16},{16,0},{1,17},{17,1},{2,18},{18,2},{3,19},{19,3},{4,20},{20... | collective-permute-start | bytes 1572872 | tf_op jit(solution)/shard_map/ppermute | solution.py:230
  45.2 1.1 %copy-start = (bf16[144,2048]{1,0:T(8,128)(2,1)S(1)}, bf16[144,2048]{1,0:T(8,128)(2,1)}, u32[]{:S(2)}) copy-start(bf16[144,2048]{1,0:T(8,128)(2,1)} %get-tuple-element.13.refs_0_) | copy-start | bytes 1769476
  94.7 8.8 %collective-permute-start.8 = (bf16[4,8,64,128]{3,2,1,0:T(8,128)(2,1)S(1)}, bf16[4,8,64,128]{3,2,1,0:T(8,128)(2,1)S(1)}, u32[]{:S(2)}, u32[]{:S(2)}) collective-permute-start(bf16[4,8,64,128]{3,2,1,0:T(8,128)(2,1)S(1)} %bitcast.8), channel_id=1, source_target_pairs={{0,16},{16,0},{1,17},{17,1},{2,18},{18,2},{3,19},{19,3},{4,20},{20... | collective-permute-start | bytes 1572872 | tf_op jit(solution)/shard_map/ppermute | solution.py:268

commit v5 on v4

--- a/solution.py
+++ b/solution.py
@@ -18,6 +18,7 @@
 TILE = 16
 COUNT_BASE = 64.0
 OLD_AT = 8
+CLUSTERS = 512
 
 VMEM = pl.BlockSpec(memory_space=pltpu.VMEM)
 ANY = pl.BlockSpec(memory_space=pl.ANY)
@@ -97,35 +98,26 @@
     spread.wait()
 
 
-def sums_kernel(positions, *refs):
-    pieces = refs[:8]
-    mine_ref, others_ref, out_ref, weight, old_ref = refs[8:]
-    owners, rows, head_size = out_ref.shape
-    block = rows - TILE
-    clusters = owners * block
+def copy_kernel(from_ref, to_ref, sem):
+    copy = pltpu.make_async_copy(from_ref, to_ref, sem)
+    copy.start()
+    copy.wait()
+
+
+def add_pieces(positions, pieces, whole, old_ref):
+    owners, _, head_size = old_ref.shape
     xs = owners // 2
+    clusters = CLUSTERS
     bf16, f32 = jnp.bfloat16, jnp.float32
     core, x, z = lax.axis_index("core"), lax.axis_index("x"), lax.axis_index("z")
     head = core * xs + x
-    model_width = pieces[0].shape[1]
-    heads = model_width // (2 * positions)
+    heads = whole.shape[0] // (2 * positions)
     first = pl.multiple_of(head * positions, positions)
     second = pl.multiple_of(first + heads * positions, positions)
     cluster = lax.broadcasted_iota(jnp.int32, (clusters, positions), 0).astype(f32)
     mine = (head == z).astype(f32)
-    @pl.when(core == 0)
-    def _():
-        weight[:, 0] = mine_ref[:, 0]
-        weight[:, 1] = others_ref[:, 0]
-
-    @pl.when(core == 1)
-    def _():
-        weight[:, 1] = mine_ref[:, 1]
-        weight[:, 0] = others_ref[:, 1]
-
-    whole = weight[...].reshape(model_width, head_size)
     keys, hots = [], []
-    for number, piece in enumerate(pieces):
+    for piece, kind, other in pieces:
         key = jnp.dot(piece[:positions, :], whole, preferred_element_type=f32)
         mean = jnp.mean(key * key, axis=1, keepdims=True)
         keys.append((key * lax.rsqrt(mean + EPSILON)).astype(bf16))
@@ -133,7 +125,6 @@
         low = piece[positions:, pl.ds(second, positions)].astype(f32)
         ids = high[:1] * 32.0 + low[:1]
         hots.append(jnp.where(cluster == ids, 1.0, 0.0).astype(bf16))
-        other, kind = divmod(number, xs)
         source = 1 - core if other else core
         sign = 2 * source - 1
         moved = (x + (0, sign, -sign, 2)[kind] + xs) % xs
@@ -143,13 +134,49 @@
     counts = lax.dot_general(
         jnp.ones((8, one_hot.shape[1]), bf16), one_hot, (((1,), (1,)), ((), ())),
         preferred_element_type=f32,
-    )[:1]
-    empty = jnp.zeros((1, head_size - block), f32)
+    )
+    return sums, counts
+
+
+def near_kernel(positions, *refs):
+    arrays, (mine_ref, others_ref, weight_ref, sums_ref, counts_ref, old_ref) = refs[:-6], refs[-6:]
+    kinds = len(arrays) // 2
+    core = lax.axis_index("core")
+
+    @pl.when(core == 0)
+    def _():
+        weight_ref[:, 0] = mine_ref[:, 0]
+        weight_ref[:, 1] = others_ref[:, 0]
+
+    @pl.when(core == 1)
+    def _():
+        weight_ref[:, 1] = mine_ref[:, 1]
+        weight_ref[:, 0] = others_ref[:, 1]
+
+    whole = weight_ref[...].reshape(arrays[0].shape[1], weight_ref.shape[3])
+    pieces = [(piece, number % kinds, number // kinds) for number, piece in enumerate(arrays)]
+    old_ref[...] = jnp.zeros_like(old_ref)
+    sums_ref[...], counts_ref[...] = add_pieces(positions, pieces, whole, old_ref)
+
+
+def far_kernel(
+    positions, far_ref, over_ref, weight_ref, near_sums_ref, near_counts_ref, near_old_ref,
+    out_ref, old_ref,
+):
+    owners, rows, head_size = out_ref.shape
+    block = rows - TILE
+    whole = weight_ref[...].reshape(far_ref.shape[1], head_size)
+    old_ref[...] = near_old_ref[...]
+    pieces = [(far_ref, 3, 0), (over_ref, 3, 1)]
+    sums, counts = add_pieces(positions, pieces, whole, old_ref)
+    sums += near_sums_ref[...]
+    counts = (counts + near_counts_ref[...])[:1]
+    empty = jnp.zeros((1, head_size - block), jnp.float32)
     for owner in range(owners):
         own = slice(owner * block, (owner + 1) * block)
-        out_ref[owner, :block, :] = sums[own].astype(bf16)
+        out_ref[owner, :block, :] = sums[own].astype(jnp.bfloat16)
         padded = jnp.concatenate([counts[:, own], empty], axis=1)
-        out_ref[owner, block:, :] = count_lines(padded, old_ref[owner]).astype(bf16)
+        out_ref[owner, block:, :] = count_lines(padded, old_ref[owner]).astype(jnp.bfloat16)
 
 
 def share_kernel(arrived_ref, out_ref):
@@ -227,24 +254,45 @@
     up = lax.ppermute(here, RING, turn(1))
     down = lax.ppermute(here, RING, turn(-1))
     weight = lax.all_to_all(spread, ("z", "ylo"), split_axis=0, concat_axis=0, tiled=True)
+    up, down = lax.optimization_barrier((up, down))
+    far = lax.ppermute(up, RING, turn(1))
+    near = pl.pallas_call(
+        copy_kernel,
+        out_shape=jax.ShapeDtypeStruct(here.shape, here.dtype),
+        in_specs=[ANY],
+        out_specs=ANY,
+        scratch_shapes=[pltpu.SemaphoreType.DMA],
+        compiler_params=PARAMS,
+    )(here)
+    near_over = lax.ppermute(near, "core", swap)
+    up_over = lax.ppermute(up, "core", swap)
+    down_over = lax.ppermute(down, "core", swap)
+    weight, near_over = lax.optimization_barrier((weight, near_over))
     others = lax.ppermute(weight, "core", swap)
-    up, down, here_too = lax.optimization_barrier((up, down, here))
-    far = lax.ppermute(up, RING, turn(1))
-    pieces = [here, up, down, far]
-    pieces += [lax.ppermute(piece, "core", swap) for piece in (here_too, up, down, far)]
-
+    far_over = lax.ppermute(far, "core", swap)
+
+    whole, *partial = pl.pallas_call(
+        functools.partial(near_kernel, positions),
+        out_shape=(
+            jax.ShapeDtypeStruct(weight.shape[:3] + (head_size,), bf16),
+            jax.ShapeDtypeStruct((clusters, head_size), f32),
+            jax.ShapeDtypeStruct((8, clusters), f32),
+            jax.ShapeDtypeStruct((zs, TILE, head_size), f32),
+        ),
+        in_specs=[VMEM] * 8,
+        out_specs=(VMEM,) * 4,
+        compiler_params=PARAMS,
+        cost_estimate=pl.CostEstimate(flops=2 * 10**9, bytes_accessed=6 * 10**6, transcendentals=0),
+    )(near, up, down, near_over, up_over, down_over, weight, others)
     payload = pl.pallas_call(
-        functools.partial(sums_kernel, positions),
+        functools.partial(far_kernel, positions),
         out_shape=jax.ShapeDtypeStruct((zs, block + TILE, head_size), bf16),
-        in_specs=[VMEM] * (len(pieces) + 2),
+        in_specs=[VMEM] * 6,
         out_specs=VMEM,
-        scratch_shapes=[
-            pltpu.VMEM(weight.shape, bf16),
-            pltpu.VMEM((zs, TILE, head_size), f32),
-        ],
-        compiler_params=PARAMS,
-        cost_estimate=pl.CostEstimate(flops=10**9, bytes_accessed=6 * 10**6, transcendentals=0),
-    )(*pieces, weight, others)
+        scratch_shapes=[pltpu.VMEM((zs, TILE, head_size), f32)],
+        compiler_params=PARAMS,
+        cost_estimate=pl.CostEstimate(flops=10**9, bytes_accessed=2 * 10**6, transcendentals=0),
+    )(far, far_over, whole, *partial)
     arrived = lax.all_to_all(payload, "z", split_axis=0, concat_axis=0, tiled=True)
 
     shares = pl.pallas_call(

time: 106 us -> 101 us (0.953)
  waiting for transfers between devices: 6.89 us -> 4.02 us
  starting transfers between devices: 44.8 us -> 43.4 us
    ppermute x4, starting transfers between devices: 15.2 us -> 9.86 us  [the longest x1 3.61 us: per_device(): near_over = lax.ppermute(near, 'core', swap)]
    ppermute x1, waiting for transfers between devices: 3.37 us -> 0.01 us  [per_device(): down = lax.ppermute(here, RING, turn(-1))]
    ppermute x1, starting transfers between devices: 1.92 us -> 4.74 us  [per_device(): others = lax.ppermute(weight, 'core', swap)]
    all_to_all x1, waiting for transfers between devices: 0.01 us -> 2.49 us  [per_device(): lax.all_to_all(spread, ('z', 'ylo'), split_axis=0, concat_axis=0, tiled=T...]
    ppermute x1, waiting for transfers between devices: 1.84 us -> 0.01 us  [per_device(): others = lax.ppermute(weight, 'core', swap)]
    ppermute x1, starting transfers between devices: 2.09 us -> 3.18 us  [per_device(): far = lax.ppermute(up, RING, turn(1))]
    pallas_call x1 -> x3, Pallas kernels: 3.16 us -> 3.55 us  [the longest x1 2.64 us: per_device(): pl.pallas_call(functools.partial(near_kernel, positions), out_shape=(jax....]
  transfers between devices with their start and end apart: 10 -> 10, of which waited for: 4 -> 2; matrix products, arithmetic and copies ran while one was open for 0% -> 0% of each run, Pallas kernels for 0% -> 3%
where the time goes in v5:
time: 101 us
  blocking collectives  44.2 us (44%)
  starting transfers between devices  43.4 us (43%)
  Pallas kernels  6 us (6%)
  waiting for transfers between devices  4.02 us (4%)
  other arithmetic  1.67 us (2%)
  local copies, waits for them, and re-layouts  1.06 us (1%)
    all_to_all x1, blocking collectives, per_device(): lax.all_to_all(owned, ('x', 'z'), split_axis=0, concat_axis=0, tiled=True)  15.7 us
    all_to_all x1, blocking collectives, per_device(): arrived = lax.all_to_all(shares, Y, split_axis=0, concat_axis=0, tiled=True)  14.4 us
    all_to_all x1, blocking collectives, per_device(): lax.all_to_all(payload, 'z', split_axis=0, concat_axis=0, tiled=True)  14.1 us
    all_to_all x1, starting transfers between devices, per_device(): lax.all_to_all(spread, ('z', 'ylo'), split_axis=0, concat_axis=0, tiled=T...  11.2 us
    ppermute x1, starting transfers between devices, per_device(): other = lax.ppermute(half, 'core', swap)  7.32 us
    ppermute x1, starting transfers between devices, per_device(): up = lax.ppermute(here, RING, turn(1))  5.22 us
    ppermute x1, starting transfers between devices, per_device(): others = lax.ppermute(weight, 'core', swap)  4.74 us
    ppermute x1, starting transfers between devices, per_device(): near_over = lax.ppermute(near, 'core', swap)  3.61 us
  transfers between devices with their start and end apart: 10, of which 2 were waited for; matrix products, arithmetic and copies ran while one was open for 0% of the time, Pallas kernels for 3%

profile of v5, /device:TPU:1, one launch (start us, length us, event | category | flops | bytes accessed | tf_op | source)
XLA Modules:
  0.0 100.5 jit_solution(17461160676797803444)
XLA Ops:
  0.0 2.2 %shard_map.46 = (bf16[144,2048]{1,0:T(8,128)(2,1)}, bf16[16,2,64,128]{3,2,1,0:T(8,128)(2,1)}) custom-call(bf16[128,2048]{1,0:T(8,128)(2,1)} %bitcast.12, s32[8,128]{1,0:T(8,128)} %bitcast.13, f32[8,128]{1,0:T(8,128)} %old_ref.1, bf16[64,1024]{1,0:T(8,128)(2,1)} %weight_ref.1), custom_call_target="tpu_custom_call" | custom-call | tf_op jit(solution)/shard_map/pallas_call | solution.py:232
  2.2 5.2 %collective-permute-start = (bf16[144,2048]{1,0:T(8,128)(2,1)}, bf16[144,2048]{1,0:T(8,128)(2,1)S(1)}, u32[]{:S(2)}, u32[]{:S(2)}) collective-permute-start(bf16[144,2048]{1,0:T(8,128)(2,1)} %get-tuple-element.15.from_ref), channel_id=1, source_target_pairs={{0,1},{1,2},{2,3},{3,0},{16,19},{17,16},{18,17},{19,18},{4,5},{5,6... | collective-permute-start | bytes 1769480 | tf_op jit(solution)/shard_map/ppermute | solution.py:254
  7.4 1.9 %collective-permute-start.1 = (bf16[144,2048]{1,0:T(8,128)(2,1)}, bf16[144,2048]{1,0:T(8,128)(2,1)S(1)}, u32[]{:S(2)}, u32[]{:S(2)}) collective-permute-start(bf16[144,2048]{1,0:T(8,128)(2,1)} %get-tuple-element.15.from_ref), channel_id=1, source_target_pairs={{0,3},{1,0},{2,1},{3,2},{16,17},{17,18},{18,19},{19,16},{4,7},{5,4... | collective-permute-start | bytes 1769480 | tf_op jit(solution)/shard_map/ppermute | solution.py:255
  9.3 11.2 %all-to-all-start = ((bf16[16,2,64,128]{3,2,1,0:T(8,128)(2,1)}), bf16[16,2,64,128]{3,2,1,0:T(8,128)(2,1)S(1)}, u32[]{:S(2)}, u32[]{:S(2)}) async-start(bf16[16,2,64,128]{3,2,1,0:T(8,128)(2,1)} %get-tuple-element.18), calls=%async_computation | async-start | bytes 1048576 | tf_op jit(solution)/shard_map/all_to_all | solution.py:256
  20.5 0.0 copy-start
  20.5 1.1 %copy-done = bf16[144,2048]{1,0:T(8,128)(2,1)S(1)} copy-done((bf16[144,2048]{1,0:T(8,128)(2,1)S(1)}, bf16[144,2048]{1,0:T(8,128)(2,1)}, u32[]{:S(2)}) %copy-start) | copy-done | bytes 589848
  21.6 0.1 shard_map.47.refs_0_
  21.7 3.6 %collective-permute-start.4 = (bf16[144,2048]{1,0:T(8,128)(2,1)S(1)}, bf16[144,2048]{1,0:T(8,128)(2,1)S(1)}, u32[]{:S(2)}, u32[]{:S(2)}) collective-permute-start(bf16[144,2048]{1,0:T(8,128)(2,1)S(1)} %shard_map.47.refs_0_), channel_id=1, source_target_pairs={{0,16},{16,0},{1,17},{17,1},{2,18},{18,2},{3,19},{19,3},{4,20},{20... | collective-permute-start | bytes 1769480 | tf_op jit(solution)/shard_map/ppermute | solution.py:267
  25.3 0.0 collective-permute-done.refs_1_
  25.3 0.0 collective-permute-done.1.refs_2_
  25.3 3.2 %collective-permute-start.2 = (bf16[144,2048]{1,0:T(8,128)(2,1)S(1)}, bf16[144,2048]{1,0:T(8,128)(2,1)S(1)}, u32[]{:S(2)}, u32[]{:S(2)}) collective-permute-start(bf16[144,2048]{1,0:T(8,128)(2,1)S(1)} %collective-permute-done.refs_1_), channel_id=1, source_target_pairs={{0,1},{1,2},{2,3},{3,0},{16,19},{17,16},{18,17},{19,18},{4,5},{5,6... | collective-permute-start | bytes 1769480 | tf_op jit(solution)/shard_map/ppermute | solution.py:258
  28.5 1.9 %collective-permute-start.5 = (bf16[144,2048]{1,0:T(8,128)(2,1)S(1)}, bf16[144,2048]{1,0:T(8,128)(2,1)}, u32[]{:S(2)}, u32[]{:S(2)}) collective-permute-start(bf16[144,2048]{1,0:T(8,128)(2,1)S(1)} %collective-permute-done.refs_1_), channel_id=1, source_target_pairs={{0,16},{16,0},{1,17},{17,1},{2,18},{18,2},{3,19},{19,3},{4,20},{20... | collective-permute-start | bytes 1769480 | tf_op jit(solution)/shard_map/ppermute | solution.py:268
  30.5 2.4 %collective-permute-start.6 = (bf16[144,2048]{1,0:T(8,128)(2,1)S(1)}, bf16[144,2048]{1,0:T(8,128)(2,1)}, u32[]{:S(2)}, u32[]{:S(2)}) collective-permute-start(bf16[144,2048]{1,0:T(8,128)(2,1)S(1)} %collective-permute-done.1.refs_2_), channel_id=1, source_target_pairs={{0,16},{16,0},{1,17},{17,1},{2,18},{18,2},{3,19},{19,3},{4,20},{20... | collective-permute-start | bytes 1769480 | tf_op jit(solution)/shard_map/ppermute | solution.py:269
  32.9 0.0 collective-permute-done.4.refs_3_
  32.9 2.5 %all-to-all-done.refs_6_ = bf16[16,2,64,128]{3,2,1,0:T(8,128)(2,1)S(1)} async-done(((bf16[16,2,64,128]{3,2,1,0:T(8,128)(2,1)}), bf16[16,2,64,128]{3,2,1,0:T(8,128)(2,1)S(1)}, u32[]{:S(2)}, u32[]{:S(2)}) %all-to-all-start) | async-done | bytes 524320 | tf_op jit(solution)/shard_map/all_to_all | solution.py:256
  35.4 4.7 %collective-permute-start.7 = (bf16[16,2,64,128]{3,2,1,0:T(8,128)(2,1)S(1)}, bf16[16,2,64,128]{3,2,1,0:T(8,128)(2,1)S(1)}, u32[]{:S(2)}, u32[]{:S(2)}) collective-permute-start(bf16[16,2,64,128]{3,2,1,0:T(8,128)(2,1)S(1)} %all-to-all-done.refs_6_), channel_id=1, source_target_pairs={{0,16},{16,0},{1,17},{17,1},{2,18},{18,2},{3,19},{19,3},{4,20},{20... | collective-permute-start | bytes 1572872 | tf_op jit(solution)/shard_map/ppermute | solution.py:271
  40.1 0.0 collective-permute-done.2.far_ref
  40.1 1.9 %collective-permute-start.3 = (bf16[144,2048]{1,0:T(8,128)(2,1)S(1)}, bf16[144,2048]{1,0:T(8,128)(2,1)S(1)}, u32[]{:S(2)}, u32[]{:S(2)}) collective-permute-start(bf16[144,2048]{1,0:T(8,128)(2,1)S(1)} %collective-permute-done.2.far_ref), channel_id=1, source_target_pairs={{0,16},{16,0},{1,17},{17,1},{2,18},{18,2},{3,19},{19,3},{4,20},{20... | collective-permute-start | bytes 1769480 | tf_op jit(solution)/shard_map/ppermute | solution.py:272
  42.1 0.0 collective-permute-done.5.refs_4_
  42.1 0.0 collective-permute-done.6.refs_5_
  42.1 0.0 collective-permute-done.7.refs_7_
  42.1 2.6 %shard_map.48 = (bf16[16,2,64,128]{3,2,1,0:T(8,128)(2,1)S(1)}, f32[512,128]{1,0:T(8,128)S(1)}, f32[8,512]{1,0:T(8,128)S(1)}, f32[8,16,128]{2,1,0:T(8,128)S(1)}) custom-call(bf16[144,2048]{1,0:T(8,128)(2,1)S(1)} %shard_map.47.refs_0_, bf16[144,2048]{1,0:T(8,128)(2,1)S(1)} %collective-permute-done.refs_1_, ...), custom_call_target="tpu_custom_call" | custom-call | flops 2000000000 | bytes 6000000 | tf_op jit(solution)/shard_map/pallas_call | solution.py:274
  44.7 0.0 collective-permute-done.3.over_ref
  44.8 0.8 shard_map.49
  45.5 14.1 %all_to_all.20.arrived_ref = bf16[8,80,128]{2,1,0:T(8,128)(2,1)S(1)} all-to-all(bf16[8,80,128]{2,1,0:T(8,128)(2,1)S(1)} %shard_map.49), channel_id=1, replica_groups=mesh['z'=8,'ylo'=2,'core'=2,'yhi'=4,'x'=4] {'z'}, dimensions={0} | all-to-all | bytes 327680 | tf_op jit(solution)/shard_map/all_to_all | solution.py:296
  59.6 14.4 %all_to_all.21.arrived_ref = bf16[8,80,128]{2,1,0:T(8,128)(2,1)S(1)} all-to-all(bf16[8,80,128]{2,1,0:T(8,128)(2,1)S(1)} %shard_map.50), channel_id=1, replica_groups=mesh['z'=8,'ylo'=2,'core'=2,'yhi'=4,'x'=4] {'yhi','ylo'}, dimensions={0} | all-to-all | bytes 327680 | tf_op jit(solution)/shard_map/all_to_all | solution.py:305
  74.0 0.2 shard_map.51
  74.3 15.7 %all_to_all.22 = bf16[32,64,128]{2,1,0:T(8,128)(2,1)S(1)} all-to-all(bf16[32,64,128]{2,1,0:T(8,128)(2,1)S(1)} %shard_map.51), channel_id=1, replica_groups=mesh['z'=8,'ylo'=2,'core'=2,'yhi'=4,'x'=4] {'x','z'}, dimensions={0} | all-to-all | bytes 1048576 | tf_op jit(solution)/shard_map/all_to_all | solution.py:314
  90.0 7.3 %collective-permute-start.8 = (bf16[4,8,64,128]{3,2,1,0:T(8,128)(2,1)S(1)}, bf16[4,8,64,128]{3,2,1,0:T(8,128)(2,1)S(1)}, u32[]{:S(2)}, u32[]{:S(2)}) collective-permute-start(bf16[4,8,64,128]{3,2,1,0:T(8,128)(2,1)S(1)} %bitcast.8), channel_id=1, source_target_pairs={{0,16},{16,0},{1,17},{17,1},{2,18},{18,2},{3,19},{19,3},{4,20},{20... | collective-permute-start | bytes 1572872 | tf_op jit(solution)/shard_map/ppermute | solution.py:316
  97.3 1.5 %collective-permute-done.8 = bf16[4,8,64,128]{3,2,1,0:T(8,128)(2,1)S(1)} collective-permute-done((bf16[4,8,64,128]{3,2,1,0:T(8,128)(2,1)S(1)}, bf16[4,8,64,128]{3,2,1,0:T(8,128)(2,1)S(1)}, u32[]{:S(2)}, u32[]{:S(2)}) %collective-permute-start.8) | collective-permute-done | bytes 524320 | tf_op jit(solution)/shard_map/ppermute | solution.py:316
  98.8 0.1 broadcast_select_fusion.1
  98.9 1.6 %copy_convert_fusion = f32[2,4,2,4,4,2,8,128]{7,6,3,4,2,5,1,0:T(8,128)} fusion(bf16[1,4,2,4,4,2,8,128]{7,6,5,4,3,2,1,0:T(8,128)(2,1)S(1)} %bitcast.11, bf16[1,4,2,4,4,2,8,128]{7,6,5,4,3,2,1,0:T(8,128)(2,1)S(1)} %bitcast.10), kind=kLoop, calls=%fused_computation.1 | loop fusion | flops 1048576 | bytes 3145728 | tf_op jit(solution)/shard_map/reshape | solution.py:321
  (1 shorter events, 0.0 us)
Async XLA Ops:
  2.2 23.1 %collective-permute-start = (bf16[144,2048]{1,0:T(8,128)(2,1)}, bf16[144,2048]{1,0:T(8,128)(2,1)S(1)}, u32[]{:S(2)}, u32[]{:S(2)}) collective-permute-start(bf16[144,2048]{1,0:T(8,128)(2,1)} %get-tuple-element.15.from_ref), channel_id=1, source_target_pairs={{0,1},{1,2},{2,3},{3,0},{16,19},{17,16},{18,17},{19,18},{4,5},{5,6... | collective-permute-start | bytes 1769480 | tf_op jit(solution)/shard_map/ppermute | solution.py:254
  7.4 17.9 %collective-permute-start.1 = (bf16[144,2048]{1,0:T(8,128)(2,1)}, bf16[144,2048]{1,0:T(8,128)(2,1)S(1)}, u32[]{:S(2)}, u32[]{:S(2)}) collective-permute-start(bf16[144,2048]{1,0:T(8,128)(2,1)} %get-tuple-element.15.from_ref), channel_id=1, source_target_pairs={{0,3},{1,0},{2,1},{3,2},{16,17},{17,18},{18,19},{19,16},{4,7},{5,4... | collective-permute-start | bytes 1769480 | tf_op jit(solution)/shard_map/ppermute | solution.py:255
  9.3 26.0 %all-to-all-start = ((bf16[16,2,64,128]{3,2,1,0:T(8,128)(2,1)}), bf16[16,2,64,128]{3,2,1,0:T(8,128)(2,1)S(1)}, u32[]{:S(2)}, u32[]{:S(2)}) async-start(bf16[16,2,64,128]{3,2,1,0:T(8,128)(2,1)} %get-tuple-element.18), calls=%async_computation | async-start | bytes 1048576 | tf_op jit(solution)/shard_map/all_to_all | solution.py:256
  20.5 1.1 %copy-start = (bf16[144,2048]{1,0:T(8,128)(2,1)S(1)}, bf16[144,2048]{1,0:T(8,128)(2,1)}, u32[]{:S(2)}) copy-start(bf16[144,2048]{1,0:T(8,128)(2,1)} %get-tuple-element.15.from_ref) | copy-start | bytes 1769476
  21.7 11.2 %collective-permute-start.4 = (bf16[144,2048]{1,0:T(8,128)(2,1)S(1)}, bf16[144,2048]{1,0:T(8,128)(2,1)S(1)}, u32[]{:S(2)}, u32[]{:S(2)}) collective-permute-start(bf16[144,2048]{1,0:T(8,128)(2,1)S(1)} %shard_map.47.refs_0_), channel_id=1, source_target_pairs={{0,16},{16,0},{1,17},{17,1},{2,18},{18,2},{3,19},{19,3},{4,20},{20... | collective-permute-start | bytes 1769480 | tf_op jit(solution)/shard_map/ppermute | solution.py:267
  25.3 14.8 %collective-permute-start.2 = (bf16[144,2048]{1,0:T(8,128)(2,1)S(1)}, bf16[144,2048]{1,0:T(8,128)(2,1)S(1)}, u32[]{:S(2)}, u32[]{:S(2)}) collective-permute-start(bf16[144,2048]{1,0:T(8,128)(2,1)S(1)} %collective-permute-done.refs_1_), channel_id=1, source_target_pairs={{0,1},{1,2},{2,3},{3,0},{16,19},{17,16},{18,17},{19,18},{4,5},{5,6... | collective-permute-start | bytes 1769480 | tf_op jit(solution)/shard_map/ppermute | solution.py:258
  28.5 13.5 %collective-permute-start.5 = (bf16[144,2048]{1,0:T(8,128)(2,1)S(1)}, bf16[144,2048]{1,0:T(8,128)(2,1)}, u32[]{:S(2)}, u32[]{:S(2)}) collective-permute-start(bf16[144,2048]{1,0:T(8,128)(2,1)S(1)} %collective-permute-done.refs_1_), channel_id=1, source_target_pairs={{0,16},{16,0},{1,17},{17,1},{2,18},{18,2},{3,19},{19,3},{4,20},{20... | collective-permute-start | bytes 1769480 | tf_op jit(solution)/shard_map/ppermute | solution.py:268
  30.5 11.6 %collective-permute-start.6 = (bf16[144,2048]{1,0:T(8,128)(2,1)S(1)}, bf16[144,2048]{1,0:T(8,128)(2,1)}, u32[]{:S(2)}, u32[]{:S(2)}) collective-permute-start(bf16[144,2048]{1,0:T(8,128)(2,1)S(1)} %collective-permute-done.1.refs_2_), channel_id=1, source_target_pairs={{0,16},{16,0},{1,17},{17,1},{2,18},{18,2},{3,19},{19,3},{4,20},{20... | collective-permute-start | bytes 1769480 | tf_op jit(solution)/shard_map/ppermute | solution.py:269
  35.4 6.7 %collective-permute-start.7 = (bf16[16,2,64,128]{3,2,1,0:T(8,128)(2,1)S(1)}, bf16[16,2,64,128]{3,2,1,0:T(8,128)(2,1)S(1)}, u32[]{:S(2)}, u32[]{:S(2)}) collective-permute-start(bf16[16,2,64,128]{3,2,1,0:T(8,128)(2,1)S(1)} %all-to-all-done.refs_6_), channel_id=1, source_target_pairs={{0,16},{16,0},{1,17},{17,1},{2,18},{18,2},{3,19},{19,3},{4,20},{20... | collective-permute-start | bytes 1572872 | tf_op jit(solution)/shard_map/ppermute | solution.py:271
  40.1 4.6 %collective-permute-start.3 = (bf16[144,2048]{1,0:T(8,128)(2,1)S(1)}, bf16[144,2048]{1,0:T(8,128)(2,1)S(1)}, u32[]{:S(2)}, u32[]{:S(2)}) collective-permute-start(bf16[144,2048]{1,0:T(8,128)(2,1)S(1)} %collective-permute-done.2.far_ref), channel_id=1, source_target_pairs={{0,16},{16,0},{1,17},{17,1},{2,18},{18,2},{3,19},{19,3},{4,20},{20... | collective-permute-start | bytes 1769480 | tf_op jit(solution)/shard_map/ppermute | solution.py:272
  90.0 8.8 %collective-permute-start.8 = (bf16[4,8,64,128]{3,2,1,0:T(8,128)(2,1)S(1)}, bf16[4,8,64,128]{3,2,1,0:T(8,128)(2,1)S(1)}, u32[]{:S(2)}, u32[]{:S(2)}) collective-permute-start(bf16[4,8,64,128]{3,2,1,0:T(8,128)(2,1)S(1)} %bitcast.8), channel_id=1, source_target_pairs={{0,16},{16,0},{1,17},{17,1},{2,18},{18,2},{3,19},{19,3},{4,20},{20... | collective-permute-start | bytes 1572872 | tf_op jit(solution)/shard_map/ppermute | solution.py:316

commit v6 on v5

--- a/solution.py
+++ b/solution.py
@@ -117,7 +117,9 @@
     cluster = lax.broadcasted_iota(jnp.int32, (clusters, positions), 0).astype(f32)
     mine = (head == z).astype(f32)
     keys, hots = [], []
-    for piece, kind, other in pieces:
+    for piece, kind, other, move in pieces:
+        if move is not None:
+            move.wait()
         key = jnp.dot(piece[:positions, :], whole, preferred_element_type=f32)
         mean = jnp.mean(key * key, axis=1, keepdims=True)
         keys.append((key * lax.rsqrt(mean + EPSILON)).astype(bf16))
@@ -139,8 +141,16 @@
 
 
 def near_kernel(positions, *refs):
-    arrays, (mine_ref, others_ref, weight_ref, sums_ref, counts_ref, old_ref) = refs[:-6], refs[-6:]
+    arrays, (mine_ref, others_ref, weight_ref, sums_ref, counts_ref, old_ref) = refs[:6], refs[6:12]
+    held, sems = refs[12:]
     kinds = len(arrays) // 2
+    late = len(arrays) - held.shape[0]
+    moves = [None] * late + [
+        pltpu.make_async_copy(arrays[late + number], held.at[number], sems.at[number])
+        for number in range(held.shape[0])
+    ]
+    for move in moves[late:]:
+        move.start()
     core = lax.axis_index("core")
 
     @pl.when(core == 0)
@@ -154,7 +164,11 @@
         weight_ref[:, 0] = others_ref[:, 1]
 
     whole = weight_ref[...].reshape(arrays[0].shape[1], weight_ref.shape[3])
-    pieces = [(piece, number % kinds, number // kinds) for number, piece in enumerate(arrays)]
+    arrays = list(arrays[:late]) + [held.at[number] for number in range(held.shape[0])]
+    pieces = [
+        (piece, number % kinds, number // kinds, move)
+        for number, (piece, move) in enumerate(zip(arrays, moves))
+    ]
     old_ref[...] = jnp.zeros_like(old_ref)
     sums_ref[...], counts_ref[...] = add_pieces(positions, pieces, whole, old_ref)
 
@@ -167,7 +181,7 @@
     block = rows - TILE
     whole = weight_ref[...].reshape(far_ref.shape[1], head_size)
     old_ref[...] = near_old_ref[...]
-    pieces = [(far_ref, 3, 0), (over_ref, 3, 1)]
+    pieces = [(far_ref, 3, 0, None), (over_ref, 3, 1, None)]
     sums, counts = add_pieces(positions, pieces, whole, old_ref)
     sums += near_sums_ref[...]
     counts = (counts + near_counts_ref[...])[:1]
@@ -254,7 +268,6 @@
     up = lax.ppermute(here, RING, turn(1))
     down = lax.ppermute(here, RING, turn(-1))
     weight = lax.all_to_all(spread, ("z", "ylo"), split_axis=0, concat_axis=0, tiled=True)
-    up, down = lax.optimization_barrier((up, down))
     far = lax.ppermute(up, RING, turn(1))
     near = pl.pallas_call(
         copy_kernel,
@@ -269,6 +282,7 @@
     down_over = lax.ppermute(down, "core", swap)
     weight, near_over = lax.optimization_barrier((weight, near_over))
     others = lax.ppermute(weight, "core", swap)
+    far, down_over = lax.optimization_barrier((far, down_over))
     far_over = lax.ppermute(far, "core", swap)
 
     whole, *partial = pl.pallas_call(
@@ -279,8 +293,9 @@
             jax.ShapeDtypeStruct((8, clusters), f32),
             jax.ShapeDtypeStruct((zs, TILE, head_size), f32),
         ),
-        in_specs=[VMEM] * 8,
+        in_specs=[VMEM] * 4 + [ANY] * 2 + [VMEM] * 2,
         out_specs=(VMEM,) * 4,
+        scratch_shapes=[pltpu.VMEM((2,) + here.shape, bf16), pltpu.SemaphoreType.DMA((2,))],
         compiler_params=PARAMS,
         cost_estimate=pl.CostEstimate(flops=2 * 10**9, bytes_accessed=6 * 10**6, transcendentals=0),
     )(near, up, down, near_over, up_over, down_over, weight, others)

time: 101 us -> 99.8 us (0.988)
  transfers between devices with their start and end apart: 10 -> 10, of which waited for: 2 -> 2; matrix products, arithmetic and copies ran while one was open for 0% -> 0% of each run, Pallas kernels for 3% -> 2%
where the time goes in v6:
time: 99.8 us; the launch traced here: 99.1 us
  blocking collectives  43.4 us (43%)
  starting transfers between devices  43.3 us (43%)
  Pallas kernels  5.51 us (6%)
  waiting for transfers between devices  4.02 us (4%)
  other arithmetic  1.67 us (2%)
  local copies, waits for them, and re-layouts  1.06 us (1%)
    all_to_all x1, blocking collectives, per_device(): lax.all_to_all(owned, ('x', 'z'), split_axis=0, concat_axis=0, tiled=True)  15.3 us
    all_to_all x1, blocking collectives, per_device(): lax.all_to_all(payload, 'z', split_axis=0, concat_axis=0, tiled=True)  14 us
    all_to_all x1, blocking collectives, per_device(): arrived = lax.all_to_all(shares, Y, split_axis=0, concat_axis=0, tiled=True)  14 us
    all_to_all x1, starting transfers between devices, per_device(): lax.all_to_all(spread, ('z', 'ylo'), split_axis=0, concat_axis=0, tiled=T...  11.2 us
    ppermute x1, starting transfers between devices, per_device(): other = lax.ppermute(half, 'core', swap)  7.26 us
    ppermute x1, starting transfers between devices, per_device(): up = lax.ppermute(here, RING, turn(1))  5.22 us
    ppermute x1, starting transfers between devices, per_device(): others = lax.ppermute(weight, 'core', swap)  4.74 us
    ppermute x1, starting transfers between devices, per_device(): near_over = lax.ppermute(near, 'core', swap)  3.61 us
  transfers between devices with their start and end apart: 10, of which 2 were waited for; matrix products, arithmetic and copies ran while one was open for 0% of the time, Pallas kernels for 2%

profile of v6, /device:TPU:1, one launch (start us, length us, event | category | flops | bytes accessed | tf_op | source)
XLA Modules:
  0.0 99.1 jit_solution(9738603898570635377)
XLA Ops:
  0.0 2.2 %shard_map.46 = (bf16[144,2048]{1,0:T(8,128)(2,1)}, bf16[16,2,64,128]{3,2,1,0:T(8,128)(2,1)}) custom-call(bf16[128,2048]{1,0:T(8,128)(2,1)} %bitcast.12, s32[8,128]{1,0:T(8,128)} %bitcast.13, f32[8,128]{1,0:T(8,128)} %old_ref.1, bf16[64,1024]{1,0:T(8,128)(2,1)} %weight_ref.1), custom_call_target="tpu_custom_call" | custom-call | tf_op jit(solution)/shard_map/pallas_call | solution.py:246
  2.2 5.2 %collective-permute-start = (bf16[144,2048]{1,0:T(8,128)(2,1)}, bf16[144,2048]{1,0:T(8,128)(2,1)S(1)}, u32[]{:S(2)}, u32[]{:S(2)}) collective-permute-start(bf16[144,2048]{1,0:T(8,128)(2,1)} %get-tuple-element.15.from_ref), channel_id=1, source_target_pairs={{0,1},{1,2},{2,3},{3,0},{16,19},{17,16},{18,17},{19,18},{4,5},{5,6... | collective-permute-start | bytes 1769480 | tf_op jit(solution)/shard_map/ppermute | solution.py:268
  7.4 1.9 %collective-permute-start.2 = (bf16[144,2048]{1,0:T(8,128)(2,1)}, bf16[144,2048]{1,0:T(8,128)(2,1)S(1)}, u32[]{:S(2)}, u32[]{:S(2)}) collective-permute-start(bf16[144,2048]{1,0:T(8,128)(2,1)} %get-tuple-element.15.from_ref), channel_id=1, source_target_pairs={{0,3},{1,0},{2,1},{3,2},{16,17},{17,18},{18,19},{19,16},{4,7},{5,4... | collective-permute-start | bytes 1769480 | tf_op jit(solution)/shard_map/ppermute | solution.py:269
  9.3 11.2 %all-to-all-start = ((bf16[16,2,64,128]{3,2,1,0:T(8,128)(2,1)}), bf16[16,2,64,128]{3,2,1,0:T(8,128)(2,1)S(1)}, u32[]{:S(2)}, u32[]{:S(2)}) async-start(bf16[16,2,64,128]{3,2,1,0:T(8,128)(2,1)} %get-tuple-element.17), calls=%async_computation | async-start | bytes 1048576 | tf_op jit(solution)/shard_map/all_to_all | solution.py:270
  20.5 0.0 copy-start
  20.5 1.1 %copy-done = bf16[144,2048]{1,0:T(8,128)(2,1)S(1)} copy-done((bf16[144,2048]{1,0:T(8,128)(2,1)S(1)}, bf16[144,2048]{1,0:T(8,128)(2,1)}, u32[]{:S(2)}) %copy-start) | copy-done | bytes 589848
  21.6 0.1 shard_map.47.refs_0_
  21.7 3.6 %collective-permute-start.5 = (bf16[144,2048]{1,0:T(8,128)(2,1)S(1)}, bf16[144,2048]{1,0:T(8,128)(2,1)S(1)}, u32[]{:S(2)}, u32[]{:S(2)}) collective-permute-start(bf16[144,2048]{1,0:T(8,128)(2,1)S(1)} %shard_map.47.refs_0_), channel_id=1, source_target_pairs={{0,16},{16,0},{1,17},{17,1},{2,18},{18,2},{3,19},{19,3},{4,20},{20... | collective-permute-start | bytes 1769480 | tf_op jit(solution)/shard_map/ppermute | solution.py:280
  25.3 0.0 collective-permute-done.refs_1_
  25.3 3.2 %collective-permute-start.1 = (bf16[144,2048]{1,0:T(8,128)(2,1)S(1)}, bf16[144,2048]{1,0:T(8,128)(2,1)S(1)}, u32[]{:S(2)}, u32[]{:S(2)}) collective-permute-start(bf16[144,2048]{1,0:T(8,128)(2,1)S(1)} %collective-permute-done.refs_1_), channel_id=1, source_target_pairs={{0,1},{1,2},{2,3},{3,0},{16,19},{17,16},{18,17},{19,18},{4,5},{5,6... | collective-permute-start | bytes 1769480 | tf_op jit(solution)/shard_map/ppermute | solution.py:271
  28.5 0.0 collective-permute-done.2.refs_2_
  28.5 1.9 %collective-permute-start.3 = (bf16[144,2048]{1,0:T(8,128)(2,1)S(1)}, bf16[144,2048]{1,0:T(8,128)(2,1)}, u32[]{:S(2)}, u32[]{:S(2)}) collective-permute-start(bf16[144,2048]{1,0:T(8,128)(2,1)S(1)} %collective-permute-done.2.refs_2_), channel_id=1, source_target_pairs={{0,16},{16,0},{1,17},{17,1},{2,18},{18,2},{3,19},{19,3},{4,20},{20... | collective-permute-start | bytes 1769480 | tf_op jit(solution)/shard_map/ppermute | solution.py:282
  30.5 2.4 %collective-permute-start.6 = (bf16[144,2048]{1,0:T(8,128)(2,1)S(1)}, bf16[144,2048]{1,0:T(8,128)(2,1)}, u32[]{:S(2)}, u32[]{:S(2)}) collective-permute-start(bf16[144,2048]{1,0:T(8,128)(2,1)S(1)} %collective-permute-done.refs_1_), channel_id=1, source_target_pairs={{0,16},{16,0},{1,17},{17,1},{2,18},{18,2},{3,19},{19,3},{4,20},{20... | collective-permute-start | bytes 1769480 | tf_op jit(solution)/shard_map/ppermute | solution.py:281
  32.9 0.0 collective-permute-done.5.refs_3_
  32.9 2.5 %all-to-all-done.refs_6_ = bf16[16,2,64,128]{3,2,1,0:T(8,128)(2,1)S(1)} async-done(((bf16[16,2,64,128]{3,2,1,0:T(8,128)(2,1)}), bf16[16,2,64,128]{3,2,1,0:T(8,128)(2,1)S(1)}, u32[]{:S(2)}, u32[]{:S(2)}) %all-to-all-start) | async-done | bytes 524320 | tf_op jit(solution)/shard_map/all_to_all | solution.py:270
  35.4 4.7 %collective-permute-start.7 = (bf16[16,2,64,128]{3,2,1,0:T(8,128)(2,1)S(1)}, bf16[16,2,64,128]{3,2,1,0:T(8,128)(2,1)S(1)}, u32[]{:S(2)}, u32[]{:S(2)}) collective-permute-start(bf16[16,2,64,128]{3,2,1,0:T(8,128)(2,1)S(1)} %all-to-all-done.refs_6_), channel_id=1, source_target_pairs={{0,16},{16,0},{1,17},{17,1},{2,18},{18,2},{3,19},{19,3},{4,20},{20... | collective-permute-start | bytes 1572872 | tf_op jit(solution)/shard_map/ppermute | solution.py:284
  40.1 0.0 collective-permute-done.1.far_ref
  40.1 0.0 collective-permute-done.3.refs_5_
  40.1 1.9 %collective-permute-start.4 = (bf16[144,2048]{1,0:T(8,128)(2,1)S(1)}, bf16[144,2048]{1,0:T(8,128)(2,1)S(1)}, u32[]{:S(2)}, u32[]{:S(2)}) collective-permute-start(bf16[144,2048]{1,0:T(8,128)(2,1)S(1)} %collective-permute-done.1.far_ref), channel_id=1, source_target_pairs={{0,16},{16,0},{1,17},{17,1},{2,18},{18,2},{3,19},{19,3},{4,20},{20... | collective-permute-start | bytes 1769480 | tf_op jit(solution)/shard_map/ppermute | solution.py:286
  42.1 0.0 collective-permute-done.6.refs_4_
  42.1 0.0 collective-permute-done.7.refs_7_
  42.1 2.1 %shard_map.48 = (bf16[16,2,64,128]{3,2,1,0:T(8,128)(2,1)S(1)}, f32[512,128]{1,0:T(8,128)S(1)}, f32[8,512]{1,0:T(8,128)S(1)}, f32[8,16,128]{2,1,0:T(8,128)S(1)}) custom-call(bf16[144,2048]{1,0:T(8,128)(2,1)S(1)} %shard_map.47.refs_0_, bf16[144,2048]{1,0:T(8,128)(2,1)S(1)} %collective-permute-done.refs_1_, ...), custom_call_target="tpu_custom_call" | custom-call | flops 2000000000 | bytes 6000000 | tf_op jit(solution)/shard_map/pallas_call | solution.py:288
  44.2 0.0 collective-permute-done.4.over_ref
  44.3 0.8 shard_map.49
  45.0 14.0 %all_to_all.20.arrived_ref = bf16[8,80,128]{2,1,0:T(8,128)(2,1)S(1)} all-to-all(bf16[8,80,128]{2,1,0:T(8,128)(2,1)S(1)} %shard_map.49), channel_id=1, replica_groups=mesh['z'=8,'ylo'=2,'core'=2,'yhi'=4,'x'=4] {'z'}, dimensions={0} | all-to-all | bytes 327680 | tf_op jit(solution)/shard_map/all_to_all | solution.py:311
  59.1 14.0 %all_to_all.21.arrived_ref = bf16[8,80,128]{2,1,0:T(8,128)(2,1)S(1)} all-to-all(bf16[8,80,128]{2,1,0:T(8,128)(2,1)S(1)} %shard_map.50), channel_id=1, replica_groups=mesh['z'=8,'ylo'=2,'core'=2,'yhi'=4,'x'=4] {'yhi','ylo'}, dimensions={0} | all-to-all | bytes 327680 | tf_op jit(solution)/shard_map/all_to_all | solution.py:320
  73.2 0.2 shard_map.51
  73.4 15.3 %all_to_all.22 = bf16[32,64,128]{2,1,0:T(8,128)(2,1)S(1)} all-to-all(bf16[32,64,128]{2,1,0:T(8,128)(2,1)S(1)} %shard_map.51), channel_id=1, replica_groups=mesh['z'=8,'ylo'=2,'core'=2,'yhi'=4,'x'=4] {'x','z'}, dimensions={0} | all-to-all | bytes 1048576 | tf_op jit(solution)/shard_map/all_to_all | solution.py:329
  88.7 7.3 %collective-permute-start.8 = (bf16[4,8,64,128]{3,2,1,0:T(8,128)(2,1)S(1)}, bf16[4,8,64,128]{3,2,1,0:T(8,128)(2,1)S(1)}, u32[]{:S(2)}, u32[]{:S(2)}) collective-permute-start(bf16[4,8,64,128]{3,2,1,0:T(8,128)(2,1)S(1)} %bitcast.8), channel_id=1, source_target_pairs={{0,16},{16,0},{1,17},{17,1},{2,18},{18,2},{3,19},{19,3},{4,20},{20... | collective-permute-start | bytes 1572872 | tf_op jit(solution)/shard_map/ppermute | solution.py:331
  96.0 1.5 %collective-permute-done.8 = bf16[4,8,64,128]{3,2,1,0:T(8,128)(2,1)S(1)} collective-permute-done((bf16[4,8,64,128]{3,2,1,0:T(8,128)(2,1)S(1)}, bf16[4,8,64,128]{3,2,1,0:T(8,128)(2,1)S(1)}, u32[]{:S(2)}, u32[]{:S(2)}) %collective-permute-start.8) | collective-permute-done | bytes 524320 | tf_op jit(solution)/shard_map/ppermute | solution.py:331
  97.5 0.1 broadcast_select_fusion.1
  97.5 1.6 %copy_convert_fusion = f32[2,4,2,4,4,2,8,128]{7,6,3,4,2,5,1,0:T(8,128)} fusion(bf16[1,4,2,4,4,2,8,128]{7,6,5,4,3,2,1,0:T(8,128)(2,1)S(1)} %bitcast.11, bf16[1,4,2,4,4,2,8,128]{7,6,5,4,3,2,1,0:T(8,128)(2,1)S(1)} %bitcast.10), kind=kLoop, calls=%fused_computation.1 | loop fusion | flops 1048576 | bytes 3145728 | tf_op jit(solution)/shard_map/reshape | solution.py:336
  (1 shorter events, 0.0 us)
Async XLA Ops:
  2.2 23.1 %collective-permute-start = (bf16[144,2048]{1,0:T(8,128)(2,1)}, bf16[144,2048]{1,0:T(8,128)(2,1)S(1)}, u32[]{:S(2)}, u32[]{:S(2)}) collective-permute-start(bf16[144,2048]{1,0:T(8,128)(2,1)} %get-tuple-element.15.from_ref), channel_id=1, source_target_pairs={{0,1},{1,2},{2,3},{3,0},{16,19},{17,16},{18,17},{19,18},{4,5},{5,6... | collective-permute-start | bytes 1769480 | tf_op jit(solution)/shard_map/ppermute | solution.py:268
  7.4 21.1 %collective-permute-start.2 = (bf16[144,2048]{1,0:T(8,128)(2,1)}, bf16[144,2048]{1,0:T(8,128)(2,1)S(1)}, u32[]{:S(2)}, u32[]{:S(2)}) collective-permute-start(bf16[144,2048]{1,0:T(8,128)(2,1)} %get-tuple-element.15.from_ref), channel_id=1, source_target_pairs={{0,3},{1,0},{2,1},{3,2},{16,17},{17,18},{18,19},{19,16},{4,7},{5,4... | collective-permute-start | bytes 1769480 | tf_op jit(solution)/shard_map/ppermute | solution.py:269
  9.3 26.0 %all-to-all-start = ((bf16[16,2,64,128]{3,2,1,0:T(8,128)(2,1)}), bf16[16,2,64,128]{3,2,1,0:T(8,128)(2,1)S(1)}, u32[]{:S(2)}, u32[]{:S(2)}) async-start(bf16[16,2,64,128]{3,2,1,0:T(8,128)(2,1)} %get-tuple-element.17), calls=%async_computation | async-start | bytes 1048576 | tf_op jit(solution)/shard_map/all_to_all | solution.py:270
  20.5 1.1 %copy-start = (bf16[144,2048]{1,0:T(8,128)(2,1)S(1)}, bf16[144,2048]{1,0:T(8,128)(2,1)}, u32[]{:S(2)}) copy-start(bf16[144,2048]{1,0:T(8,128)(2,1)} %get-tuple-element.15.from_ref) | copy-start | bytes 1769476
  21.7 11.2 %collective-permute-start.5 = (bf16[144,2048]{1,0:T(8,128)(2,1)S(1)}, bf16[144,2048]{1,0:T(8,128)(2,1)S(1)}, u32[]{:S(2)}, u32[]{:S(2)}) collective-permute-start(bf16[144,2048]{1,0:T(8,128)(2,1)S(1)} %shard_map.47.refs_0_), channel_id=1, source_target_pairs={{0,16},{16,0},{1,17},{17,1},{2,18},{18,2},{3,19},{19,3},{4,20},{20... | collective-permute-start | bytes 1769480 | tf_op jit(solution)/shard_map/ppermute | solution.py:280
  25.3 14.8 %collective-permute-start.1 = (bf16[144,2048]{1,0:T(8,128)(2,1)S(1)}, bf16[144,2048]{1,0:T(8,128)(2,1)S(1)}, u32[]{:S(2)}, u32[]{:S(2)}) collective-permute-start(bf16[144,2048]{1,0:T(8,128)(2,1)S(1)} %collective-permute-done.refs_1_), channel_id=1, source_target_pairs={{0,1},{1,2},{2,3},{3,0},{16,19},{17,16},{18,17},{19,18},{4,5},{5,6... | collective-permute-start | bytes 1769480 | tf_op jit(solution)/shard_map/ppermute | solution.py:271
  28.5 11.6 %collective-permute-start.3 = (bf16[144,2048]{1,0:T(8,128)(2,1)S(1)}, bf16[144,2048]{1,0:T(8,128)(2,1)}, u32[]{:S(2)}, u32[]{:S(2)}) collective-permute-start(bf16[144,2048]{1,0:T(8,128)(2,1)S(1)} %collective-permute-done.2.refs_2_), channel_id=1, source_target_pairs={{0,16},{16,0},{1,17},{17,1},{2,18},{18,2},{3,19},{19,3},{4,20},{20... | collective-permute-start | bytes 1769480 | tf_op jit(solution)/shard_map/ppermute | solution.py:282
  30.5 11.6 %collective-permute-start.6 = (bf16[144,2048]{1,0:T(8,128)(2,1)S(1)}, bf16[144,2048]{1,0:T(8,128)(2,1)}, u32[]{:S(2)}, u32[]{:S(2)}) collective-permute-start(bf16[144,2048]{1,0:T(8,128)(2,1)S(1)} %collective-permute-done.refs_1_), channel_id=1, source_target_pairs={{0,16},{16,0},{1,17},{17,1},{2,18},{18,2},{3,19},{19,3},{4,20},{20... | collective-permute-start | bytes 1769480 | tf_op jit(solution)/shard_map/ppermute | solution.py:281
  35.4 6.7 %collective-permute-start.7 = (bf16[16,2,64,128]{3,2,1,0:T(8,128)(2,1)S(1)}, bf16[16,2,64,128]{3,2,1,0:T(8,128)(2,1)S(1)}, u32[]{:S(2)}, u32[]{:S(2)}) collective-permute-start(bf16[16,2,64,128]{3,2,1,0:T(8,128)(2,1)S(1)} %all-to-all-done.refs_6_), channel_id=1, source_target_pairs={{0,16},{16,0},{1,17},{17,1},{2,18},{18,2},{3,19},{19,3},{4,20},{20... | collective-permute-start | bytes 1572872 | tf_op jit(solution)/shard_map/ppermute | solution.py:284
  40.1 4.1 %collective-permute-start.4 = (bf16[144,2048]{1,0:T(8,128)(2,1)S(1)}, bf16[144,2048]{1,0:T(8,128)(2,1)S(1)}, u32[]{:S(2)}, u32[]{:S(2)}) collective-permute-start(bf16[144,2048]{1,0:T(8,128)(2,1)S(1)} %collective-permute-done.1.far_ref), channel_id=1, source_target_pairs={{0,16},{16,0},{1,17},{17,1},{2,18},{18,2},{3,19},{19,3},{4,20},{20... | collective-permute-start | bytes 1769480 | tf_op jit(solution)/shard_map/ppermute | solution.py:286
  88.7 8.8 %collective-permute-start.8 = (bf16[4,8,64,128]{3,2,1,0:T(8,128)(2,1)S(1)}, bf16[4,8,64,128]{3,2,1,0:T(8,128)(2,1)S(1)}, u32[]{:S(2)}, u32[]{:S(2)}) collective-permute-start(bf16[4,8,64,128]{3,2,1,0:T(8,128)(2,1)S(1)} %bitcast.8), channel_id=1, source_target_pairs={{0,16},{16,0},{1,17},{17,1},{2,18},{18,2},{3,19},{19,3},{4,20},{20... | collective-permute-start | bytes 1572872 | tf_op jit(solution)/shard_map/ppermute | solution.py:331

commit v7 on v6

--- a/solution.py
+++ b/solution.py
@@ -282,7 +282,7 @@
     down_over = lax.ppermute(down, "core", swap)
     weight, near_over = lax.optimization_barrier((weight, near_over))
     others = lax.ppermute(weight, "core", swap)
-    far, down_over = lax.optimization_barrier((far, down_over))
+    far, down_over, up_over = lax.optimization_barrier((far, down_over, up_over))
     far_over = lax.ppermute(far, "core", swap)
 
     whole, *partial = pl.pallas_call(

time: 99.8 us -> 99.9 us (level)
  no operation moved by 1% of the time
where the time goes in v7:
time: 99.9 us; the launch traced here: 99.2 us
  blocking collectives  43.7 us (44%)
  starting transfers between devices  43.1 us (43%)
  Pallas kernels  5.51 us (6%)
  waiting for transfers between devices  4.02 us (4%)
  other arithmetic  1.67 us (2%)
  local copies, waits for them, and re-layouts  1.06 us (1%)
    all_to_all x1, blocking collectives, per_device(): lax.all_to_all(owned, ('x', 'z'), split_axis=0, concat_axis=0, tiled=True)  15.5 us
    all_to_all x1, blocking collectives, per_device(): arrived = lax.all_to_all(shares, Y, split_axis=0, concat_axis=0, tiled=True)  14.1 us
    all_to_all x1, blocking collectives, per_device(): lax.all_to_all(payload, 'z', split_axis=0, concat_axis=0, tiled=True)  14.1 us
    all_to_all x1, starting transfers between devices, per_device(): lax.all_to_all(spread, ('z', 'ylo'), split_axis=0, concat_axis=0, tiled=T...  11.2 us
    ppermute x1, starting transfers between devices, per_device(): other = lax.ppermute(half, 'core', swap)  7.01 us
    ppermute x1, starting transfers between devices, per_device(): up = lax.ppermute(here, RING, turn(1))  5.22 us
    ppermute x1, starting transfers between devices, per_device(): others = lax.ppermute(weight, 'core', swap)  4.74 us
    ppermute x1, starting transfers between devices, per_device(): near_over = lax.ppermute(near, 'core', swap)  3.61 us
  transfers between devices with their start and end apart: 10, of which 2 were waited for; matrix products, arithmetic and copies ran while one was open for 0% of the time, Pallas kernels for 2%

profile of v7, /device:TPU:1, one launch (start us, length us, event | category | flops | bytes accessed | tf_op | source)
XLA Modules:
  0.0 99.2 jit_solution(9159439787297017072)
XLA Ops:
  0.0 2.2 %shard_map.46 = (bf16[144,2048]{1,0:T(8,128)(2,1)}, bf16[16,2,64,128]{3,2,1,0:T(8,128)(2,1)}) custom-call(bf16[128,2048]{1,0:T(8,128)(2,1)} %bitcast.12, s32[8,128]{1,0:T(8,128)} %bitcast.13, f32[8,128]{1,0:T(8,128)} %old_ref.1, bf16[64,1024]{1,0:T(8,128)(2,1)} %weight_ref.1), custom_call_target="tpu_custom_call" | custom-call | tf_op jit(solution)/shard_map/pallas_call | solution.py:246
  2.2 5.2 %collective-permute-start = (bf16[144,2048]{1,0:T(8,128)(2,1)}, bf16[144,2048]{1,0:T(8,128)(2,1)S(1)}, u32[]{:S(2)}, u32[]{:S(2)}) collective-permute-start(bf16[144,2048]{1,0:T(8,128)(2,1)} %get-tuple-element.16.from_ref), channel_id=1, source_target_pairs={{0,1},{1,2},{2,3},{3,0},{16,19},{17,16},{18,17},{19,18},{4,5},{5,6... | collective-permute-start | bytes 1769480 | tf_op jit(solution)/shard_map/ppermute | solution.py:268
  7.4 1.9 %collective-permute-start.2 = (bf16[144,2048]{1,0:T(8,128)(2,1)}, bf16[144,2048]{1,0:T(8,128)(2,1)S(1)}, u32[]{:S(2)}, u32[]{:S(2)}) collective-permute-start(bf16[144,2048]{1,0:T(8,128)(2,1)} %get-tuple-element.16.from_ref), channel_id=1, source_target_pairs={{0,3},{1,0},{2,1},{3,2},{16,17},{17,18},{18,19},{19,16},{4,7},{5,4... | collective-permute-start | bytes 1769480 | tf_op jit(solution)/shard_map/ppermute | solution.py:269
  9.3 11.2 %all-to-all-start = ((bf16[16,2,64,128]{3,2,1,0:T(8,128)(2,1)}), bf16[16,2,64,128]{3,2,1,0:T(8,128)(2,1)S(1)}, u32[]{:S(2)}, u32[]{:S(2)}) async-start(bf16[16,2,64,128]{3,2,1,0:T(8,128)(2,1)} %get-tuple-element.18), calls=%async_computation | async-start | bytes 1048576 | tf_op jit(solution)/shard_map/all_to_all | solution.py:270
  20.5 0.0 copy-start
  20.5 1.1 %copy-done = bf16[144,2048]{1,0:T(8,128)(2,1)S(1)} copy-done((bf16[144,2048]{1,0:T(8,128)(2,1)S(1)}, bf16[144,2048]{1,0:T(8,128)(2,1)}, u32[]{:S(2)}) %copy-start) | copy-done | bytes 589848
  21.6 0.1 shard_map.47.refs_0_
  21.7 3.6 %collective-permute-start.6 = (bf16[144,2048]{1,0:T(8,128)(2,1)S(1)}, bf16[144,2048]{1,0:T(8,128)(2,1)S(1)}, u32[]{:S(2)}, u32[]{:S(2)}) collective-permute-start(bf16[144,2048]{1,0:T(8,128)(2,1)S(1)} %shard_map.47.refs_0_), channel_id=1, source_target_pairs={{0,16},{16,0},{1,17},{17,1},{2,18},{18,2},{3,19},{19,3},{4,20},{20... | collective-permute-start | bytes 1769480 | tf_op jit(solution)/shard_map/ppermute | solution.py:280
  25.3 0.0 collective-permute-done.refs_1_
  25.3 3.2 %collective-permute-start.1 = (bf16[144,2048]{1,0:T(8,128)(2,1)S(1)}, bf16[144,2048]{1,0:T(8,128)(2,1)S(1)}, u32[]{:S(2)}, u32[]{:S(2)}) collective-permute-start(bf16[144,2048]{1,0:T(8,128)(2,1)S(1)} %collective-permute-done.refs_1_), channel_id=1, source_target_pairs={{0,1},{1,2},{2,3},{3,0},{16,19},{17,16},{18,17},{19,18},{4,5},{5,6... | collective-permute-start | bytes 1769480 | tf_op jit(solution)/shard_map/ppermute | solution.py:271
  28.5 1.9 %collective-permute-start.4 = (bf16[144,2048]{1,0:T(8,128)(2,1)S(1)}, bf16[144,2048]{1,0:T(8,128)(2,1)}, u32[]{:S(2)}, u32[]{:S(2)}) collective-permute-start(bf16[144,2048]{1,0:T(8,128)(2,1)S(1)} %collective-permute-done.refs_1_), channel_id=1, source_target_pairs={{0,16},{16,0},{1,17},{17,1},{2,18},{18,2},{3,19},{19,3},{4,20},{20... | collective-permute-start | bytes 1769480 | tf_op jit(solution)/shard_map/ppermute | solution.py:281
  30.5 0.0 collective-permute-done.2.refs_2_
  30.5 2.4 %collective-permute-start.3 = (bf16[144,2048]{1,0:T(8,128)(2,1)S(1)}, bf16[144,2048]{1,0:T(8,128)(2,1)}, u32[]{:S(2)}, u32[]{:S(2)}) collective-permute-start(bf16[144,2048]{1,0:T(8,128)(2,1)S(1)} %collective-permute-done.2.refs_2_), channel_id=1, source_target_pairs={{0,16},{16,0},{1,17},{17,1},{2,18},{18,2},{3,19},{19,3},{4,20},{20... | collective-permute-start | bytes 1769480 | tf_op jit(solution)/shard_map/ppermute | solution.py:282
  32.9 0.0 collective-permute-done.6.refs_3_
  32.9 2.5 %all-to-all-done.refs_6_ = bf16[16,2,64,128]{3,2,1,0:T(8,128)(2,1)S(1)} async-done(((bf16[16,2,64,128]{3,2,1,0:T(8,128)(2,1)}), bf16[16,2,64,128]{3,2,1,0:T(8,128)(2,1)S(1)}, u32[]{:S(2)}, u32[]{:S(2)}) %all-to-all-start) | async-done | bytes 524320 | tf_op jit(solution)/shard_map/all_to_all | solution.py:270
  35.4 4.7 %collective-permute-start.7 = (bf16[16,2,64,128]{3,2,1,0:T(8,128)(2,1)S(1)}, bf16[16,2,64,128]{3,2,1,0:T(8,128)(2,1)S(1)}, u32[]{:S(2)}, u32[]{:S(2)}) collective-permute-start(bf16[16,2,64,128]{3,2,1,0:T(8,128)(2,1)S(1)} %all-to-all-done.refs_6_), channel_id=1, source_target_pairs={{0,16},{16,0},{1,17},{17,1},{2,18},{18,2},{3,19},{19,3},{4,20},{20... | collective-permute-start | bytes 1572872 | tf_op jit(solution)/shard_map/ppermute | solution.py:284
  40.1 0.0 collective-permute-done.1.far_ref
  40.1 0.0 collective-permute-done.4.refs_4_
  40.1 0.0 collective-permute-done.3.refs_5_
  40.2 1.9 %collective-permute-start.5 = (bf16[144,2048]{1,0:T(8,128)(2,1)S(1)}, bf16[144,2048]{1,0:T(8,128)(2,1)S(1)}, u32[]{:S(2)}, u32[]{:S(2)}) collective-permute-start(bf16[144,2048]{1,0:T(8,128)(2,1)S(1)} %collective-permute-done.1.far_ref), channel_id=1, source_target_pairs={{0,16},{16,0},{1,17},{17,1},{2,18},{18,2},{3,19},{19,3},{4,20},{20... | collective-permute-start | bytes 1769480 | tf_op jit(solution)/shard_map/ppermute | solution.py:286
  42.1 0.0 collective-permute-done.7.refs_7_
  42.1 2.1 %shard_map.48 = (bf16[16,2,64,128]{3,2,1,0:T(8,128)(2,1)S(1)}, f32[512,128]{1,0:T(8,128)S(1)}, f32[8,512]{1,0:T(8,128)S(1)}, f32[8,16,128]{2,1,0:T(8,128)S(1)}) custom-call(bf16[144,2048]{1,0:T(8,128)(2,1)S(1)} %shard_map.47.refs_0_, bf16[144,2048]{1,0:T(8,128)(2,1)S(1)} %collective-permute-done.refs_1_, ...), custom_call_target="tpu_custom_call" | custom-call | flops 2000000000 | bytes 6000000 | tf_op jit(solution)/shard_map/pallas_call | solution.py:288
  44.2 0.0 collective-permute-done.5.over_ref
  44.3 0.8 shard_map.49
  45.0 14.1 %all_to_all.20.arrived_ref = bf16[8,80,128]{2,1,0:T(8,128)(2,1)S(1)} all-to-all(bf16[8,80,128]{2,1,0:T(8,128)(2,1)S(1)} %shard_map.49), channel_id=1, replica_groups=mesh['z'=8,'ylo'=2,'core'=2,'yhi'=4,'x'=4] {'z'}, dimensions={0} | all-to-all | bytes 327680 | tf_op jit(solution)/shard_map/all_to_all | solution.py:311
  59.1 14.1 %all_to_all.21.arrived_ref = bf16[8,80,128]{2,1,0:T(8,128)(2,1)S(1)} all-to-all(bf16[8,80,128]{2,1,0:T(8,128)(2,1)S(1)} %shard_map.50), channel_id=1, replica_groups=mesh['z'=8,'ylo'=2,'core'=2,'yhi'=4,'x'=4] {'yhi','ylo'}, dimensions={0} | all-to-all | bytes 327680 | tf_op jit(solution)/shard_map/all_to_all | solution.py:320
  73.3 0.2 shard_map.51
  73.5 15.5 %all_to_all.22 = bf16[32,64,128]{2,1,0:T(8,128)(2,1)S(1)} all-to-all(bf16[32,64,128]{2,1,0:T(8,128)(2,1)S(1)} %shard_map.51), channel_id=1, replica_groups=mesh['z'=8,'ylo'=2,'core'=2,'yhi'=4,'x'=4] {'x','z'}, dimensions={0} | all-to-all | bytes 1048576 | tf_op jit(solution)/shard_map/all_to_all | solution.py:329
  89.0 7.0 %collective-permute-start.8 = (bf16[4,8,64,128]{3,2,1,0:T(8,128)(2,1)S(1)}, bf16[4,8,64,128]{3,2,1,0:T(8,128)(2,1)S(1)}, u32[]{:S(2)}, u32[]{:S(2)}) collective-permute-start(bf16[4,8,64,128]{3,2,1,0:T(8,128)(2,1)S(1)} %bitcast.8), channel_id=1, source_target_pairs={{0,16},{16,0},{1,17},{17,1},{2,18},{18,2},{3,19},{19,3},{4,20},{20... | collective-permute-start | bytes 1572872 | tf_op jit(solution)/shard_map/ppermute | solution.py:331
  96.1 1.5 %collective-permute-done.8 = bf16[4,8,64,128]{3,2,1,0:T(8,128)(2,1)S(1)} collective-permute-done((bf16[4,8,64,128]{3,2,1,0:T(8,128)(2,1)S(1)}, bf16[4,8,64,128]{3,2,1,0:T(8,128)(2,1)S(1)}, u32[]{:S(2)}, u32[]{:S(2)}) %collective-permute-start.8) | collective-permute-done | bytes 524320 | tf_op jit(solution)/shard_map/ppermute | solution.py:331
  97.6 0.1 broadcast_select_fusion.1
  97.6 1.6 %copy_convert_fusion = f32[2,4,2,4,4,2,8,128]{7,6,3,4,2,5,1,0:T(8,128)} fusion(bf16[1,4,2,4,4,2,8,128]{7,6,5,4,3,2,1,0:T(8,128)(2,1)S(1)} %bitcast.11, bf16[1,4,2,4,4,2,8,128]{7,6,5,4,3,2,1,0:T(8,128)(2,1)S(1)} %bitcast.10), kind=kLoop, calls=%fused_computation.1 | loop fusion | flops 1048576 | bytes 3145728 | tf_op jit(solution)/shard_map/reshape | solution.py:336
  (1 shorter events, 0.0 us)
Async XLA Ops:
  2.2 23.1 %collective-permute-start = (bf16[144,2048]{1,0:T(8,128)(2,1)}, bf16[144,2048]{1,0:T(8,128)(2,1)S(1)}, u32[]{:S(2)}, u32[]{:S(2)}) collective-permute-start(bf16[144,2048]{1,0:T(8,128)(2,1)} %get-tuple-element.16.from_ref), channel_id=1, source_target_pairs={{0,1},{1,2},{2,3},{3,0},{16,19},{17,16},{18,17},{19,18},{4,5},{5,6... | collective-permute-start | bytes 1769480 | tf_op jit(solution)/shard_map/ppermute | solution.py:268
  7.4 23.0 %collective-permute-start.2 = (bf16[144,2048]{1,0:T(8,128)(2,1)}, bf16[144,2048]{1,0:T(8,128)(2,1)S(1)}, u32[]{:S(2)}, u32[]{:S(2)}) collective-permute-start(bf16[144,2048]{1,0:T(8,128)(2,1)} %get-tuple-element.16.from_ref), channel_id=1, source_target_pairs={{0,3},{1,0},{2,1},{3,2},{16,17},{17,18},{18,19},{19,16},{4,7},{5,4... | collective-permute-start | bytes 1769480 | tf_op jit(solution)/shard_map/ppermute | solution.py:269
  9.3 26.0 %all-to-all-start = ((bf16[16,2,64,128]{3,2,1,0:T(8,128)(2,1)}), bf16[16,2,64,128]{3,2,1,0:T(8,128)(2,1)S(1)}, u32[]{:S(2)}, u32[]{:S(2)}) async-start(bf16[16,2,64,128]{3,2,1,0:T(8,128)(2,1)} %get-tuple-element.18), calls=%async_computation | async-start | bytes 1048576 | tf_op jit(solution)/shard_map/all_to_all | solution.py:270
  20.5 1.1 %copy-start = (bf16[144,2048]{1,0:T(8,128)(2,1)S(1)}, bf16[144,2048]{1,0:T(8,128)(2,1)}, u32[]{:S(2)}) copy-start(bf16[144,2048]{1,0:T(8,128)(2,1)} %get-tuple-element.16.from_ref) | copy-start | bytes 1769476
  21.7 11.2 %collective-permute-start.6 = (bf16[144,2048]{1,0:T(8,128)(2,1)S(1)}, bf16[144,2048]{1,0:T(8,128)(2,1)S(1)}, u32[]{:S(2)}, u32[]{:S(2)}) collective-permute-start(bf16[144,2048]{1,0:T(8,128)(2,1)S(1)} %shard_map.47.refs_0_), channel_id=1, source_target_pairs={{0,16},{16,0},{1,17},{17,1},{2,18},{18,2},{3,19},{19,3},{4,20},{20... | collective-permute-start | bytes 1769480 | tf_op jit(solution)/shard_map/ppermute | solution.py:280
  25.3 14.8 %collective-permute-start.1 = (bf16[144,2048]{1,0:T(8,128)(2,1)S(1)}, bf16[144,2048]{1,0:T(8,128)(2,1)S(1)}, u32[]{:S(2)}, u32[]{:S(2)}) collective-permute-start(bf16[144,2048]{1,0:T(8,128)(2,1)S(1)} %collective-permute-done.refs_1_), channel_id=1, source_target_pairs={{0,1},{1,2},{2,3},{3,0},{16,19},{17,16},{18,17},{19,18},{4,5},{5,6... | collective-permute-start | bytes 1769480 | tf_op jit(solution)/shard_map/ppermute | solution.py:271
  28.5 11.6 %collective-permute-start.4 = (bf16[144,2048]{1,0:T(8,128)(2,1)S(1)}, bf16[144,2048]{1,0:T(8,128)(2,1)}, u32[]{:S(2)}, u32[]{:S(2)}) collective-permute-start(bf16[144,2048]{1,0:T(8,128)(2,1)S(1)} %collective-permute-done.refs_1_), channel_id=1, source_target_pairs={{0,16},{16,0},{1,17},{17,1},{2,18},{18,2},{3,19},{19,3},{4,20},{20... | collective-permute-start | bytes 1769480 | tf_op jit(solution)/shard_map/ppermute | solution.py:281
  30.5 9.7 %collective-permute-start.3 = (bf16[144,2048]{1,0:T(8,128)(2,1)S(1)}, bf16[144,2048]{1,0:T(8,128)(2,1)}, u32[]{:S(2)}, u32[]{:S(2)}) collective-permute-start(bf16[144,2048]{1,0:T(8,128)(2,1)S(1)} %collective-permute-done.2.refs_2_), channel_id=1, source_target_pairs={{0,16},{16,0},{1,17},{17,1},{2,18},{18,2},{3,19},{19,3},{4,20},{20... | collective-permute-start | bytes 1769480 | tf_op jit(solution)/shard_map/ppermute | solution.py:282
  35.4 6.7 %collective-permute-start.7 = (bf16[16,2,64,128]{3,2,1,0:T(8,128)(2,1)S(1)}, bf16[16,2,64,128]{3,2,1,0:T(8,128)(2,1)S(1)}, u32[]{:S(2)}, u32[]{:S(2)}) collective-permute-start(bf16[16,2,64,128]{3,2,1,0:T(8,128)(2,1)S(1)} %all-to-all-done.refs_6_), channel_id=1, source_target_pairs={{0,16},{16,0},{1,17},{17,1},{2,18},{18,2},{3,19},{19,3},{4,20},{20... | collective-permute-start | bytes 1572872 | tf_op jit(solution)/shard_map/ppermute | solution.py:284
  40.2 4.1 %collective-permute-start.5 = (bf16[144,2048]{1,0:T(8,128)(2,1)S(1)}, bf16[144,2048]{1,0:T(8,128)(2,1)S(1)}, u32[]{:S(2)}, u32[]{:S(2)}) collective-permute-start(bf16[144,2048]{1,0:T(8,128)(2,1)S(1)} %collective-permute-done.1.far_ref), channel_id=1, source_target_pairs={{0,16},{16,0},{1,17},{17,1},{2,18},{18,2},{3,19},{19,3},{4,20},{20... | collective-permute-start | bytes 1769480 | tf_op jit(solution)/shard_map/ppermute | solution.py:286
  89.0 8.5 %collective-permute-start.8 = (bf16[4,8,64,128]{3,2,1,0:T(8,128)(2,1)S(1)}, bf16[4,8,64,128]{3,2,1,0:T(8,128)(2,1)S(1)}, u32[]{:S(2)}, u32[]{:S(2)}) collective-permute-start(bf16[4,8,64,128]{3,2,1,0:T(8,128)(2,1)S(1)} %bitcast.8), channel_id=1, source_target_pairs={{0,16},{16,0},{1,17},{17,1},{2,18},{18,2},{3,19},{19,3},{4,20},{20... | collective-permute-start | bytes 1572872 | tf_op jit(solution)/shard_map/ppermute | solution.py:331
